TPU v7x, 128 devices: a whole 4x4x4 slice. The times are simulated.
128 devices in a mesh: region: 4 (over x_hi, core), node: 32 (over x_lo, y, z).
Axes of the slice: x: 4 (x_hi: 2, x_lo: 2; x = x_hi * 2 + x_lo), y: 4, z: 4, core: 2. Of those that a mesh axis runs over, the one named last changes fastest.
Arguments:
- start_modes: float32 [3, 32, 128, 4096], P(None, None, 'region', 'node'), may hold values from -6 to 6
- stiffness_tiles: float32 [9, 3, 3, 128, 4096], P(None, None, None, 'region', 'node'), may hold values from -1 to 9, as said below
- free_mask: int32 [128, 4096], P('region', 'node'), may hold values 0 or 1
- group_ids: int32 [128, 4096], P('region', 'node'), may hold values from 0 to 63
- design: float32 [64], replicated, may hold values from 0.5 to 2
- node_mass: float32 [128, 4096], P('region'), may hold values from 0.3 to 3
Outputs:
- modes: float32 [3, 32, 128, 4096], P(None, None, 'region', 'node')
- modes_by_column: float32 [3, 32, 128, 4096], P(None, 'node', 'region')
- reduced_stiffness: float32 [32, 32], replicated
- participation: float32 [6, 32], P(None, 'node')
- design_adjoint: float32 [64], replicated
Inputs may be any that keep to these rules, and one draw needn't show every extreme that they name: `stiffness_tiles`: the centre tile (s = 4) has 8 plus a term in -1..1 on its diagonal; every other entry of every tile lies in -1..1.
All inputs are finite; a program needn't handle non-finite values. No bound on the sum of `free_mask` on one device may be relied on, other than what follows from the above.
Results may differ from a plain program's by a relative error of at most 0.00017.
Values sent between devices are 32-bit elements; how exact they have to be, the bound alone decides.
No kernel may reach another device: no remote copies, remote signals or barrier semaphores. Data moves between devices by JAX's collectives and lax.ppermute only.
A program may use at most 64 MiB of HBM per device.

v0:
```python
import jax
import jax.numpy as jnp
from jax import lax
from jax.sharding import PartitionSpec as P

ITERS = 2


HIGH = lax.Precision.HIGHEST


def with_halo(array, sides, width):
    for axis, dim in sides:
        size, length = (lax.axis_size(axis), array.shape[dim])
        up = [(i, (i + 1) % size) for i in range(size - 1)]
        down = [(j, i) for i, j in up]
        last = lax.slice_in_dim(array, length - width, length, axis=dim)
        initial = lax.slice_in_dim(array, 0, width, axis=dim)
        before = lax.ppermute(last, axis, up)
        after = lax.ppermute(initial, axis, down)
        array = jnp.concatenate([before, array, after], axis=dim)
    return array


def apply_operator(field, tiles, scale):
    padded = with_halo(field, (("region", 2), ("node", 3)), 1)
    rows = field.shape[2]
    cols = field.shape[3]
    parts = []
    for i in range(3):
        total = jnp.zeros(field.shape[1:], jnp.float32)
        for s in range(9):
            step_x = s // 3 - 1
            step_y = s % 3 - 1
            beside = padded[:, :, 1 + step_x : 1 + step_x + rows, 1 + step_y : 1 + step_y + cols]
            for j in range(3):
                total = total + tiles[s, i, j][None] * beside[j]
        parts.append(total)
    return jnp.stack(parts) * scale[None, None]


def inverse_factor(gram, width):
    lower = jnp.linalg.cholesky(gram)
    return jax.scipy.linalg.solve_triangular(lower, jnp.eye(width, dtype=jnp.float32), lower=True)


def combine_modes(inverse, block, root):
    return root * jnp.einsum("km,imxy->ikxy", inverse, block, precision=HIGH)


def invariants(modes, mass, pos_x, pos_y):
    weighted = modes * mass[None, None]
    part_t = jnp.sum(weighted, axis=(2, 3))
    rot_x = jnp.sum(weighted[2] * pos_y[None, None, :], axis=(1, 2))
    rot_y = -jnp.sum(weighted[2] * pos_x[None, :, None], axis=(1, 2))
    rot_z = jnp.sum(
        weighted[1] * pos_x[None, :, None] - weighted[0] * pos_y[None, None, :], axis=(1, 2)
    )
    return jnp.concatenate([part_t, jnp.stack([rot_x, rot_y, rot_z])], axis=0)


def per_device(start_modes, stiffness_tiles, free_mask, group_ids, design, node_mass):
    rows = start_modes.shape[2]
    cols = start_modes.shape[3]
    width = start_modes.shape[1]
    groups = design.shape[0]
    regions = lax.axis_size("region")
    columns = lax.axis_size("node")
    total_x = rows * regions
    total_y = cols * columns
    nodes = jnp.float32(total_x * total_y)
    root = jnp.sqrt(nodes)
    freedom = free_mask.astype(jnp.float32)
    onehot = (group_ids[None] == jnp.arange(groups, dtype=jnp.int32)[:, None, None]).astype(
        jnp.float32
    )
    factor = jnp.sum(onehot * design[:, None, None], axis=0)
    scale = freedom * factor
    modes = start_modes
    image = modes
    for step in range(ITERS):
        iterated = 16.0 * freedom[None, None] * modes - apply_operator(
            modes, stiffness_tiles, scale
        )
        gram_local = jnp.einsum("imxy,ikxy->mk", iterated, iterated, precision=HIGH)
        gram = lax.psum(gram_local, ("region", "node"))
        inverse = inverse_factor(gram, width)
        modes = combine_modes(inverse, iterated, root)
    weight = jnp.sum(modes * image, axis=(0, 1)) / factor
    image = apply_operator(modes, stiffness_tiles, scale)
    weight = jnp.sum(modes * image, axis=(0, 1)) / factor
    reduced_local = jnp.einsum("imxy,ikxy->mk", modes, image, precision=HIGH)
    reduced_sum, adjoint_sum = lax.psum(
        (reduced_local, jnp.sum(onehot * weight[None], axis=(1, 2))), ("region", "node")
    )
    reduced = reduced_sum / nodes
    adjoint = adjoint_sum / nodes
    by_column = lax.all_to_all(modes, "node", split_axis=1, concat_axis=3, tiled=True)
    start_x = lax.axis_index("region") * rows
    pos_x = (
        2.0 * ((start_x + jnp.arange(rows, dtype=jnp.int32)).astype(jnp.float32) + 0.5) / total_x
        - 1.0
    )
    pos_y = 2.0 * (jnp.arange(total_y, dtype=jnp.int32).astype(jnp.float32) + 0.5) / total_y - 1.0
    participation = lax.psum(invariants(by_column, node_mass, pos_x, pos_y), "region") / root
    return (modes, by_column, reduced, participation, adjoint)


def solution(mesh):
    placed = (
        P(None, None, "region", "node"),
        P(None, None, None, "region", "node"),
        P("region", "node"),
        P("region", "node"),
        P(),
        P("region", None),
    )
    return jax.shard_map(
        per_device,
        mesh=mesh,
        in_specs=placed,
        out_specs=(
            P(None, None, "region", "node"),
            P(None, "node", "region", None),
            P(),
            P(None, "node"),
            P(),
        ),
        check_vma=False,
    )
```

profile of v0, /device:TPU:1, one launch (start us, length us, event | category | flops | bytes accessed | tf_op | source)
XLA Modules:
  0.0 412.3 jit_solution(4445898719743661301)
XLA Ops:
  3.1 6.3 %collective-permute-start = (f32[3,32,1,128]{3,1,2,0:T(8,128)S(1)}, f32[3,32,1,128]{3,1,2,0:T(8,128)S(1)}, u32[]{:S(2)}, u32[]{:S(2)}) collective-permute-start(f32[3,32,1,128]{3,1,2,0:T(8,128)S(1)} %get-tuple-element.66), channel_id=1, source_target_pairs={{0,32},{32,64},{64,96},{1,33},{33,65},{65,97},{2,34},{34,66},{66,9... | collective-permute-start | bytes 147464 | tf_op jit(solution)/shard_map/ppermute | solution.py:19
  19.8 3.0 copy.91
  22.8 4.1 %collective-permute-start.2 = (f32[3,32,34,1]{2,1,3,0:T(8,128)}, f32[3,32,34,1]{2,1,3,0:T(8,128)}, u32[]{:S(2)}, u32[]{:S(2)}) collective-permute-start(f32[3,32,34,1]{2,1,3,0:T(8,128)} %copy.91), channel_id=1, source_target_pairs={{0,1},{1,2},{2,3},{3,4},{4,5},{5,6},{6,7},{7,8},{8,9},{9,10},{10,1... | collective-permute-start | bytes 39176 | tf_op jit(solution)/shard_map/ppermute | solution.py:19
  33.9 3.4 copy.95
  37.4 7.5 %multiply_add_fusion.8 = (f32[1,32,32,128]{3,1,2,0:T(8,128)S(1)}, f32[1,32,32,128]{3,1,2,0:T(8,128)S(1)}, f32[1,32,32,128]{3,1,2,0:T(8,128)S(1)}) fusion(f32[3,32,33,128]{3,1,2,0:T(8,128)} %copy-done.3, f32[3,32,32,128]{3,1,2,0:T(8,128)} %copy-done.1, f32[3,32,33,128]{3,1,2,0:T(8,128)} %copy-done.10, f32[32,128]{1,0:T(8,128)S(1)} %get-tuple-element.120, ...), kind=kLoop, calls=%fused_computation.104 | loop fusion | flops 9306112 | bytes 8431104 | tf_op jit(solution)/shard_map/add | solution.py:37
  45.4 5.1 %multiply_add_fusion.7 = f32[1,32,32,128]{3,1,2,0:T(8,128)S(1)} fusion(f32[1,32,32,128]{3,1,2,0:T(8,128)S(1)} %get-tuple-element.48, f32[1,32,32,128]{3,1,2,0:T(8,128)S(1)} %get-tuple-element.47, f32[3,32,33,128]{3,1,2,0:T(8,128)S(1)} %copy-done.4, f32[3,32,32,128]{3,1,2,0:T(8,128)S(1)} %copy-done.2, f32[3,32,33,128]{3,1,2,0:T(8,128)S(1)} %copy-done.11, ...), kind=kLoop, calls=%fused_computation.103 | loop fusion | flops 9043968 | bytes 8431104 | tf_op jit(solution)/shard_map/add | solution.py:37
  50.8 5.0 %multiply_add_fusion.6 = f32[1,32,32,128]{3,1,2,0:T(8,128)S(1)} fusion(f32[1,32,32,128]{3,1,2,0:T(8,128)S(1)} %get-tuple-element.48, f32[1,32,32,128]{3,1,2,0:T(8,128)S(1)} %get-tuple-element.47, f32[3,32,33,128]{3,1,2,0:T(8,128)S(1)} %copy-done.4, f32[3,32,32,128]{3,1,2,0:T(8,128)S(1)} %copy-done.2, f32[3,32,33,128]{3,1,2,0:T(8,128)S(1)} %copy-done.11, ...), kind=kLoop, calls=%fused_computation.102 | loop fusion | flops 9043968 | bytes 8431104 | tf_op jit(solution)/shard_map/add | solution.py:37
  58.9 69.6 %psum.35 = f32[32,32]{0,1:T(8,128)S(1)} all-reduce(f32[32,32]{0,1:T(8,128)S(1)} %convolution_bitcast_fusion.4), channel_id=1, replica_groups=mesh['region'=4,'node'=32] {'region','node'}, use_global_device_ids=true, to_apply=%region_1.0 | all-reduce | flops 1024 | bytes 8192 | tf_op jit(solution)/shard_map/psum | solution.py:86
  128.5 2.9 cholesky.44
  135.5 3.8 fusion.26
  140.5 5.0 %collective-permute-start.4 = (f32[3,32,1,128]{3,1,2,0:T(8,128)S(1)}, f32[3,32,1,128]{3,1,2,0:T(8,128)S(1)}, u32[]{:S(2)}, u32[]{:S(2)}) collective-permute-start(f32[3,32,1,128]{3,1,2,0:T(8,128)S(1)} %get-tuple-element.61), channel_id=1, source_target_pairs={{0,32},{32,64},{64,96},{1,33},{33,65},{65,97},{2,34},{34,66},{66,9... | collective-permute-start | bytes 147464 | tf_op jit(solution)/shard_map/ppermute | solution.py:19
  147.4 5.0 %collective-permute-done.5 = f32[3,32,1,128]{3,1,2,0:T(8,128)S(1)} collective-permute-done((f32[3,32,1,128]{3,1,2,0:T(8,128)S(1)}, f32[3,32,1,128]{3,1,2,0:T(8,128)S(1)}, u32[]{:S(2)}, u32[]{:S(2)}) %collective-permute-start.5) | collective-permute-done | bytes 49184 | tf_op jit(solution)/shard_map/ppermute | solution.py:20
  154.9 3.2 copy.102
  166.8 3.4 copy.105
  173.5 3.1 multiply_add_fusion.5
  177.0 3.2 multiply_add_fusion.4
  180.4 3.4 multiply_add_fusion.3
  187.1 67.7 %psum.36 = f32[32,32]{0,1:T(8,128)S(1)} all-reduce(f32[32,32]{0,1:T(8,128)S(1)} %convolution_bitcast_fusion.2), channel_id=1, replica_groups=mesh['region'=4,'node'=32] {'region','node'}, use_global_device_ids=true, to_apply=%region_4.0 | all-reduce | flops 1024 | bytes 8192 | tf_op jit(solution)/shard_map/psum | solution.py:86
  254.9 2.9 cholesky.55
  261.8 3.0 multiply_bitcast_fusion
  264.8 3.6 collective-permute-start.8
  270.9 4.4 %collective-permute-done.9 = f32[3,32,1,128]{3,1,2,0:T(8,128)S(1)} collective-permute-done((f32[3,32,1,128]{3,1,2,0:T(8,128)S(1)}, f32[3,32,1,128]{3,1,2,0:T(8,128)S(1)}, u32[]{:S(2)}, u32[]{:S(2)}) %collective-permute-start.9) | collective-permute-done | bytes 49184 | tf_op jit(solution)/shard_map/ppermute | solution.py:20
  277.8 3.2 copy.110
  281.0 4.0 collective-permute-start.10
  294.5 8.2 %all-to-all-start = ((f32[3,32,32,128]{3,2,0,1:T(8,128)}), f32[3,32,32,128]{3,2,0,1:T(8,128)S(1)}, u32[]{:S(2)}, u32[]{:S(2)}) async-start(f32[3,32,32,128]{3,2,0,1:T(8,128)} %copy.108), calls=%async_computation | async-start | bytes 3145728 | tf_op jit(solution)/shard_map/all_to_all | solution.py:98
  302.7 3.4 copy.111
  308.9 3.2 maximum_maximum_fusion.1
  312.3 3.1 multiply_add_fusion.2
  315.8 3.2 multiply_add_fusion.1
  319.3 3.1 multiply_add_fusion
  325.1 65.5 %all-reduce = (f32[32,32]{1,0:T(8,128)S(1)}, f32[64]{0:T(128)S(1)}) all-reduce(f32[32,32]{1,0:T(8,128)S(1)} %convolution_bitcast_fusion, f32[64]{0:T(128)S(1)} %select_reduce_fusion), channel_id=1, replica_groups=mesh['region'=4,'node'=32] {'region','node'}, use_global_device_ids=true, to_apply=%region_5.0 | all-reduce | flops 1088 | bytes 8704 | tf_op jit(solution)/shard_map/psum | solution.py:93
  403.9 7.6 %psum.38 = f32[6,1]{0,1:T(1,128)S(1)} all-reduce(f32[6,1]{0,1:T(1,128)S(1)} %pad_maximum_fusion.18), channel_id=1, replica_groups=mesh['region'=4,'node'=32] {'region'}, use_global_device_ids=true, to_apply=%region_10.0 | all-reduce | flops 6 | bytes 48 | tf_op jit(solution)/shard_map/psum | solution.py:105
  (429 shorter events, 84.9 us)
Async XLA Ops:
  0.6 10.7 %copy-start.20 = (f32[9,3,3,32,128]{4,3,2,1,0:T(8,128)S(1)}, f32[9,3,3,32,128]{4,3,2,1,0:T(8,128)}, u32[]{:S(2)}) copy-start(f32[9,3,3,32,128]{4,3,2,1,0:T(8,128)} %param.10) | copy-start | bytes 3981316
  3.1 12.7 %copy-start.1 = (f32[3,32,32,128]{3,1,2,0:T(8,128)}, f32[3,32,32,128]{3,1,2,0:T(8,128)S(1)}, u32[]{:S(2)}) copy-start(f32[3,32,32,128]{3,1,2,0:T(8,128)S(1)} %copy.87) | copy-start | bytes 4718596
  3.1 11.9 %copy-start.171 = (s32[32,128]{1,0:T(8,128)S(1)}, s32[32,128]{1,0:T(8,128)}, u32[]{:S(2)}) copy-start(s32[32,128]{1,0:T(8,128)} %param.12) | copy-start | bytes 49156
  3.1 11.9 %copy-start.173 = (f32[64]{0:T(128)S(1)}, f32[64]{0:T(128)}, u32[]{:S(2)}) copy-start(f32[64]{0:T(128)} %param.13) | copy-start | bytes 772
  3.1 12.7 %copy-start.5 = (f32[3,32,32,128]{3,2,1,0:T(8,128)S(1)}, f32[3,32,32,128]{3,2,1,0:T(8,128)}, u32[]{:S(2)}) copy-start(f32[3,32,32,128]{3,2,1,0:T(8,128)} %param.9) | copy-start | bytes 4718596
  3.1 12.6 %collective-permute-start = (f32[3,32,1,128]{3,1,2,0:T(8,128)S(1)}, f32[3,32,1,128]{3,1,2,0:T(8,128)S(1)}, u32[]{:S(2)}, u32[]{:S(2)}) collective-permute-start(f32[3,32,1,128]{3,1,2,0:T(8,128)S(1)} %get-tuple-element.66), channel_id=1, source_target_pairs={{0,32},{32,64},{64,96},{1,33},{33,65},{65,97},{2,34},{34,66},{66,9... | collective-permute-start | bytes 147464 | tf_op jit(solution)/shard_map/ppermute | solution.py:19
  9.4 7.4 %collective-permute-start.1 = (f32[3,32,1,128]{3,1,2,0:T(8,128)S(1)}, f32[3,32,1,128]{3,1,2,0:T(8,128)S(1)}, u32[]{:S(2)}, u32[]{:S(2)}) collective-permute-start(f32[3,32,1,128]{3,1,2,0:T(8,128)S(1)} %get-tuple-element.67), channel_id=1, source_target_pairs={{32,0},{64,32},{96,64},{33,1},{65,33},{97,65},{34,2},{66,34},{98,6... | collective-permute-start | bytes 147464 | tf_op jit(solution)/shard_map/ppermute | solution.py:20
  22.8 8.7 %collective-permute-start.2 = (f32[3,32,34,1]{2,1,3,0:T(8,128)}, f32[3,32,34,1]{2,1,3,0:T(8,128)}, u32[]{:S(2)}, u32[]{:S(2)}) collective-permute-start(f32[3,32,34,1]{2,1,3,0:T(8,128)} %copy.91), channel_id=1, source_target_pairs={{0,1},{1,2},{2,3},{3,4},{4,5},{5,6},{6,7},{7,8},{8,9},{9,10},{10,1... | collective-permute-start | bytes 39176 | tf_op jit(solution)/shard_map/ppermute | solution.py:19
  28.7 5.2 %collective-permute-start.3 = (f32[3,32,34,1]{2,1,3,0:T(8,128)}, f32[3,32,34,1]{2,1,3,0:T(8,128)}, u32[]{:S(2)}, u32[]{:S(2)}) collective-permute-start(f32[3,32,34,1]{2,1,3,0:T(8,128)} %copy.94), channel_id=1, source_target_pairs={{1,0},{2,1},{3,2},{4,3},{5,4},{6,5},{7,6},{8,7},{9,8},{10,9},{11,1... | collective-permute-start | bytes 39176 | tf_op jit(solution)/shard_map/ppermute | solution.py:20
  37.3 7.7 %copy-start.51 = (f32[32,128]{1,0:T(8,128)S(1)}, f32[32,128]{1,0:T(8,128)}, u32[]{:S(2)}) copy-start(f32[32,128]{1,0:T(8,128)} %get-tuple-element.106) | copy-start | bytes 49156
  37.3 7.7 %copy-start.54 = (f32[32,128]{1,0:T(8,128)S(1)}, f32[32,128]{1,0:T(8,128)}, u32[]{:S(2)}) copy-start(f32[32,128]{1,0:T(8,128)} %get-tuple-element.107) | copy-start | bytes 49156
  37.3 7.7 %copy-start.57 = (f32[32,128]{1,0:T(8,128)S(1)}, f32[32,128]{1,0:T(8,128)}, u32[]{:S(2)}) copy-start(f32[32,128]{1,0:T(8,128)} %get-tuple-element.108) | copy-start | bytes 49156
  37.3 7.7 %copy-start.60 = (f32[32,128]{1,0:T(8,128)S(1)}, f32[32,128]{1,0:T(8,128)}, u32[]{:S(2)}) copy-start(f32[32,128]{1,0:T(8,128)} %get-tuple-element.109) | copy-start | bytes 49156
  37.3 7.7 %copy-start.63 = (f32[32,128]{1,0:T(8,128)S(1)}, f32[32,128]{1,0:T(8,128)}, u32[]{:S(2)}) copy-start(f32[32,128]{1,0:T(8,128)} %get-tuple-element.110) | copy-start | bytes 49156
  37.3 7.7 %copy-start.66 = (f32[32,128]{1,0:T(8,128)S(1)}, f32[32,128]{1,0:T(8,128)}, u32[]{:S(2)}) copy-start(f32[32,128]{1,0:T(8,128)} %get-tuple-element.111) | copy-start | bytes 49156
  37.4 7.7 %copy-start.69 = (f32[32,128]{1,0:T(8,128)S(1)}, f32[32,128]{1,0:T(8,128)}, u32[]{:S(2)}) copy-start(f32[32,128]{1,0:T(8,128)} %get-tuple-element.112) | copy-start | bytes 49156
  37.4 7.7 %copy-start.72 = (f32[32,128]{1,0:T(8,128)S(1)}, f32[32,128]{1,0:T(8,128)}, u32[]{:S(2)}) copy-start(f32[32,128]{1,0:T(8,128)} %get-tuple-element.113) | copy-start | bytes 49156
  37.4 7.7 %copy-start.75 = (f32[32,128]{1,0:T(8,128)S(1)}, f32[32,128]{1,0:T(8,128)}, u32[]{:S(2)}) copy-start(f32[32,128]{1,0:T(8,128)} %get-tuple-element.114) | copy-start | bytes 49156
  37.4 7.7 %copy-start.78 = (f32[32,128]{1,0:T(8,128)S(1)}, f32[32,128]{1,0:T(8,128)}, u32[]{:S(2)}) copy-start(f32[32,128]{1,0:T(8,128)} %get-tuple-element.115) | copy-start | bytes 49156
  45.0 10.9 %copy-start.14 = (f32[1,32,32,128]{3,1,2,0:T(8,128)}, f32[1,32,32,128]{3,1,2,0:T(8,128)S(1)}, u32[]{:S(2)}) copy-start(f32[1,32,32,128]{3,1,2,0:T(8,128)S(1)} %get-tuple-element.46) | copy-start | bytes 1572868
  56.6 78.9 %copy-start.7 = (f32[3,32,32,128]{3,2,1,0:T(8,128)S(1)}, f32[3,32,32,128]{3,2,1,0:T(8,128)}, u32[]{:S(2)}) copy-start(f32[3,32,32,128]{3,2,1,0:T(8,128)} %param.9) | copy-start | bytes 4718596
  56.6 78.9 %copy-start.169 = (f32[32,128]{1,0:T(8,128)S(1)}, f32[32,128]{1,0:T(8,128)}, u32[]{:S(2)}) copy-start(f32[32,128]{1,0:T(8,128)} %get-tuple-element.155) | copy-start | bytes 49156
  140.5 6.9 %collective-permute-start.4 = (f32[3,32,1,128]{3,1,2,0:T(8,128)S(1)}, f32[3,32,1,128]{3,1,2,0:T(8,128)S(1)}, u32[]{:S(2)}, u32[]{:S(2)}) collective-permute-start(f32[3,32,1,128]{3,1,2,0:T(8,128)S(1)} %get-tuple-element.61), channel_id=1, source_target_pairs={{0,32},{32,64},{64,96},{1,33},{33,65},{65,97},{2,34},{34,66},{66,9... | collective-permute-start | bytes 147464 | tf_op jit(solution)/shard_map/ppermute | solution.py:19
  145.5 6.9 %collective-permute-start.5 = (f32[3,32,1,128]{3,1,2,0:T(8,128)S(1)}, f32[3,32,1,128]{3,1,2,0:T(8,128)S(1)}, u32[]{:S(2)}, u32[]{:S(2)}) collective-permute-start(f32[3,32,1,128]{3,1,2,0:T(8,128)S(1)} %get-tuple-element.62), channel_id=1, source_target_pairs={{32,0},{64,32},{96,64},{33,1},{65,33},{97,65},{34,2},{66,34},{98,6... | collective-permute-start | bytes 147464 | tf_op jit(solution)/shard_map/ppermute | solution.py:20
  158.0 5.3 %collective-permute-start.6 = (f32[3,32,34,1]{2,1,3,0:T(8,128)}, f32[3,32,34,1]{2,1,3,0:T(8,128)}, u32[]{:S(2)}, u32[]{:S(2)}) collective-permute-start(f32[3,32,34,1]{2,1,3,0:T(8,128)} %copy.102), channel_id=1, source_target_pairs={{0,1},{1,2},{2,3},{3,4},{4,5},{5,6},{6,7},{7,8},{8,9},{9,10},{10,1... | collective-permute-start | bytes 39176 | tf_op jit(solution)/shard_map/ppermute | solution.py:19
  161.6 5.1 %collective-permute-start.7 = (f32[3,32,34,1]{2,1,3,0:T(8,128)}, f32[3,32,34,1]{2,1,3,0:T(8,128)}, u32[]{:S(2)}, u32[]{:S(2)}) collective-permute-start(f32[3,32,34,1]{2,1,3,0:T(8,128)} %copy.104), channel_id=1, source_target_pairs={{1,0},{2,1},{3,2},{4,3},{5,4},{6,5},{7,6},{8,7},{9,8},{10,9},{11,1... | collective-permute-start | bytes 39176 | tf_op jit(solution)/shard_map/ppermute | solution.py:20
  184.6 77.2 %copy-start.167 = (f32[32,128]{1,0:T(8,128)S(1)}, f32[32,128]{1,0:T(8,128)}, u32[]{:S(2)}) copy-start(f32[32,128]{1,0:T(8,128)} %get-tuple-element.153) | copy-start | bytes 49156
  264.8 6.1 %collective-permute-start.8 = (f32[3,32,1,128]{3,1,2,0:T(8,128)S(1)}, f32[3,32,1,128]{3,1,2,0:T(8,128)S(1)}, u32[]{:S(2)}, u32[]{:S(2)}) collective-permute-start(f32[3,32,1,128]{3,1,2,0:T(8,128)S(1)} %get-tuple-element.59), channel_id=1, source_target_pairs={{0,32},{32,64},{64,96},{1,33},{33,65},{65,97},{2,34},{34,66},{66,9... | collective-permute-start | bytes 147464 | tf_op jit(solution)/shard_map/ppermute | solution.py:19
  268.4 6.9 %collective-permute-start.9 = (f32[3,32,1,128]{3,1,2,0:T(8,128)S(1)}, f32[3,32,1,128]{3,1,2,0:T(8,128)S(1)}, u32[]{:S(2)}, u32[]{:S(2)}) collective-permute-start(f32[3,32,1,128]{3,1,2,0:T(8,128)S(1)} %get-tuple-element.60), channel_id=1, source_target_pairs={{32,0},{64,32},{96,64},{33,1},{65,33},{97,65},{34,2},{66,34},{98,6... | collective-permute-start | bytes 147464 | tf_op jit(solution)/shard_map/ppermute | solution.py:20
  281.0 21.7 %collective-permute-start.10 = (f32[3,32,34,1]{2,1,3,0:T(8,128)}, f32[3,32,34,1]{2,1,3,0:T(8,128)}, u32[]{:S(2)}, u32[]{:S(2)}) collective-permute-start(f32[3,32,34,1]{2,1,3,0:T(8,128)} %copy.110), channel_id=1, source_target_pairs={{0,1},{1,2},{2,3},{3,4},{4,5},{5,6},{6,7},{7,8},{8,9},{9,10},{10,1... | collective-permute-start | bytes 39176 | tf_op jit(solution)/shard_map/ppermute | solution.py:19
  286.6 19.5 %collective-permute-start.11 = (f32[3,32,34,1]{2,1,3,0:T(8,128)}, f32[3,32,34,1]{2,1,3,0:T(8,128)S(1)}, u32[]{:S(2)}, u32[]{:S(2)}) collective-permute-start(f32[3,32,34,1]{2,1,3,0:T(8,128)} %copy.112), channel_id=1, source_target_pairs={{1,0},{2,1},{3,2},{4,3},{5,4},{6,5},{7,6},{8,7},{9,8},{10,9},{11,1... | collective-permute-start | bytes 39176 | tf_op jit(solution)/shard_map/ppermute | solution.py:20
  294.5 97.3 %all-to-all-start = ((f32[3,32,32,128]{3,2,0,1:T(8,128)}), f32[3,32,32,128]{3,2,0,1:T(8,128)S(1)}, u32[]{:S(2)}, u32[]{:S(2)}) async-start(f32[3,32,32,128]{3,2,0,1:T(8,128)} %copy.108), calls=%async_computation | async-start | bytes 3145728 | tf_op jit(solution)/shard_map/all_to_all | solution.py:98
  (156 other events, 601.0 us)
where the time goes:
time: 418 us; the launch traced here: 412 us
  blocking collectives  210 us (50%)
  other arithmetic  70.7 us (17%)
  local copies, waits for them, and re-layouts  59.5 us (14%)
  starting transfers between devices  43.2 us (10%)
  matrix products  13.5 us (3%)
  waiting for transfers between devices  10.4 us (2%)
  between operations  4.51 us (1%)
    psum x2, blocking collectives, per_device(): gram = lax.psum(gram_local, ('region', 'node'))  137 us
    psum x1, blocking collectives, per_device(): lax.psum((reduced_local, jnp.sum(onehot * weight[None], axis=(1, 2))), ('...  65.5 us
    add x9, other arithmetic, apply_operator(): total = total + tiles[s, i, j][None] * beside[j]  36.7 us
    ppermute x6, starting transfers between devices, with_halo(): before = lax.ppermute(last, axis, up)  24.9 us
    unnamed x356, local copies, waits for them, and re-layouts  14.3 us
    slice x8, local copies, waits for them, and re-layouts, with_halo(): last = lax.slice_in_dim(array, length - width, length, axis=dim)  14.1 us
    ppermute x6, waiting for transfers between devices, with_halo(): after = lax.ppermute(initial, axis, down)  10.4 us
    ppermute x6, starting transfers between devices, with_halo(): after = lax.ppermute(initial, axis, down)  10.2 us
  transfers between devices with their start and end apart: 13, of which 3 were waited for; matrix products, arithmetic and copies ran while one was open for 11% of the time, Pallas kernels for 0%

commit v1 on v0

--- a/solution.py
+++ b/solution.py
@@ -37,6 +37,21 @@
                 total = total + tiles[s, i, j][None] * beside[j]
         parts.append(total)
     return jnp.stack(parts) * scale[None, None]
+
+
+def sum_devices(parts):
+    axes = ("region", "node")
+    devices = lax.axis_size(axes)
+    flat = jnp.concatenate([p.reshape(-1) for p in parts])
+    count = flat.shape[0]
+    flat = jnp.pad(flat, (0, -count % 1024))
+    copies = jnp.broadcast_to(flat[None], (devices, flat.shape[0]))
+    total = jnp.sum(lax.all_to_all(copies, axes, 0, 0, tiled=True), axis=0)
+    out, at = [], 0
+    for p in parts:
+        out.append(total[at : at + p.size].reshape(p.shape))
+        at += p.size
+    return out
 
 
 def inverse_factor(gram, width):
@@ -83,15 +98,15 @@
             modes, stiffness_tiles, scale
         )
         gram_local = jnp.einsum("imxy,ikxy->mk", iterated, iterated, precision=HIGH)
-        gram = lax.psum(gram_local, ("region", "node"))
+        (gram,) = sum_devices([gram_local])
         inverse = inverse_factor(gram, width)
         modes = combine_modes(inverse, iterated, root)
     weight = jnp.sum(modes * image, axis=(0, 1)) / factor
     image = apply_operator(modes, stiffness_tiles, scale)
     weight = jnp.sum(modes * image, axis=(0, 1)) / factor
     reduced_local = jnp.einsum("imxy,ikxy->mk", modes, image, precision=HIGH)
-    reduced_sum, adjoint_sum = lax.psum(
-        (reduced_local, jnp.sum(onehot * weight[None], axis=(1, 2))), ("region", "node")
+    reduced_sum, adjoint_sum = sum_devices(
+        [reduced_local, jnp.sum(onehot * weight[None], axis=(1, 2))]
     )
     reduced = reduced_sum / nodes
     adjoint = adjoint_sum / nodes

time: 418 us -> 310 us (0.74)
  blocking collectives: 210 us -> 62 us
  waiting for transfers between devices: 10.4 us -> 41.6 us
  starting transfers between devices: 43.2 us -> 48.6 us
    psum x3 -> x0, blocking collectives: 203 us -> none  [the longest x2 137 us: per_device(): gram = lax.psum(gram_local, ('region', 'node'))]
    all_to_all x0 -> x2, blocking collectives: none -> 52.6 us  [sum_devices(): total = jnp.sum(lax.all_to_all(copies, axes, 0, 0, tiled=True), axis=0)]
    all_to_all x0 -> x1, waiting for transfers between devices: none -> 16.6 us  [sum_devices(): total = jnp.sum(lax.all_to_all(copies, axes, 0, 0, tiled=True), axis=0)]
    all_to_all x1, waiting for transfers between devices: 0.01 us -> 12.7 us  [per_device(): lax.all_to_all(modes, 'node', split_axis=1, concat_axis=3, tiled=True)]
    all_to_all x0 -> x1, starting transfers between devices: none -> 11.7 us  [sum_devices(): total = jnp.sum(lax.all_to_all(copies, axes, 0, 0, tiled=True), axis=0)]
    unnamed x356 -> x348, local copies, waits for them, and re-layouts: 14.3 us -> 14.7 us
  transfers between devices with their start and end apart: 13 -> 14, of which waited for: 3 -> 6; matrix products, arithmetic and copies ran while one was open for 11% -> 10% of each run, Pallas kernels for 0% -> 0%
where the time goes in v1:
time: 310 us; the launch traced here: 304 us
  other arithmetic  71.1 us (23%)
  local copies, waits for them, and re-layouts  62.9 us (20%)
  blocking collectives  62 us (20%)
  starting transfers between devices  48.6 us (16%)
  waiting for transfers between devices  41.6 us (13%)
  matrix products  13.4 us (4%)
  between operations  4.53 us (1%)
    all_to_all x2, blocking collectives, sum_devices(): total = jnp.sum(lax.all_to_all(copies, axes, 0, 0, tiled=True), axis=0)  52.6 us
    add x9, other arithmetic, apply_operator(): total = total + tiles[s, i, j][None] * beside[j]  36.3 us
    ppermute x6, starting transfers between devices, with_halo(): before = lax.ppermute(last, axis, up)  22.5 us
    all_to_all x1, waiting for transfers between devices, sum_devices(): total = jnp.sum(lax.all_to_all(copies, axes, 0, 0, tiled=True), axis=0)  16.6 us
    unnamed x348, local copies, waits for them, and re-layouts  14.7 us
    all_to_all x1, waiting for transfers between devices, per_device(): lax.all_to_all(modes, 'node', split_axis=1, concat_axis=3, tiled=True)  12.7 us
    slice x8, local copies, waits for them, and re-layouts, with_halo(): last = lax.slice_in_dim(array, length - width, length, axis=dim)  12.6 us
    ppermute x6, waiting for transfers between devices, with_halo(): after = lax.ppermute(initial, axis, down)  12.2 us
  transfers between devices with their start and end apart: 14, of which 6 were waited for; matrix products, arithmetic and copies ran while one was open for 10% of the time, Pallas kernels for 0%

profile of v1, /device:TPU:1, one launch (start us, length us, event | category | flops | bytes accessed | tf_op | source)
XLA Modules:
  0.0 304.3 jit_solution(15033233832836620953)
XLA Ops:
  3.1 6.3 %collective-permute-start = (f32[3,32,1,128]{3,1,2,0:T(8,128)S(1)}, f32[3,32,1,128]{3,1,2,0:T(8,128)S(1)}, u32[]{:S(2)}, u32[]{:S(2)}) collective-permute-start(f32[3,32,1,128]{3,1,2,0:T(8,128)S(1)} %get-tuple-element.74), channel_id=1, source_target_pairs={{0,32},{32,64},{64,96},{1,33},{33,65},{65,97},{2,34},{34,66},{66,9... | collective-permute-start | bytes 147464 | tf_op jit(solution)/shard_map/ppermute | solution.py:19
  20.3 3.0 copy.129
  23.3 4.1 %collective-permute-start.2 = (f32[3,32,34,1]{2,1,3,0:T(8,128)}, f32[3,32,34,1]{2,1,3,0:T(8,128)}, u32[]{:S(2)}, u32[]{:S(2)}) collective-permute-start(f32[3,32,34,1]{2,1,3,0:T(8,128)} %copy.129), channel_id=1, source_target_pairs={{0,1},{1,2},{2,3},{3,4},{4,5},{5,6},{6,7},{7,8},{8,9},{9,10},{10,1... | collective-permute-start | bytes 39176 | tf_op jit(solution)/shard_map/ppermute | solution.py:19
  34.4 3.4 %copy.133 = f32[3,32,34,1]{3,1,2,0:T(8,128)} copy(f32[3,32,34,1]{2,1,3,0:T(8,128)} %collective-permute-done.3) | data formatting | bytes 26112 | tf_op jit(solution)/shard_map/ppermute | solution.py:20
  37.9 7.4 %multiply_add_fusion.8 = (f32[1,32,32,128]{3,1,2,0:T(8,128)S(1)}, f32[1,32,32,128]{3,1,2,0:T(8,128)S(1)}, f32[1,32,32,128]{3,1,2,0:T(8,128)S(1)}) fusion(f32[3,32,33,128]{3,1,2,0:T(8,128)} %copy-done.3, f32[3,32,32,128]{3,1,2,0:T(8,128)} %copy-done.1, f32[3,32,33,128]{3,1,2,0:T(8,128)} %copy-done.8, f32[32,128]{1,0:T(8,128)S(1)} %get-tuple-element.128, ...), kind=kLoop, calls=%fused_computation.104 | loop fusion | flops 9306112 | bytes 8431104 | tf_op jit(solution)/shard_map/add | solution.py:37
  45.7 5.1 %multiply_add_fusion.7 = f32[1,32,32,128]{3,1,2,0:T(8,128)S(1)} fusion(f32[1,32,32,128]{3,1,2,0:T(8,128)S(1)} %get-tuple-element.56, f32[1,32,32,128]{3,1,2,0:T(8,128)S(1)} %get-tuple-element.55, f32[3,32,33,128]{3,1,2,0:T(8,128)S(1)} %copy-done.4, f32[3,32,32,128]{3,1,2,0:T(8,128)S(1)} %copy-done.2, f32[3,32,33,128]{3,1,2,0:T(8,128)S(1)} %copy-done.9, ...), kind=kLoop, calls=%fused_computation.103 | loop fusion | flops 9043968 | bytes 8431104 | tf_op jit(solution)/shard_map/add | solution.py:37
  51.1 5.0 %multiply_add_fusion.6 = f32[1,32,32,128]{3,1,2,0:T(8,128)S(1)} fusion(f32[1,32,32,128]{3,1,2,0:T(8,128)S(1)} %get-tuple-element.56, f32[1,32,32,128]{3,1,2,0:T(8,128)S(1)} %get-tuple-element.55, f32[3,32,33,128]{3,1,2,0:T(8,128)S(1)} %copy-done.4, f32[3,32,32,128]{3,1,2,0:T(8,128)S(1)} %copy-done.2, f32[3,32,33,128]{3,1,2,0:T(8,128)S(1)} %copy-done.9, ...), kind=kLoop, calls=%fused_computation.102 | loop fusion | flops 9043968 | bytes 8431104 | tf_op jit(solution)/shard_map/add | solution.py:37
  59.5 26.8 %all_to_all.36 = f32[128,1,1024]{2,1,0:T(1,128)S(1)} all-to-all(f32[128,1,1024]{2,1,0:T(1,128)S(1)} %broadcast_in_dim.12), channel_id=1, replica_groups=mesh['region'=4,'node'=32] {'region','node'}, dimensions={0} | all-to-all | bytes 1048576 | tf_op jit(solution)/shard_map/all_to_all | solution.py:49
  93.8 3.8 %fusion.26 = f32[3,32,128,32]{2,3,1,0:T(8,128)S(1)} fusion(f32[32,32,1,1]{1,0,3,2:T(8,128)S(1)} %convolution_bitcast_fusion.3, f32[1,32,32,128]{3,1,2,0:T(8,128)} %copy-done.16, f32[1,32,32,128]{3,1,2,0:T(8,128)} %copy-done.13, f32[1,32,32,128]{3,1,2,0:T(8,128)} %copy-done.11, f32[32,128]{1,0:T(8,128)S(1)} %get-tuple-element.162, ...), kind=kOutput, calls=%fused_computation.106 | convolution fusion | flops 152961024 | bytes 4755456 | tf_op jit(solution)/shard_map/km,imxy->ikxy/dot_general | solution.py:63
  97.9 3.3 %collective-permute-start.4 = (f32[3,32,1,128]{3,1,2,0:T(8,128)S(1)}, f32[3,32,1,128]{3,1,2,0:T(8,128)S(1)}, u32[]{:S(2)}, u32[]{:S(2)}) collective-permute-start(f32[3,32,1,128]{3,1,2,0:T(8,128)S(1)} %get-tuple-element.69), channel_id=1, source_target_pairs={{0,32},{32,64},{64,96},{1,33},{33,65},{65,97},{2,34},{34,66},{66,9... | collective-permute-start | bytes 147464 | tf_op jit(solution)/shard_map/ppermute | solution.py:19
  103.1 5.0 %collective-permute-done.5 = f32[3,32,1,128]{3,1,2,0:T(8,128)S(1)} collective-permute-done((f32[3,32,1,128]{3,1,2,0:T(8,128)S(1)}, f32[3,32,1,128]{3,1,2,0:T(8,128)S(1)}, u32[]{:S(2)}, u32[]{:S(2)}) %collective-permute-start.5) | collective-permute-done | bytes 49184 | tf_op jit(solution)/shard_map/ppermute | solution.py:20
  115.4 3.0 copy.142
  123.6 3.4 %copy.143 = f32[3,32,34,1]{3,1,2,0:T(8,128)} copy(f32[3,32,34,1]{2,1,3,0:T(8,128)} %collective-permute-done.7) | data formatting | bytes 26112 | tf_op jit(solution)/shard_map/ppermute | solution.py:20
  127.2 3.2 %maximum_maximum_fusion = (f32[3,32,34,129]{3,1,2,0:T(8,128)S(1)}, f32[3,32,34,129]{3,1,2,0:T(8,128)S(1)}) fusion(f32[3,32,1,128]{3,1,2,0:T(8,128)S(1)} %collective-permute-done.5, f32[3,32,32,128]{3,1,2,0:T(8,128)S(1)} %multiply_bitcast_fusion.1, f32[3,32,1,128]{3,1,2,0:T(8,128)S(1)} %collective-permute-done.4, f32[3,32,34,1]{3,1,2,0:T(8,128)} %copy.141, ...), kind=kLoop, calls=%fused_computation.32 | loop fusion | flops 2526336 | bytes 5065728 | tf_op jit(solution)/shard_map/concatenate | solution.py:21
  130.6 3.1 %multiply_add_fusion.5 = (f32[1,32,32,128]{3,1,2,0:T(8,128)S(1)}, f32[1,32,32,128]{3,1,2,0:T(8,128)S(1)}, f32[1,32,32,128]{3,1,2,0:T(8,128)S(1)}, f32[1,32,32,12...) fusion(f32[3,32,34,129]{3,1,2,0:T(8,128)S(1)} %get-tuple-elemen, ...), kind=kLoop, calls=%fused_computation.101 | loop fusion | flops 7733248 | bytes 16793600 | tf_op jit(solution)/shard_map/add | solution.py:37
  134.1 3.2 %multiply_add_fusion.4 = f32[1,32,32,128]{3,1,2,0:T(8,128)S(1)} fusion(f32[1,32,32,128]{3,1,2,0:T(8,128)S(1)} %get-tuple-element.53, f32[1,32,32,128]{3,1,2,0:T(8,128)S(1)} %get-tuple-element.52, f32[1,32,32,128]{3,1,2,0:T(8,128)S(1)} %get-tuple-element.51, f32[1,32,32,128]{3,1,2,0:T(8,128)S(1)} %get-tuple-element.50, ...), kind=kLoop, calls=%fused_computation.100 | loop fusion | flops 6946816 | bytes 15122432 | tf_op jit(solution)/shard_map/add | solution.py:37
  137.6 3.1 %multiply_add_fusion.3 = f32[1,32,32,128]{3,1,2,0:T(8,128)S(1)} fusion(f32[1,32,32,128]{3,1,2,0:T(8,128)S(1)} %get-tuple-element.53, f32[1,32,32,128]{3,1,2,0:T(8,128)S(1)} %get-tuple-element.52, f32[1,32,32,128]{3,1,2,0:T(8,128)S(1)} %get-tuple-element.51, f32[1,32,32,128]{3,1,2,0:T(8,128)S(1)} %get-tuple-element.50, ...), kind=kLoop, calls=%fused_computation.99 | loop fusion | flops 6946816 | bytes 15122432 | tf_op jit(solution)/shard_map/add | solution.py:37
  144.3 25.9 %all_to_all.37 = f32[128,1,1024]{2,1,0:T(1,128)S(1)} all-to-all(f32[128,1,1024]{2,1,0:T(1,128)S(1)} %broadcast_in_dim.14), channel_id=1, replica_groups=mesh['region'=4,'node'=32] {'region','node'}, dimensions={0} | all-to-all | bytes 1048576 | tf_op jit(solution)/shard_map/all_to_all | solution.py:49
  177.7 3.0 multiply_bitcast_fusion
  180.6 3.2 %collective-permute-start.8 = (f32[3,32,1,128]{3,1,2,0:T(8,128)S(1)}, f32[3,32,1,128]{3,1,2,0:T(8,128)S(1)}, u32[]{:S(2)}, u32[]{:S(2)}) collective-permute-start(f32[3,32,1,128]{3,1,2,0:T(8,128)S(1)} %get-tuple-element.67), channel_id=1, source_target_pairs={{0,32},{32,64},{64,96},{1,33},{33,65},{65,97},{2,34},{34,66},{66,9... | collective-permute-start | bytes 147464 | tf_op jit(solution)/shard_map/ppermute | solution.py:19
  185.8 5.0 %collective-permute-done.9 = f32[3,32,1,128]{3,1,2,0:T(8,128)S(1)} collective-permute-done((f32[3,32,1,128]{3,1,2,0:T(8,128)S(1)}, f32[3,32,1,128]{3,1,2,0:T(8,128)S(1)}, u32[]{:S(2)}, u32[]{:S(2)}) %collective-permute-start.9) | collective-permute-done | bytes 49184 | tf_op jit(solution)/shard_map/ppermute | solution.py:20
  192.7 3.0 copy.148
  195.8 3.1 %collective-permute-start.10 = (f32[3,32,34,1]{2,1,3,0:T(8,128)}, f32[3,32,34,1]{2,1,3,0:T(8,128)}, u32[]{:S(2)}, u32[]{:S(2)}) collective-permute-start(f32[3,32,34,1]{2,1,3,0:T(8,128)} %copy.148), channel_id=1, source_target_pairs={{0,1},{1,2},{2,3},{3,4},{4,5},{5,6},{6,7},{7,8},{8,9},{9,10},{10,1... | collective-permute-start | bytes 39176 | tf_op jit(solution)/shard_map/ppermute | solution.py:19
  205.7 3.4 %copy.151 = f32[3,32,34,1]{3,1,2,0:T(8,128)} copy(f32[3,32,34,1]{2,1,3,0:T(8,128)} %collective-permute-done.11) | data formatting | bytes 26112 | tf_op jit(solution)/shard_map/ppermute | solution.py:20
  212.4 3.1 %multiply_add_fusion.2 = (f32[1,32,32,128]{3,1,2,0:T(8,128)S(1)}, f32[1,32,32,128]{3,1,2,0:T(8,128)S(1)}, f32[1,32,32,128]{3,1,2,0:T(8,128)S(1)}, f32[1,32,32,12...) fusion(f32[3,32,34,129]{3,1,2,0:T(8,128)S(1)} %get-tuple-elemen, ...), kind=kLoop, calls=%fused_computation.98 | loop fusion | flops 7733248 | bytes 16793600 | tf_op jit(solution)/shard_map/add | solution.py:37
  215.9 3.2 %multiply_add_fusion.1 = f32[1,32,32,128]{3,1,2,0:T(8,128)S(1)} fusion(f32[1,32,32,128]{3,1,2,0:T(8,128)S(1)} %get-tuple-element.46, f32[1,32,32,128]{3,1,2,0:T(8,128)S(1)} %get-tuple-element.45, f32[1,32,32,128]{3,1,2,0:T(8,128)S(1)} %get-tuple-element.44, f32[1,32,32,128]{3,1,2,0:T(8,128)S(1)} %get-tuple-element.43, ...), kind=kLoop, calls=%fused_computation.97 | loop fusion | flops 6946816 | bytes 15122432 | tf_op jit(solution)/shard_map/add | solution.py:37
  219.3 3.0 multiply_add_fusion
  226.6 11.7 %all-to-all-start.3 = ((f32[128,1,2048]{2,1,0:T(1,128)}), f32[128,1,2048]{2,1,0:T(1,128)S(1)}, u32[]{:S(2)}, u32[]{:S(2)}) async-start(f32[128,1,2048]{2,1,0:T(1,128)} %broadcast_in_dim.15), calls=%async_computation.3 | async-start | bytes 2097152 | tf_op jit(solution)/shard_map/all_to_all | solution.py:49
  240.4 16.6 %all-to-all-done.3 = f32[128,1,2048]{2,1,0:T(1,128)S(1)} async-done(((f32[128,1,2048]{2,1,0:T(1,128)}), f32[128,1,2048]{2,1,0:T(1,128)S(1)}, u32[]{:S(2)}, u32[]{:S(2)}) %all-to-all-start.3) | async-done | bytes 1048608 | tf_op jit(solution)/shard_map/all_to_all | solution.py:49
  258.0 4.2 %all-to-all-start.2 = ((f32[3,32,32,128]{3,2,0,1:T(8,128)}), f32[3,32,32,128]{3,2,0,1:T(8,128)S(1)}, u32[]{:S(2)}, u32[]{:S(2)}) async-start(f32[3,32,32,128]{3,2,0,1:T(8,128)} %copy.146), calls=%async_computation.2 | async-start | bytes 3145728 | tf_op jit(solution)/shard_map/all_to_all | solution.py:113
  269.3 12.7 %all-to-all-done.2 = f32[3,32,32,128]{3,2,0,1:T(8,128)S(1)} async-done(((f32[3,32,32,128]{3,2,0,1:T(8,128)}), f32[3,32,32,128]{3,2,0,1:T(8,128)S(1)}, u32[]{:S(2)}, u32[]{:S(2)}) %all-to-all-start.2) | async-done | bytes 1572896 | tf_op jit(solution)/shard_map/all_to_all | solution.py:113
  294.1 9.4 %psum.7 = f32[6,1]{0,1:T(1,128)S(1)} all-reduce(f32[6,1]{0,1:T(1,128)S(1)} %pad_maximum_fusion.18), channel_id=1, replica_groups=mesh['region'=4,'node'=32] {'region'}, use_global_device_ids=true, to_apply=%region_12.15 | all-reduce | flops 6 | bytes 48 | tf_op jit(solution)/shard_map/psum | solution.py:120
  (435 shorter events, 96.9 us)
Async XLA Ops:
  0.6 10.7 %copy-start.17 = (f32[9,3,3,32,128]{4,3,2,1,0:T(8,128)S(1)}, f32[9,3,3,32,128]{4,3,2,1,0:T(8,128)}, u32[]{:S(2)}) copy-start(f32[9,3,3,32,128]{4,3,2,1,0:T(8,128)} %param.10) | copy-start | bytes 3981316
  3.1 12.7 %copy-start.1 = (f32[3,32,32,128]{3,1,2,0:T(8,128)}, f32[3,32,32,128]{3,1,2,0:T(8,128)S(1)}, u32[]{:S(2)}) copy-start(f32[3,32,32,128]{3,1,2,0:T(8,128)S(1)} %copy.125) | copy-start | bytes 4718596
  3.1 11.9 %copy-start.168 = (s32[32,128]{1,0:T(8,128)S(1)}, s32[32,128]{1,0:T(8,128)}, u32[]{:S(2)}) copy-start(s32[32,128]{1,0:T(8,128)} %param.12) | copy-start | bytes 49156
  3.1 11.9 %copy-start.170 = (f32[64]{0:T(128)S(1)}, f32[64]{0:T(128)}, u32[]{:S(2)}) copy-start(f32[64]{0:T(128)} %param.13) | copy-start | bytes 772
  3.1 12.6 %copy-start.5 = (f32[3,32,32,128]{3,2,1,0:T(8,128)S(1)}, f32[3,32,32,128]{3,2,1,0:T(8,128)}, u32[]{:S(2)}) copy-start(f32[3,32,32,128]{3,2,1,0:T(8,128)} %param.9) | copy-start | bytes 4718596
  3.1 12.6 %collective-permute-start = (f32[3,32,1,128]{3,1,2,0:T(8,128)S(1)}, f32[3,32,1,128]{3,1,2,0:T(8,128)S(1)}, u32[]{:S(2)}, u32[]{:S(2)}) collective-permute-start(f32[3,32,1,128]{3,1,2,0:T(8,128)S(1)} %get-tuple-element.74), channel_id=1, source_target_pairs={{0,32},{32,64},{64,96},{1,33},{33,65},{65,97},{2,34},{34,66},{66,9... | collective-permute-start | bytes 147464 | tf_op jit(solution)/shard_map/ppermute | solution.py:19
  9.4 7.3 %collective-permute-start.1 = (f32[3,32,1,128]{3,1,2,0:T(8,128)S(1)}, f32[3,32,1,128]{3,1,2,0:T(8,128)S(1)}, u32[]{:S(2)}, u32[]{:S(2)}) collective-permute-start(f32[3,32,1,128]{3,1,2,0:T(8,128)S(1)} %get-tuple-element.75), channel_id=1, source_target_pairs={{32,0},{64,32},{96,64},{33,1},{65,33},{97,65},{34,2},{66,34},{98,6... | collective-permute-start | bytes 147464 | tf_op jit(solution)/shard_map/ppermute | solution.py:20
  23.3 8.7 %collective-permute-start.2 = (f32[3,32,34,1]{2,1,3,0:T(8,128)}, f32[3,32,34,1]{2,1,3,0:T(8,128)}, u32[]{:S(2)}, u32[]{:S(2)}) collective-permute-start(f32[3,32,34,1]{2,1,3,0:T(8,128)} %copy.129), channel_id=1, source_target_pairs={{0,1},{1,2},{2,3},{3,4},{4,5},{5,6},{6,7},{7,8},{8,9},{9,10},{10,1... | collective-permute-start | bytes 39176 | tf_op jit(solution)/shard_map/ppermute | solution.py:19
  29.2 5.2 %collective-permute-start.3 = (f32[3,32,34,1]{2,1,3,0:T(8,128)}, f32[3,32,34,1]{2,1,3,0:T(8,128)}, u32[]{:S(2)}, u32[]{:S(2)}) collective-permute-start(f32[3,32,34,1]{2,1,3,0:T(8,128)} %copy.132), channel_id=1, source_target_pairs={{1,0},{2,1},{3,2},{4,3},{5,4},{6,5},{7,6},{8,7},{9,8},{10,9},{11,1... | collective-permute-start | bytes 39176 | tf_op jit(solution)/shard_map/ppermute | solution.py:20
  37.8 7.6 %copy-start.48 = (f32[32,128]{1,0:T(8,128)S(1)}, f32[32,128]{1,0:T(8,128)}, u32[]{:S(2)}) copy-start(f32[32,128]{1,0:T(8,128)} %get-tuple-element.114) | copy-start | bytes 49156
  37.8 7.6 %copy-start.51 = (f32[32,128]{1,0:T(8,128)S(1)}, f32[32,128]{1,0:T(8,128)}, u32[]{:S(2)}) copy-start(f32[32,128]{1,0:T(8,128)} %get-tuple-element.115) | copy-start | bytes 49156
  37.8 7.6 %copy-start.54 = (f32[32,128]{1,0:T(8,128)S(1)}, f32[32,128]{1,0:T(8,128)}, u32[]{:S(2)}) copy-start(f32[32,128]{1,0:T(8,128)} %get-tuple-element.116) | copy-start | bytes 49156
  37.8 7.6 %copy-start.57 = (f32[32,128]{1,0:T(8,128)S(1)}, f32[32,128]{1,0:T(8,128)}, u32[]{:S(2)}) copy-start(f32[32,128]{1,0:T(8,128)} %get-tuple-element.117) | copy-start | bytes 49156
  37.8 7.6 %copy-start.60 = (f32[32,128]{1,0:T(8,128)S(1)}, f32[32,128]{1,0:T(8,128)}, u32[]{:S(2)}) copy-start(f32[32,128]{1,0:T(8,128)} %get-tuple-element.118) | copy-start | bytes 49156
  37.8 7.6 %copy-start.63 = (f32[32,128]{1,0:T(8,128)S(1)}, f32[32,128]{1,0:T(8,128)}, u32[]{:S(2)}) copy-start(f32[32,128]{1,0:T(8,128)} %get-tuple-element.119) | copy-start | bytes 49156
  37.8 7.6 %copy-start.66 = (f32[32,128]{1,0:T(8,128)S(1)}, f32[32,128]{1,0:T(8,128)}, u32[]{:S(2)}) copy-start(f32[32,128]{1,0:T(8,128)} %get-tuple-element.120) | copy-start | bytes 49156
  37.8 7.6 %copy-start.69 = (f32[32,128]{1,0:T(8,128)S(1)}, f32[32,128]{1,0:T(8,128)}, u32[]{:S(2)}) copy-start(f32[32,128]{1,0:T(8,128)} %get-tuple-element.121) | copy-start | bytes 49156
  37.8 7.6 %copy-start.72 = (f32[32,128]{1,0:T(8,128)S(1)}, f32[32,128]{1,0:T(8,128)}, u32[]{:S(2)}) copy-start(f32[32,128]{1,0:T(8,128)} %get-tuple-element.122) | copy-start | bytes 49156
  45.3 10.9 %copy-start.11 = (f32[1,32,32,128]{3,1,2,0:T(8,128)}, f32[1,32,32,128]{3,1,2,0:T(8,128)S(1)}, u32[]{:S(2)}) copy-start(f32[1,32,32,128]{3,1,2,0:T(8,128)S(1)} %get-tuple-element.54) | copy-start | bytes 1572868
  59.2 34.6 %copy-start.7 = (f32[3,32,32,128]{3,2,1,0:T(8,128)S(1)}, f32[3,32,32,128]{3,2,1,0:T(8,128)}, u32[]{:S(2)}) copy-start(f32[3,32,32,128]{3,2,1,0:T(8,128)} %param.9) | copy-start | bytes 4718596
  59.2 34.6 %copy-start.167 = (f32[32,128]{1,0:T(8,128)S(1)}, f32[32,128]{1,0:T(8,128)}, u32[]{:S(2)}) copy-start(f32[32,128]{1,0:T(8,128)} %get-tuple-element.163) | copy-start | bytes 49156
  97.9 5.3 %collective-permute-start.4 = (f32[3,32,1,128]{3,1,2,0:T(8,128)S(1)}, f32[3,32,1,128]{3,1,2,0:T(8,128)S(1)}, u32[]{:S(2)}, u32[]{:S(2)}) collective-permute-start(f32[3,32,1,128]{3,1,2,0:T(8,128)S(1)} %get-tuple-element.69), channel_id=1, source_target_pairs={{0,32},{32,64},{64,96},{1,33},{33,65},{65,97},{2,34},{34,66},{66,9... | collective-permute-start | bytes 147464 | tf_op jit(solution)/shard_map/ppermute | solution.py:19
  101.2 6.9 %collective-permute-start.5 = (f32[3,32,1,128]{3,1,2,0:T(8,128)S(1)}, f32[3,32,1,128]{3,1,2,0:T(8,128)S(1)}, u32[]{:S(2)}, u32[]{:S(2)}) collective-permute-start(f32[3,32,1,128]{3,1,2,0:T(8,128)S(1)} %get-tuple-element.70), channel_id=1, source_target_pairs={{32,0},{64,32},{96,64},{33,1},{65,33},{97,65},{34,2},{66,34},{98,6... | collective-permute-start | bytes 147464 | tf_op jit(solution)/shard_map/ppermute | solution.py:20
  113.0 7.2 %collective-permute-start.6 = (f32[3,32,34,1]{2,1,3,0:T(8,128)S(1)}, f32[3,32,34,1]{2,1,3,0:T(8,128)S(1)}, u32[]{:S(2)}, u32[]{:S(2)}) collective-permute-start(f32[3,32,34,1]{2,1,3,0:T(8,128)S(1)} %copy.140), channel_id=1, source_target_pairs={{0,1},{1,2},{2,3},{3,4},{4,5},{5,6},{6,7},{7,8},{8,9},{9,10},{10,1... | collective-permute-start | bytes 39176 | tf_op jit(solution)/shard_map/ppermute | solution.py:19
  118.5 5.1 %collective-permute-start.7 = (f32[3,32,34,1]{2,1,3,0:T(8,128)}, f32[3,32,34,1]{2,1,3,0:T(8,128)}, u32[]{:S(2)}, u32[]{:S(2)}) collective-permute-start(f32[3,32,34,1]{2,1,3,0:T(8,128)} %copy.142), channel_id=1, source_target_pairs={{1,0},{2,1},{3,2},{4,3},{5,4},{6,5},{7,6},{8,7},{9,8},{10,9},{11,1... | collective-permute-start | bytes 39176 | tf_op jit(solution)/shard_map/ppermute | solution.py:20
  144.0 33.7 %copy-start.165 = (f32[32,128]{1,0:T(8,128)S(1)}, f32[32,128]{1,0:T(8,128)}, u32[]{:S(2)}) copy-start(f32[32,128]{1,0:T(8,128)} %get-tuple-element.161) | copy-start | bytes 49156
  180.6 5.2 %collective-permute-start.8 = (f32[3,32,1,128]{3,1,2,0:T(8,128)S(1)}, f32[3,32,1,128]{3,1,2,0:T(8,128)S(1)}, u32[]{:S(2)}, u32[]{:S(2)}) collective-permute-start(f32[3,32,1,128]{3,1,2,0:T(8,128)S(1)} %get-tuple-element.67), channel_id=1, source_target_pairs={{0,32},{32,64},{64,96},{1,33},{33,65},{65,97},{2,34},{34,66},{66,9... | collective-permute-start | bytes 147464 | tf_op jit(solution)/shard_map/ppermute | solution.py:19
  183.9 6.9 %collective-permute-start.9 = (f32[3,32,1,128]{3,1,2,0:T(8,128)S(1)}, f32[3,32,1,128]{3,1,2,0:T(8,128)S(1)}, u32[]{:S(2)}, u32[]{:S(2)}) collective-permute-start(f32[3,32,1,128]{3,1,2,0:T(8,128)S(1)} %get-tuple-element.68), channel_id=1, source_target_pairs={{32,0},{64,32},{96,64},{33,1},{65,33},{97,65},{34,2},{66,34},{98,6... | collective-permute-start | bytes 147464 | tf_op jit(solution)/shard_map/ppermute | solution.py:20
  195.8 6.1 %collective-permute-start.10 = (f32[3,32,34,1]{2,1,3,0:T(8,128)}, f32[3,32,34,1]{2,1,3,0:T(8,128)}, u32[]{:S(2)}, u32[]{:S(2)}) collective-permute-start(f32[3,32,34,1]{2,1,3,0:T(8,128)} %copy.148), channel_id=1, source_target_pairs={{0,1},{1,2},{2,3},{3,4},{4,5},{5,6},{6,7},{7,8},{8,9},{9,10},{10,1... | collective-permute-start | bytes 39176 | tf_op jit(solution)/shard_map/ppermute | solution.py:19
  200.5 5.1 %collective-permute-start.11 = (f32[3,32,34,1]{2,1,3,0:T(8,128)}, f32[3,32,34,1]{2,1,3,0:T(8,128)}, u32[]{:S(2)}, u32[]{:S(2)}) collective-permute-start(f32[3,32,34,1]{2,1,3,0:T(8,128)} %copy.150), channel_id=1, source_target_pairs={{1,0},{2,1},{3,2},{4,3},{5,4},{6,5},{7,6},{8,7},{9,8},{10,9},{11,1... | collective-permute-start | bytes 39176 | tf_op jit(solution)/shard_map/ppermute | solution.py:20
  226.6 30.5 %all-to-all-start.3 = ((f32[128,1,2048]{2,1,0:T(1,128)}), f32[128,1,2048]{2,1,0:T(1,128)S(1)}, u32[]{:S(2)}, u32[]{:S(2)}) async-start(f32[128,1,2048]{2,1,0:T(1,128)} %broadcast_in_dim.15), calls=%async_computation.3 | async-start | bytes 2097152 | tf_op jit(solution)/shard_map/all_to_all | solution.py:49
  258.0 23.9 %all-to-all-start.2 = ((f32[3,32,32,128]{3,2,0,1:T(8,128)}), f32[3,32,32,128]{3,2,0,1:T(8,128)S(1)}, u32[]{:S(2)}, u32[]{:S(2)}) async-start(f32[3,32,32,128]{3,2,0,1:T(8,128)} %copy.146), calls=%async_computation.2 | async-start | bytes 3145728 | tf_op jit(solution)/shard_map/all_to_all | solution.py:113
  (153 other events, 589.2 us)

commit v2 on v0

v2 whole, which is shorter than its diff:
```python
import jax
import jax.numpy as jnp
from jax import lax
from jax.experimental import pallas as pl
from jax.experimental.pallas import tpu as pltpu
from jax.sharding import PartitionSpec as P

F32 = jnp.float32
BF16 = jnp.bfloat16
ROWS, COLS, MODES, GROUPS = 32, 128, 32, 64
QPAD = 88
VROWS = 9 * MODES
MSG = VROWS + 2 * QPAD
MGS = MODES // 8
VMEM = 100 * 1024 * 1024 // 2
EXTRA = 8
PIECE = 3 * ROWS + EXTRA


def lane_of(shape=(8, COLS)):
    return lax.broadcasted_iota(jnp.int32, shape, 1)


def row_of_lane():
    return ((lane_of() + 1) >> 1) & 63


def pick_lanes(value, even, odd):
    lane = lane_of()
    index = jnp.where(lane % 2 == 0, even, odd)
    return jnp.take_along_axis(value, index, axis=1, mode="promise_in_bounds")


def group(mg):
    return slice(mg * 8, mg * 8 + 8)


def prepare_kernel(v_ref, t_ref, free_ref, gid_ref, design_ref, vt_ref, ct_ref, up_ref, dn_ref, scale, freed):
    free = free_ref[...].astype(F32)
    gid = gid_ref[...]
    factor = jnp.zeros((ROWS, COLS), F32)
    for g in range(GROUPS):
        factor = jnp.where(gid == g, design_ref[g], factor)
    scale[...] = free * factor
    freed[...] = 16.0 * free
    v2 = v_ref.reshape(3 * MODES * ROWS, COLS)
    t2 = t_ref.reshape(81 * ROWS, COLS)
    sub = lax.broadcasted_iota(jnp.int32, (8, COLS), 0)

    def row(x, _):
        for j in range(3):
            for mg in range(MGS):
                vt_ref[j, x, group(mg), :] = v2[pl.ds((j * MODES + mg * 8) * ROWS + x, 8, stride=ROWS), :]
        sc = scale[pl.ds(x, 1), :]
        fr = freed[pl.ds(x, 1), :]
        for qg in range(10):
            c = -sc * t2[pl.ds(qg * 8 * ROWS + x, 8, stride=ROWS), :]
            for q in (36, 40, 44):
                if q // 8 == qg:
                    c = c + jnp.where(sub == q % 8, fr, 0.0)
            ct_ref[x, group(qg), :] = c
        last = -sc * t2[pl.ds(80 * ROWS + x, 1), :]
        ct_ref[x, group(10), :] = jnp.where(sub == 0, last, 0.0)
        return 0

    lax.fori_loop(0, ROWS, row, 0)
    for ref, x0, c0 in ((up_ref, 0, 0), (dn_ref, ROWS - 3, ROWS - 2)):
        for j in range(3):
            for k in range(3):
                at = (j * 3 + k) * MODES
                ref[at : at + MODES, :] = vt_ref[j, x0 + k]
        for k in range(2):
            at = VROWS + k * QPAD
            ref[at : at + QPAD, :] = ct_ref[c0 + k]


def pack_kernel(vt_ref, ct_ref, ru_ref, rd_ref, out_ref):
    rid = row_of_lane()

    def modes_part(n, _):
        j = n // MGS
        mg8 = pl.multiple_of((n % MGS) * 8, 8)
        acc = [jnp.zeros((8, COLS), F32)] * 3
        for b in range(ROWS + 6):
            if b < 3:
                v = ru_ref[pl.ds(pl.multiple_of((j * 3 + b) * MODES + mg8, 8), 8), :]
            elif b < ROWS + 3:
                v = vt_ref[j, b - 3, pl.ds(mg8, 8), :]
            else:
                v = rd_ref[pl.ds(pl.multiple_of((j * 3 + b - ROWS - 3) * MODES + mg8, 8), 8), :]
            for c in range(3):
                acc[c] = jnp.where(rid == b, pick_lanes(v, COLS - 3 + c, 2 - c), acc[c])
        for c in range(3):
            out_ref[pl.ds(pl.multiple_of((j * 3 + c) * MODES + mg8, 8), 8), :] = acc[c]
        return 0

    lax.fori_loop(0, 3 * MGS, modes_part, 0)

    def coef_part(qg, _):
        q8 = pl.multiple_of(qg * 8, 8)
        acc = [jnp.zeros((8, COLS), F32)] * 2
        for b in range(1, ROWS + 5):
            if b < 3:
                v = ru_ref[pl.ds(pl.multiple_of(VROWS + (b - 1) * QPAD + q8, 8), 8), :]
            elif b < ROWS + 3:
                v = ct_ref[b - 3, pl.ds(q8, 8), :]
            else:
                v = rd_ref[pl.ds(pl.multiple_of(VROWS + (b - ROWS - 3) * QPAD + q8, 8), 8), :]
            for c in range(2):
                acc[c] = jnp.where(rid == b, pick_lanes(v, COLS - 2 + c, 1 - c), acc[c])
        for c in range(2):
            out_ref[pl.ds(pl.multiple_of(VROWS + c * QPAD + q8, 8), 8), :] = acc[c]
        return 0

    lax.fori_loop(0, QPAD // 8, coef_part, 0)


def taps():
    for dx in range(3):
        for dy in range(3):
            for j in range(3):
                yield dx, dy, j, (dx * 3 + dy) * 9 + j


def main_stencil(field, coefs, b):
    acc = [[None] * MGS for _ in range(3)]
    for dx, dy, j, q in taps():
        vs = [field[dy, j, b + dx - 1, group(mg), :] for mg in range(MGS)]
        for i in range(3):
            c = coefs[b - 1, pl.ds(q + 3 * i, 1), :]
            for mg in range(MGS):
                term = c * vs[mg]
                acc[i][mg] = term if acc[i][mg] is None else acc[i][mg] + term
    return acc


def edge_stencil(rolled, pl_ref, pr_ref, c):
    even = lane_of((1, COLS)) % 2 == 0
    acc = [[None] * MGS for _ in range(3)]
    at = VROWS + (c - 1) * QPAD
    for dx, dy, j, q in taps():
        mirror = (dx * 3 + 2 - dy) * 9 + j
        vs = [rolled[dx, j, c + dy - 1, group(mg), :] for mg in range(MGS)]
        for i in range(3):
            left = pl_ref[pl.ds(at + q + 3 * i, 1), :]
            right = pr_ref[pl.ds(at + mirror + 3 * i, 1), :]
            k = jnp.where(even, left, right)
            for mg in range(MGS):
                term = k * vs[mg]
                acc[i][mg] = term if acc[i][mg] is None else acc[i][mg] + term
    return acc


def roll_edges(edges, rolled, cs):
    for j in range(3):
        for c in cs:
            for mg in range(MGS):
                v = edges[j, c, group(mg), :]
                rolled[0, j, c, group(mg), :] = pltpu.roll(v, 2, 1)
                rolled[1, j, c, group(mg), :] = v
                rolled[2, j, c, group(mg), :] = pltpu.roll(v, COLS - 2, 1)


def put_row(field, edges, b, j, mg, v, gather):
    lane = lane_of()
    e = pltpu.roll(edges[j, 2, group(mg), :], (2 * COLS - 2 * b) % COLS, 1)
    field[1, j, b, group(mg), :] = v
    field[0, j, b, group(mg), :] = jnp.where(lane == 0, e, pltpu.roll(v, 1, 1))
    field[2, j, b, group(mg), :] = jnp.where(lane == COLS - 1, e, pltpu.roll(v, COLS - 1, 1))
    if gather:
        old = edges[j, 3, group(mg), :]
        edges[j, 3, group(mg), :] = jnp.where(row_of_lane() == b, pick_lanes(v, 0, COLS - 1), old)


def split_store(ref, j, at, x, value):
    lanes = pl.ds(pl.multiple_of(x * COLS, COLS), COLS)
    high = value.astype(BF16)
    ref[j, at : at + MODES, lanes] = high
    ref[j, at + MODES : at + 2 * MODES, lanes] = (value - high.astype(F32)).astype(BF16)


def iterate_kernel(
    vt_ref, ct_ref, ru_ref, rd_ref, pl_ref, pr_ref, mass_ref, x_ref, q_ref,
    field_a, field_b, coefs, edges_a, edges_b, edges_c, rolled, first, masses,
):
    even = lane_of() % 2 == 0
    for k in range(2):
        coefs[k] = ru_ref[VROWS + k * QPAD : VROWS + (k + 1) * QPAD, :]
        coefs[ROWS + 2 + k] = rd_ref[VROWS + k * QPAD : VROWS + (k + 1) * QPAD, :]

    def copy_coefs(x, _):
        coefs[x + 2] = ct_ref[x]
        return 0

    lax.fori_loop(0, ROWS, copy_coefs, 0)
    for j in range(3):
        for c in range(3):
            for mg in range(MGS):
                at = (j * 3 + c) * MODES + mg * 8
                edges_a[j, c, group(mg), :] = jnp.where(even, pl_ref[at : at + 8, :], pr_ref[at : at + 8, :])
    edges_a[:, 3] = jnp.zeros((3, MODES, COLS), F32)
    edges_b[:, 3] = jnp.zeros((3, MODES, COLS), F32)

    for k in range(3):
        for j in range(3):
            for mg in range(MGS):
                at = (j * 3 + k) * MODES + mg * 8
                put_row(field_a, edges_a, k, j, mg, ru_ref[at : at + 8, :], True)
                put_row(field_a, edges_a, ROWS + 3 + k, j, mg, rd_ref[at : at + 8, :], True)

    def load_row(x, _):
        for j in range(3):
            for mg in range(MGS):
                put_row(field_a, edges_a, x + 3, j, mg, vt_ref[j, x, group(mg), :], True)
        return 0

    lax.fori_loop(0, ROWS, load_row, 0)

    roll_edges(edges_a, rolled, range(4))
    for c in (1, 2):
        acc = edge_stencil(rolled, pl_ref, pr_ref, c)
        for i in range(3):
            for mg in range(MGS):
                edges_b[i, c, group(mg), :] = acc[i][mg]

    def first_row(b, _):
        acc = main_stencil(field_a, coefs, b)
        for i in range(3):
            for mg in range(MGS):
                put_row(field_b, edges_b, b, i, mg, acc[i][mg], True)
        return 0

    lax.fori_loop(1, ROWS + 5, first_row, 0)

    roll_edges(edges_b, rolled, (1, 2, 3))
    acc = edge_stencil(rolled, pl_ref, pr_ref, 2)
    for i in range(3):
        for mg in range(MGS):
            edges_c[i, 2, group(mg), :] = acc[i][mg]

    def second_row(b, _):
        acc = main_stencil(field_b, coefs, b)
        for i in range(3):
            for mg in range(MGS):
                put_row(field_a, edges_c, b, i, mg, acc[i][mg], False)
        return 0

    lax.fori_loop(2, ROWS + 4, second_row, 0)

    sub = lax.broadcasted_iota(jnp.int32, (16, COLS), 0)

    def third_row(b, _):
        x = b - 3
        acc = main_stencil(field_a, coefs, b)
        for i in range(3):
            u = field_a[1, i, b]
            split_store(x_ref, i, 0, x, u)
            split_store(x_ref, i, 2 * MODES, x, 16.0 * u - jnp.concatenate(acc[i], axis=0))
            split_store(first, i, 0, x, field_b[1, i, b])
        lanes = pl.ds(pl.multiple_of(x * COLS, COLS), COLS)
        w = jnp.zeros((16, COLS), F32)
        for k in range(3):
            w = jnp.where(sub == k, mass_ref[k, pl.ds(x, 1), :], w)
        high = w.astype(BF16)
        masses[0:16, lanes] = high
        masses[16:32, lanes] = (w - high.astype(F32)).astype(BF16)
        return 0

    lax.fori_loop(3, ROWS + 3, third_row, 0)

    def contract(a, b):
        return lax.dot_general(a, b, (((1,), (1,)), ((), ())), preferred_element_type=F32)

    g1 = jnp.zeros((2 * MODES, 2 * MODES), F32)
    g2 = jnp.zeros((2 * MODES, 4 * MODES), F32)
    sums = []
    for j in range(3):
        u = x_ref[j, 0 : 2 * MODES, :]
        f = first[j]
        g1 = g1 + contract(f, f)
        g2 = g2 + contract(u, x_ref[j])
        p = contract(u, masses[...])
        p = p[:MODES] + p[MODES:]
        sums.append(p[:, 0:3] + p[:, 16:19])
    g1 = g1[:MODES] + g1[MODES:]
    g2 = g2[:MODES] + g2[MODES:]
    q_ref[...] = jnp.zeros((MODES, COLS), F32)
    q_ref[:, 0:32] = g1[:, 0:32] + g1[:, 32:64]
    q_ref[:, 32:64] = g2[:, 0:32] + g2[:, 32:64]
    q_ref[:, 64:96] = g2[:, 64:96] + g2[:, 96:128]
    for j in range(3):
        q_ref[:, 96 + 3 * j : 99 + 3 * j] = sums[j]


def inverse_factor(gram):
    shape = (MODES, 2 * MODES)
    lane = lax.broadcasted_iota(jnp.int32, shape, 1)
    sub = lax.broadcasted_iota(jnp.int32, shape, 0)
    eye = jnp.where(lax.broadcasted_iota(jnp.int32, (MODES, MODES), 0) == lax.broadcasted_iota(jnp.int32, (MODES, MODES), 1), 1.0, 0.0)
    a = jnp.concatenate([gram, eye], axis=1)
    for k in range(MODES):
        f = jnp.where(sub > k, a[:, k : k + 1] / a[k : k + 1, k : k + 1], 0.0)
        a = a - f * a[k : k + 1, :]
    pivots = jnp.sum(jnp.where(lane == sub, a, 0.0), axis=1, keepdims=True)
    return a[:, MODES:] / jnp.sqrt(pivots)


def product(a, b, transposed=False):
    dims = (((1,), (1 if transposed else 0,)), ((), ()))
    return lax.dot_general(a, b, dims, precision=lax.Precision.HIGHEST, preferred_element_type=F32)


def combine_kernel(nodes, q_ref, x_ref, gid_ref, modes_ref, send_ref, small_ref, weight, bins):
    q = q_ref[...]
    w1 = inverse_factor(q[:, 0:32])
    gram = nodes * product(product(w1, q[:, 32:64]), w1, True)
    w = nodes * product(inverse_factor(gram), w1)
    small_ref[...] = jnp.zeros((MODES, COLS), F32)
    small_ref[:, 0:32] = product(product(w, q[:, 64:96]), w, True) / nodes
    small_ref[:, 32:64] = product(w, q[:, 96:128])
    high = w.astype(BF16)
    low = (w - high.astype(F32)).astype(BF16)
    mix = jnp.concatenate([jnp.concatenate([high, high], axis=1), jnp.concatenate([low, low], axis=1)], axis=0)
    m2 = modes_ref.reshape(3 * MODES * ROWS, COLS)
    s2 = send_ref.reshape(MODES * PIECE, COLS)
    step = 4

    def chunk(n, _):
        lanes = pl.ds(pl.multiple_of(n * step * COLS, step * COLS), step * COLS)
        total = jnp.zeros((8, step * COLS), F32)
        for j in range(3):
            v = jnp.dot(mix, x_ref[j, 0 : 2 * MODES, lanes], preferred_element_type=F32)
            z = jnp.dot(mix, x_ref[j, 2 * MODES : 4 * MODES, lanes], preferred_element_type=F32)
            v = v[:MODES] + v[MODES:]
            z = z[:MODES] + z[MODES:]
            vz = v * z
            for mg in range(MGS):
                total = total + vz[group(mg)]
                for k in range(step):
                    piece = v[group(mg), k * COLS : (k + 1) * COLS]
                    x = n * step + k
                    m2[pl.ds((j * MODES + mg * 8) * ROWS + x, 8, stride=ROWS), :] = piece
                    s2[pl.ds(mg * 8 * PIECE + j * ROWS + x, 8, stride=PIECE), :] = piece
        total = jnp.sum(total, axis=0, keepdims=True)
        for k in range(step):
            weight[pl.ds(n * step + k, 1), :] = total[:, k * COLS : (k + 1) * COLS]
        return 0

    lax.fori_loop(0, ROWS // step, chunk, 0)
    gid = gid_ref[...]
    wgt = weight[...]
    for g in range(GROUPS):
        bins[g : g + 1, :] = jnp.sum(jnp.where(gid == g, wgt, 0.0), axis=0, keepdims=True)
    adjoint = product(jnp.ones((8, COLS), F32), bins[...], True)
    adjoint = jnp.concatenate([adjoint, jnp.zeros((8, COLS - GROUPS), F32)], axis=1)

    def put(k, _):
        send_ref[k, 3 * ROWS : PIECE, :] = adjoint
        return 0

    lax.fori_loop(0, MODES, put, 0)


def spread_kernel(columns, recv_ref, out_ref, sum_ref):
    total = jnp.zeros((EXTRA, COLS), F32)
    for n in range(columns):
        for i in range(3):
            out_ref[i, :, n * COLS : (n + 1) * COLS] = recv_ref[n, i * ROWS : (i + 1) * ROWS, :]
        total = total + recv_ref[n, 3 * ROWS : PIECE, :]
    sum_ref[...] = total


def call(kernel, outs, scratch, cost, *args, smem=()):
    flops, size = cost
    return pl.pallas_call(
        kernel,
        out_shape=[jax.ShapeDtypeStruct(s, d) for s, d in outs],
        in_specs=[pl.BlockSpec(memory_space=pltpu.SMEM if k in smem else pltpu.VMEM) for k in range(len(args))],
        out_specs=[pl.BlockSpec(memory_space=pltpu.VMEM) for _ in outs],
        scratch_shapes=[pltpu.VMEM(s, d) for s, d in scratch],
        compiler_params=pltpu.CompilerParams(vmem_limit_bytes=VMEM),
        cost_estimate=pl.CostEstimate(flops=flops, bytes_accessed=size, transcendentals=0),
    )(*args)


def swap(x, axis, k):
    n = lax.axis_size(axis)
    return lax.ppermute(x, axis, [(i, i ^ k) for i in range(n)])


def sum_group(x, axis, generators):
    combos = [0]
    for k in generators:
        combos = combos + [c ^ k for c in combos]
    level = [x if c == 0 else swap(x, axis, c) for c in combos]
    while len(level) > 1:
        level = [level[2 * i] + level[2 * i + 1] for i in range(len(level) // 2)]
    return level[0]


def sum_devices(x):
    x = sum_group(x, "region", (1, 2))
    x = sum_group(x, "node", (1, 2))
    x = sum_group(x, "node", (4, 8))
    return sum_group(x, "node", (16,))


def shift(x, axis, step):
    n = lax.axis_size(axis)
    return lax.ppermute(x, axis, [(i, i + step) for i in range(n) if 0 <= i + step < n])


def per_device(start_modes, stiffness_tiles, free_mask, group_ids, design, node_mass):
    regions = lax.axis_size("region")
    columns = lax.axis_size("node")
    total_x = ROWS * regions
    total_y = COLS * columns
    nodes = float(total_x * total_y)
    region = lax.axis_index("region")
    column = lax.axis_index("node")

    tiles = stiffness_tiles.reshape(81, ROWS, COLS)
    vt, ct, up, dn = call(
        prepare_kernel,
        [((3, ROWS, MODES, COLS), F32), ((ROWS, QPAD, COLS), F32), ((MSG, COLS), F32), ((MSG, COLS), F32)],
        [((ROWS, COLS), F32), ((ROWS, COLS), F32)],
        (1000000, 6000000),
        start_modes, tiles, free_mask, group_ids, design, smem=(4,),
    )
    ru = shift(dn, "region", 1)
    rd = shift(up, "region", -1)
    (packed,) = call(pack_kernel, [((MSG, COLS), F32)], [], (1000000, 4000000), vt, ct, ru, rd)
    left = shift(packed, "node", 1)
    right = shift(packed, "node", -1)

    mass = lax.dynamic_slice(node_mass, (0, column * COLS), (ROWS, COLS))
    xs = (region * ROWS + jnp.arange(ROWS, dtype=jnp.int32)).astype(F32)
    ys = (column * COLS + jnp.arange(COLS, dtype=jnp.int32)).astype(F32)
    pos_x = 2.0 * (xs + 0.5) / total_x - 1.0
    pos_y = 2.0 * (ys + 0.5) / total_y - 1.0
    weights = jnp.stack([mass, mass * pos_x[:, None], mass * pos_y[None, :]])

    field = (3, 3, ROWS + 6, MODES, COLS)
    edge = (3, 4, MODES, COLS)
    x, q = call(
        iterate_kernel,
        [((3, 4 * MODES, ROWS * COLS), BF16), ((MODES, COLS), F32)],
        [
            (field, F32), (field, F32), ((ROWS + 4, QPAD, COLS), F32), (edge, F32), (edge, F32), (edge, F32),
            ((3,) + edge, F32), ((3, 2 * MODES, ROWS * COLS), BF16), ((32, ROWS * COLS), BF16),
        ],
        (100000000, 20000000),
        vt, ct, ru, rd, left, right, weights,
    )
    q = sum_devices(q)
    modes, send, small = call(
        lambda *refs: combine_kernel(nodes, *refs),
        [((3, MODES, ROWS, COLS), F32), ((MODES, PIECE, COLS), F32), ((MODES, COLS), F32)],
        [((ROWS, COLS), F32), ((GROUPS, COLS), F32)],
        (10000000, 10000000),
        q, x, group_ids,
    )
    recv = lax.all_to_all(send, "node", 0, 0, tiled=True)
    by_column, extra = call(
        lambda *refs: spread_kernel(columns, *refs),
        [((3, ROWS, total_y), F32), ((EXTRA, COLS), F32)],
        [],
        (10000, 6000000),
        recv,
    )
    extra = sum_group(extra, "region", (1, 2))
    adjoint = extra[0, :GROUPS] / design / nodes
    reduced = small[:, 0:MODES]
    s = lax.dynamic_slice(small, (column, MODES), (1, 9))[0] / jnp.sqrt(F32(nodes))
    participation = jnp.stack([s[0], s[3], s[6], s[8], -s[7], s[4] - s[2]])[:, None]
    return (modes, by_column[:, None], reduced, participation, adjoint)


def solution(mesh):
    placed = (
        P(None, None, "region", "node"),
        P(None, None, None, "region", "node"),
        P("region", "node"),
        P("region", "node"),
        P(),
        P("region", None),
    )
    return jax.shard_map(
        per_device,
        mesh=mesh,
        in_specs=placed,
        out_specs=(
            P(None, None, "region", "node"),
            P(None, "node", "region", None),
            P(),
            P(None, "node"),
            P(),
        ),
        check_vma=False,
    )
```

time: 418 us -> 150 us (0.36); the launches traced: 412 us -> 149 us
  blocking collectives: 210 us -> 0 us
  other arithmetic: 70.7 us -> 2.14 us
  local copies, waits for them, and re-layouts: 59.5 us -> 8.47 us
  Pallas kernels: 0 us -> 50.7 us
  waiting for transfers between devices: 10.4 us -> 36.3 us
  matrix products: 13.5 us -> 0 us
  starting transfers between devices: 43.2 us -> 48.6 us
    psum x4 -> x0, blocking collectives: 210 us -> none  [the longest x2 137 us: per_device(): gram = lax.psum(gram_local, ('region', 'node'))]
    pallas_call x0 -> x5, Pallas kernels: none -> 50.7 us  [call(): pl.pallas_call(kernel, out_shape=[jax.ShapeDtypeStruct(s, d) for s, d in...]
    add x9 -> x5, other arithmetic: 36.7 us -> 0.03 us  [sum_group(): level = [level[2 * i] + level[2 * i + 1] for i in range(len(level) // 2)]]
    slice x12 -> x1, local copies, waits for them, and re-layouts: 21 us -> 0.69 us  [per_device(): s[2]]
    ppermute x6 -> x0, local copies, waits for them, and re-layouts: 17.6 us -> none  [the longest x3 9.44 us: with_halo(): after = lax.ppermute(initial, axis, down)]
    all_to_all x1, waiting for transfers between devices: 0.01 us -> 17.5 us  [per_device(): recv = lax.all_to_all(send, 'node', 0, 0, tiled=True)]
    dot_general x5 -> x0, matrix products: 13 us -> none  [the longest x2 6.81 us: combine_modes(): return root * jnp.einsum('km,imxy->ikxy', inverse, block, precision=HIGH)]
    another operation x10 -> x2, other arithmetic: 13.4 us -> 0.81 us  [per_device(): weights = jnp.stack([mass, mass * pos_x[:, None], mass * pos_y[None, :]])]
  transfers between devices with their start and end apart: 13 -> 18, of which waited for: 3 -> 12; matrix products, arithmetic and copies ran while one was open for 11% -> 4% of each run, Pallas kernels for 0% -> 0%
where the time goes in v2:
time: 150 us; the launch traced here: 149 us
  Pallas kernels  50.7 us (34%)
  starting transfers between devices  48.6 us (32%)
  waiting for transfers between devices  36.3 us (24%)
  local copies, waits for them, and re-layouts  8.47 us (6%)
  between operations  2.77 us (2%)
  other arithmetic  2.14 us (1%)
    pallas_call x5, Pallas kernels, call(): pl.pallas_call(kernel, out_shape=[jax.ShapeDtypeStruct(s, d) for s, d in...  50.7 us
    ppermute x13, starting transfers between devices, swap(): return lax.ppermute(x, axis, [(i, i ^ k) for i in range(n)])  28.2 us
    all_to_all x1, waiting for transfers between devices, per_device(): recv = lax.all_to_all(send, 'node', 0, 0, tiled=True)  17.5 us
    ppermute x4, starting transfers between devices, shift(): lax.ppermute(x, axis, [(i, i + step) for i in range(n) if 0 <= i + step <...  13.4 us
    ppermute x13, waiting for transfers between devices, swap(): return lax.ppermute(x, axis, [(i, i ^ k) for i in range(n)])  9.61 us
    ppermute x4, waiting for transfers between devices, shift(): lax.ppermute(x, axis, [(i, i + step) for i in range(n) if 0 <= i + step <...  9.18 us
    all_to_all x1, starting transfers between devices, per_device(): recv = lax.all_to_all(send, 'node', 0, 0, tiled=True)  6.99 us
    unnamed x14, local copies, waits for them, and re-layouts  4.82 us
  transfers between devices with their start and end apart: 18, of which 12 were waited for; matrix products, arithmetic and copies ran while one was open for 4% of the time, Pallas kernels for 0%

profile of v2, /device:TPU:1, one launch (start us, length us, event | category | flops | bytes accessed | tf_op | source)
XLA Modules:
  0.0 148.9 jit_solution(8923260992228239207)
XLA Ops:
  0.6 1.3 copy-done.1
  2.0 0.7 copy-done.2
  4.0 5.8 %shard_map.101 = (f32[3,32,32,128]{3,2,1,0:T(8,128)}, f32[32,88,128]{2,1,0:T(8,128)S(1)}, f32[464,128]{1,0:T(8,128)S(1)}, f32[464,128]{1,0:T(8,128)S(1)}) custom-call(f32[3,32,32,128]{3,2,1,0:T(8,128)} %v_ref.1, f32[81,32,128]{2,1,0:T(8,128)S(1)} %bitcast.22, s32[32,128]{1,0:T(8,128)S(1)} %copy-done.4, s32[32,128]{1,0:T(8,128)S(1)} %copy-done.2, f32[64]{0:T(128)S(1)} %copy-done.5), custom_call_target="tpu_custom_call" | custom-call | flops 1000000 | bytes 6000000 | tf_op jit(solution)/shard_map/pallas_call | solution.py:375
  9.9 6.0 %collective-permute-start = (f32[464,128]{1,0:T(8,128)S(1)}, f32[464,128]{1,0:T(8,128)S(1)}, u32[]{:S(2)}, u32[]{:S(2)}) collective-permute-start(f32[464,128]{1,0:T(8,128)S(1)} %get-tuple-element.18), channel_id=1, source_target_pairs={{0,32},{32,64},{64,96},{1,33},{33,65},{65,97},{2,34},{34,66},{66,9... | collective-permute-start | bytes 712712 | tf_op jit(solution)/shard_map/ppermute | solution.py:410
  15.9 1.9 %collective-permute-start.1 = (f32[464,128]{1,0:T(8,128)S(1)}, f32[464,128]{1,0:T(8,128)S(1)}, u32[]{:S(2)}, u32[]{:S(2)}) collective-permute-start(f32[464,128]{1,0:T(8,128)S(1)} %get-tuple-element.19), channel_id=1, source_target_pairs={{32,0},{64,32},{96,64},{33,1},{65,33},{97,65},{34,2},{66,34},{98,6... | collective-permute-start | bytes 712712 | tf_op jit(solution)/shard_map/ppermute | solution.py:410
  17.9 1.1 collective-permute-done.ru_ref
  18.9 5.9 %collective-permute-done.1.rd_ref = f32[464,128]{1,0:T(8,128)S(1)} collective-permute-done((f32[464,128]{1,0:T(8,128)S(1)}, f32[464,128]{1,0:T(8,128)S(1)}, u32[]{:S(2)}, u32[]{:S(2)}) %collective-permute-start.1) | collective-permute-done | bytes 237600 | tf_op jit(solution)/shard_map/ppermute | solution.py:410
  24.8 1.4 copy-done
  26.2 5.9 %shard_map.102 = f32[464,128]{1,0:T(8,128)S(1)} custom-call(f32[3,32,32,128]{3,2,1,0:T(8,128)S(1)} %copy-done, f32[32,88,128]{2,1,0:T(8,128)S(1)} %get-tuple-element.17.ct_ref, f32[464,128]{1,0:T(8,128)S(1)} %collective-permute-done.ru_ref, f32[464,128]{1,0:T(8,128)S(1)} %collective-permute-done.1.rd_ref), custom_call_target="tpu_custom_call" | custom-call | flops 1000000 | bytes 4000000 | tf_op jit(solution)/shard_map/pallas_call | solution.py:375
  32.1 1.3 collective-permute-start.3
  33.4 4.2 %collective-permute-start.2 = (f32[464,128]{1,0:T(8,128)S(1)}, f32[464,128]{1,0:T(8,128)S(1)}, u32[]{:S(2)}, u32[]{:S(2)}) collective-permute-start(f32[464,128]{1,0:T(8,128)S(1)} %shard_map.102), channel_id=1, source_target_pairs={{0,1},{1,2},{2,3},{3,4},{4,5},{5,6},{6,7},{7,8},{8,9},{9,10},{10,1... | collective-permute-start | bytes 712712 | tf_op jit(solution)/shard_map/ppermute | solution.py:410
  37.6 0.8 dynamic-slice_bitcast_fusion
  38.4 0.7 collective-permute-done.3.pr_ref
  39.2 1.5 collective-permute-done.2.pl_ref
  40.7 24.8 %shard_map.103 = (bf16[3,128,4096]{2,1,0:T(8,128)(2,1)}, f32[32,128]{1,0:T(8,128)S(1)}) custom-call(f32[3,32,32,128]{3,2,1,0:T(8,128)S(1)} %copy-done, f32[32,88,128]{2,1,0:T(8,128)S(1)} %get-tuple-element.17.ct_ref, f32[464,128]{1,0:T(8,128)S(1)} %collective-permute-done.ru_ref, f32[464,128]{1,0:T(8,128)S(1)} %collective-permute-done.1.rd_ref, ...), custom_call_target="tpu_custom_call" | custom-call | flops 100000000 | bytes 20000000 | tf_op jit(solution)/shard_map/pallas_call | solution.py:375
  65.5 0.9 collective-permute-start.6
  66.3 2.9 %collective-permute-start.4 = (f32[32,128]{1,0:T(8,128)S(1)}, f32[32,128]{1,0:T(8,128)S(1)}, u32[]{:S(2)}, u32[]{:S(2)}) collective-permute-start(f32[32,128]{1,0:T(8,128)S(1)} %get-tuple-element.20), channel_id=1, source_target_pairs={{0,32},{32,0},{64,96},{96,64},{1,33},{33,1},{65,97},{97,65},{2,34}... | collective-permute-start | bytes 49160 | tf_op jit(solution)/shard_map/ppermute | solution.py:388
  69.2 1.0 collective-permute-done.6
  70.8 5.6 %collective-permute-start.9 = (f32[32,128]{1,0:T(8,128)S(1)}, f32[32,128]{1,0:T(8,128)S(1)}, u32[]{:S(2)}, u32[]{:S(2)}) collective-permute-start(f32[32,128]{1,0:T(8,128)S(1)} %add_add_fusion.2), channel_id=1, source_target_pairs={{0,3},{1,2},{2,1},{3,0},{4,7},{5,6},{6,5},{7,4},{8,11},{9,10},{10,... | collective-permute-start | bytes 49160 | tf_op jit(solution)/shard_map/ppermute | solution.py:388
  77.6 3.0 %collective-permute-done.8 = f32[32,128]{1,0:T(8,128)S(1)} collective-permute-done((f32[32,128]{1,0:T(8,128)S(1)}, f32[32,128]{1,0:T(8,128)S(1)}, u32[]{:S(2)}, u32[]{:S(2)}) %collective-permute-start.8) | collective-permute-done | bytes 16416 | tf_op jit(solution)/shard_map/ppermute | solution.py:388
  80.6 4.9 %collective-permute-start.12 = (f32[32,128]{1,0:T(8,128)S(1)}, f32[32,128]{1,0:T(8,128)S(1)}, u32[]{:S(2)}, u32[]{:S(2)}) collective-permute-start(f32[32,128]{1,0:T(8,128)S(1)} %add_add_fusion.1), channel_id=1, source_target_pairs={{0,12},{1,13},{2,14},{3,15},{4,8},{5,9},{6,10},{7,11},{8,4},{9,5},... | collective-permute-start | bytes 49160 | tf_op jit(solution)/shard_map/ppermute | solution.py:388
  86.6 3.0 %collective-permute-done.11 = f32[32,128]{1,0:T(8,128)S(1)} collective-permute-done((f32[32,128]{1,0:T(8,128)S(1)}, f32[32,128]{1,0:T(8,128)S(1)}, u32[]{:S(2)}, u32[]{:S(2)}) %collective-permute-start.11) | collective-permute-done | bytes 16416 | tf_op jit(solution)/shard_map/ppermute | solution.py:388
  89.6 2.7 %collective-permute-start.13 = (f32[32,128]{1,0:T(8,128)S(1)}, f32[32,128]{1,0:T(8,128)S(1)}, u32[]{:S(2)}, u32[]{:S(2)}) collective-permute-start(f32[32,128]{1,0:T(8,128)S(1)} %add_add_fusion), channel_id=1, source_target_pairs={{0,16},{1,17},{2,18},{3,19},{4,20},{5,21},{6,22},{7,23},{8,24},{9,... | collective-permute-start | bytes 49160 | tf_op jit(solution)/shard_map/ppermute | solution.py:388
  92.3 1.1 collective-permute-done.13
  93.5 12.9 %shard_map.104 = (f32[3,32,32,128]{3,2,1,0:T(8,128)}, f32[32,104,128]{2,1,0:T(8,128)}, f32[32,128]{1,0:T(8,128)}) custom-call(f32[32,128]{1,0:T(8,128)S(1)} %add.113.refs_0_, bf16[3,128,4096]{2,1,0:T(8,128)(2,1)} %get-tuple-element.21.refs_1_, s32[32,128]{1,0:T(8,128)S(1)} %copy-done.3), custom_call_target="tpu_custom_call" | custom-call | flops 10000000 | bytes 10000000 | tf_op jit(solution)/shard_map/pallas_call | solution.py:375
  106.4 7.0 %all-to-all-start = ((f32[32,104,128]{2,1,0:T(8,128)}), f32[32,104,128]{2,1,0:T(8,128)S(1)}, u32[]{:S(2)}, u32[]{:S(2)}) async-start(f32[32,104,128]{2,1,0:T(8,128)} %get-tuple-element.23), calls=%async_computation | async-start | bytes 3407872 | tf_op jit(solution)/shard_map/all_to_all | solution.py:463
  113.4 0.8 dynamic-slice_multiply_fusion
  114.1 17.5 %all-to-all-done.refs_0_ = f32[32,104,128]{2,1,0:T(8,128)S(1)} async-done(((f32[32,104,128]{2,1,0:T(8,128)}), f32[32,104,128]{2,1,0:T(8,128)S(1)}, u32[]{:S(2)}, u32[]{:S(2)}) %all-to-all-start) | async-done | bytes 1703968 | tf_op jit(solution)/shard_map/all_to_all | solution.py:463
  131.6 1.3 shard_map.105
  132.9 6.8 %collective-permute-start.16 = (f32[8,128]{1,0:T(8,128)S(1)}, f32[8,128]{1,0:T(8,128)S(1)}, u32[]{:S(2)}, u32[]{:S(2)}) collective-permute-start(f32[8,128]{1,0:T(8,128)S(1)} %get-tuple-element.26), channel_id=1, source_target_pairs={{0,96},{32,64},{64,32},{96,0},{1,97},{33,65},{65,33},{97,1},{2,98}... | collective-permute-start | bytes 12296 | tf_op jit(solution)/shard_map/ppermute | solution.py:388
  139.7 3.1 %collective-permute-start.15 = (f32[8,128]{1,0:T(8,128)S(1)}, f32[8,128]{1,0:T(8,128)S(1)}, u32[]{:S(2)}, u32[]{:S(2)}) collective-permute-start(f32[8,128]{1,0:T(8,128)S(1)} %get-tuple-element.26), channel_id=1, source_target_pairs={{0,64},{32,96},{64,0},{96,32},{1,65},{33,97},{65,1},{97,33},{2,66}... | collective-permute-start | bytes 12296 | tf_op jit(solution)/shard_map/ppermute | solution.py:388
  145.4 3.0 %stack.21 = f32[6]{0:T(128)} concatenate(f32[1]{0:T(128)} %bitcast.6, f32[1]{0:T(128)} %bitcast.7, f32[1]{0:T(128)} %bitcast.8, f32[1]{0:T(128)} %bitcast.9, f32[1]{0:T(128)} %bitcast.10, f32[1]{0:T(128)} %bitcast.11), dimensions={0} | concatenate | bytes 48 | tf_op jit(solution)/shard_map/stack | solution.py:475
  (36 shorter events, 5.5 us)
Async XLA Ops:
  0.6 1.3 copy-start.1
  2.0 0.7 copy-start.2
  2.7 0.7 copy-start.4
  3.4 0.7 copy-start.5
  9.9 9.1 %collective-permute-start = (f32[464,128]{1,0:T(8,128)S(1)}, f32[464,128]{1,0:T(8,128)S(1)}, u32[]{:S(2)}, u32[]{:S(2)}) collective-permute-start(f32[464,128]{1,0:T(8,128)S(1)} %get-tuple-element.18), channel_id=1, source_target_pairs={{0,32},{32,64},{64,96},{1,33},{33,65},{65,97},{2,34},{34,66},{66,9... | collective-permute-start | bytes 712712 | tf_op jit(solution)/shard_map/ppermute | solution.py:410
  15.9 8.9 %collective-permute-start.1 = (f32[464,128]{1,0:T(8,128)S(1)}, f32[464,128]{1,0:T(8,128)S(1)}, u32[]{:S(2)}, u32[]{:S(2)}) collective-permute-start(f32[464,128]{1,0:T(8,128)S(1)} %get-tuple-element.19), channel_id=1, source_target_pairs={{32,0},{64,32},{96,64},{33,1},{65,33},{97,65},{34,2},{66,34},{98,6... | collective-permute-start | bytes 712712 | tf_op jit(solution)/shard_map/ppermute | solution.py:410
  24.8 1.4 copy-start
  32.1 7.0 %collective-permute-start.3 = (f32[464,128]{1,0:T(8,128)S(1)}, f32[464,128]{1,0:T(8,128)S(1)}, u32[]{:S(2)}, u32[]{:S(2)}) collective-permute-start(f32[464,128]{1,0:T(8,128)S(1)} %shard_map.102), channel_id=1, source_target_pairs={{1,0},{2,1},{3,2},{4,3},{5,4},{6,5},{7,6},{8,7},{9,8},{10,9},{11,1... | collective-permute-start | bytes 712712 | tf_op jit(solution)/shard_map/ppermute | solution.py:410
  33.4 7.2 %collective-permute-start.2 = (f32[464,128]{1,0:T(8,128)S(1)}, f32[464,128]{1,0:T(8,128)S(1)}, u32[]{:S(2)}, u32[]{:S(2)}) collective-permute-start(f32[464,128]{1,0:T(8,128)S(1)} %shard_map.102), channel_id=1, source_target_pairs={{0,1},{1,2},{2,3},{3,4},{4,5},{5,6},{6,7},{7,8},{8,9},{9,10},{10,1... | collective-permute-start | bytes 712712 | tf_op jit(solution)/shard_map/ppermute | solution.py:410
  38.4 55.0 %copy-start.3 = (s32[32,128]{1,0:T(8,128)S(1)}, s32[32,128]{1,0:T(8,128)}, u32[]{:S(2)}) copy-start(s32[32,128]{1,0:T(8,128)} %refs_2_.1) | copy-start | bytes 49156
  65.5 4.7 %collective-permute-start.6 = (f32[32,128]{1,0:T(8,128)S(1)}, f32[32,128]{1,0:T(8,128)S(1)}, u32[]{:S(2)}, u32[]{:S(2)}) collective-permute-start(f32[32,128]{1,0:T(8,128)S(1)} %get-tuple-element.20), channel_id=1, source_target_pairs={{0,96},{32,64},{64,32},{96,0},{1,97},{33,65},{65,33},{97,1},{2,98}... | collective-permute-start | bytes 49160 | tf_op jit(solution)/shard_map/ppermute | solution.py:388
  66.3 4.5 %collective-permute-start.5 = (f32[32,128]{1,0:T(8,128)S(1)}, f32[32,128]{1,0:T(8,128)S(1)}, u32[]{:S(2)}, u32[]{:S(2)}) collective-permute-start(f32[32,128]{1,0:T(8,128)S(1)} %get-tuple-element.20), channel_id=1, source_target_pairs={{0,64},{32,96},{64,0},{96,32},{1,65},{33,97},{65,1},{97,33},{2,66}... | collective-permute-start | bytes 49160 | tf_op jit(solution)/shard_map/ppermute | solution.py:388
  66.3 4.5 %collective-permute-start.4 = (f32[32,128]{1,0:T(8,128)S(1)}, f32[32,128]{1,0:T(8,128)S(1)}, u32[]{:S(2)}, u32[]{:S(2)}) collective-permute-start(f32[32,128]{1,0:T(8,128)S(1)} %get-tuple-element.20), channel_id=1, source_target_pairs={{0,32},{32,0},{64,96},{96,64},{1,33},{33,1},{65,97},{97,65},{2,34}... | collective-permute-start | bytes 49160 | tf_op jit(solution)/shard_map/ppermute | solution.py:388
  70.8 6.8 %collective-permute-start.9 = (f32[32,128]{1,0:T(8,128)S(1)}, f32[32,128]{1,0:T(8,128)S(1)}, u32[]{:S(2)}, u32[]{:S(2)}) collective-permute-start(f32[32,128]{1,0:T(8,128)S(1)} %add_add_fusion.2), channel_id=1, source_target_pairs={{0,3},{1,2},{2,1},{3,0},{4,7},{5,6},{6,5},{7,4},{8,11},{9,10},{10,... | collective-permute-start | bytes 49160 | tf_op jit(solution)/shard_map/ppermute | solution.py:388
  76.5 4.1 %collective-permute-start.8 = (f32[32,128]{1,0:T(8,128)S(1)}, f32[32,128]{1,0:T(8,128)S(1)}, u32[]{:S(2)}, u32[]{:S(2)}) collective-permute-start(f32[32,128]{1,0:T(8,128)S(1)} %add_add_fusion.2), channel_id=1, source_target_pairs={{0,2},{1,3},{2,0},{3,1},{4,6},{5,7},{6,4},{7,5},{8,10},{9,11},{10,... | collective-permute-start | bytes 49160 | tf_op jit(solution)/shard_map/ppermute | solution.py:388
  76.5 4.1 %collective-permute-start.7 = (f32[32,128]{1,0:T(8,128)S(1)}, f32[32,128]{1,0:T(8,128)S(1)}, u32[]{:S(2)}, u32[]{:S(2)}) collective-permute-start(f32[32,128]{1,0:T(8,128)S(1)} %add_add_fusion.2), channel_id=1, source_target_pairs={{0,1},{1,0},{2,3},{3,2},{4,5},{5,4},{6,7},{7,6},{8,9},{9,8},{10,11... | collective-permute-start | bytes 49160 | tf_op jit(solution)/shard_map/ppermute | solution.py:388
  80.6 6.1 %collective-permute-start.12 = (f32[32,128]{1,0:T(8,128)S(1)}, f32[32,128]{1,0:T(8,128)S(1)}, u32[]{:S(2)}, u32[]{:S(2)}) collective-permute-start(f32[32,128]{1,0:T(8,128)S(1)} %add_add_fusion.1), channel_id=1, source_target_pairs={{0,12},{1,13},{2,14},{3,15},{4,8},{5,9},{6,10},{7,11},{8,4},{9,5},... | collective-permute-start | bytes 49160 | tf_op jit(solution)/shard_map/ppermute | solution.py:388
  85.5 4.1 %collective-permute-start.11 = (f32[32,128]{1,0:T(8,128)S(1)}, f32[32,128]{1,0:T(8,128)S(1)}, u32[]{:S(2)}, u32[]{:S(2)}) collective-permute-start(f32[32,128]{1,0:T(8,128)S(1)} %add_add_fusion.1), channel_id=1, source_target_pairs={{0,8},{1,9},{2,10},{3,11},{4,12},{5,13},{6,14},{7,15},{8,0},{9,1},... | collective-permute-start | bytes 49160 | tf_op jit(solution)/shard_map/ppermute | solution.py:388
  85.5 4.1 %collective-permute-start.10 = (f32[32,128]{1,0:T(8,128)S(1)}, f32[32,128]{1,0:T(8,128)S(1)}, u32[]{:S(2)}, u32[]{:S(2)}) collective-permute-start(f32[32,128]{1,0:T(8,128)S(1)} %add_add_fusion.1), channel_id=1, source_target_pairs={{0,4},{1,5},{2,6},{3,7},{4,0},{5,1},{6,2},{7,3},{8,12},{9,13},{10,... | collective-permute-start | bytes 49160 | tf_op jit(solution)/shard_map/ppermute | solution.py:388
  89.6 3.8 %collective-permute-start.13 = (f32[32,128]{1,0:T(8,128)S(1)}, f32[32,128]{1,0:T(8,128)S(1)}, u32[]{:S(2)}, u32[]{:S(2)}) collective-permute-start(f32[32,128]{1,0:T(8,128)S(1)} %add_add_fusion), channel_id=1, source_target_pairs={{0,16},{1,17},{2,18},{3,19},{4,20},{5,21},{6,22},{7,23},{8,24},{9,... | collective-permute-start | bytes 49160 | tf_op jit(solution)/shard_map/ppermute | solution.py:388
  106.4 25.2 %all-to-all-start = ((f32[32,104,128]{2,1,0:T(8,128)}), f32[32,104,128]{2,1,0:T(8,128)S(1)}, u32[]{:S(2)}, u32[]{:S(2)}) async-start(f32[32,104,128]{2,1,0:T(8,128)} %get-tuple-element.23), calls=%async_computation | async-start | bytes 3407872 | tf_op jit(solution)/shard_map/all_to_all | solution.py:463
  113.4 35.0 %copy-start.6 = (f32[64]{0:T(128)S(1)}, f32[64]{0:T(128)}, u32[]{:S(2)}) copy-start(f32[64]{0:T(128)} %design_ref.1) | copy-start | bytes 772
  132.9 15.5 %collective-permute-start.16 = (f32[8,128]{1,0:T(8,128)S(1)}, f32[8,128]{1,0:T(8,128)S(1)}, u32[]{:S(2)}, u32[]{:S(2)}) collective-permute-start(f32[8,128]{1,0:T(8,128)S(1)} %get-tuple-element.26), channel_id=1, source_target_pairs={{0,96},{32,64},{64,32},{96,0},{1,97},{33,65},{65,33},{97,1},{2,98}... | collective-permute-start | bytes 12296 | tf_op jit(solution)/shard_map/ppermute | solution.py:388
  139.7 8.7 %collective-permute-start.15 = (f32[8,128]{1,0:T(8,128)S(1)}, f32[8,128]{1,0:T(8,128)S(1)}, u32[]{:S(2)}, u32[]{:S(2)}) collective-permute-start(f32[8,128]{1,0:T(8,128)S(1)} %get-tuple-element.26), channel_id=1, source_target_pairs={{0,64},{32,96},{64,0},{96,32},{1,65},{33,97},{65,1},{97,33},{2,66}... | collective-permute-start | bytes 12296 | tf_op jit(solution)/shard_map/ppermute | solution.py:388
  142.7 5.7 %collective-permute-start.14 = (f32[8,128]{1,0:T(8,128)S(1)}, f32[8,128]{1,0:T(8,128)S(1)}, u32[]{:S(2)}, u32[]{:S(2)}) collective-permute-start(f32[8,128]{1,0:T(8,128)S(1)} %get-tuple-element.26), channel_id=1, source_target_pairs={{0,32},{32,0},{64,96},{96,64},{1,33},{33,1},{65,97},{97,65},{2,34}... | collective-permute-start | bytes 12296 | tf_op jit(solution)/shard_map/ppermute | solution.py:388

commit v3 on v2

v3 whole, which is shorter than its diff:
```python
import jax
import jax.numpy as jnp
from jax import lax
from jax.experimental import pallas as pl
from jax.experimental.pallas import tpu as pltpu
from jax.sharding import PartitionSpec as P

F32 = jnp.float32
BF16 = jnp.bfloat16
ROWS, COLS, MODES, GROUPS = 32, 128, 32, 64
QPAD = 88
VROWS = 9 * MODES
MSG = VROWS + 2 * QPAD
MGS = MODES // 8
VMEM = 100 * 1024 * 1024 // 2
EXTRA = 8
PIECE = 3 * ROWS + EXTRA


def lane_of(shape=(8, COLS)):
    return lax.broadcasted_iota(jnp.int32, shape, 1)


def row_of_lane():
    return ((lane_of() + 1) >> 1) & 63


def pick_lanes(value, even, odd):
    lane = lane_of()
    index = jnp.where(lane % 2 == 0, even, odd)
    return jnp.take_along_axis(value, index, axis=1, mode="promise_in_bounds")


def group(mg):
    return slice(mg * 8, mg * 8 + 8)


def diagonal(q0, sub, fr):
    hit = (sub + q0 == 36) | (sub + q0 == 40) | (sub + q0 == 44)
    return jnp.where(hit, fr, 0.0)


def rows_kernel(
    v_hbm, t_hbm, free_ref, gid_ref, design_ref, base_ref, up_ref, dn_ref, v_top, v_end, t_top, t_end, sems
):
    top, end = pl.ds(0, 8), pl.ds(ROWS - 8, 8)
    copies = [
        pltpu.make_async_copy(v_hbm.at[:, :, top, :], v_top, sems.at[0]),
        pltpu.make_async_copy(t_hbm.at[:, top, :], t_top, sems.at[1]),
        pltpu.make_async_copy(v_hbm.at[:, :, end, :], v_end, sems.at[2]),
        pltpu.make_async_copy(t_hbm.at[:, end, :], t_end, sems.at[3]),
    ]
    for copy in copies:
        copy.start()
    free = free_ref[...].astype(F32)
    gid = gid_ref[...]
    factor = jnp.zeros((ROWS, COLS), F32)
    for g in range(GROUPS):
        factor = jnp.where(gid == g, design_ref[g], factor)
    base_ref[0] = free * factor
    base_ref[1] = 16.0 * free
    for copy in copies:
        copy.wait()
    sub = lax.broadcasted_iota(jnp.int32, (8, COLS), 0)
    for ref, vv, tt, x0, v0, c0 in ((up_ref, v_top, t_top, 0, 0, 0), (dn_ref, v_end, t_end, ROWS - 8, 5, 6)):
        v2 = vv.reshape(3 * MODES * 8, COLS)
        t2 = tt.reshape(81 * 8, COLS)
        for j in range(3):
            for k in range(3):
                for mg in range(MGS):
                    at = (j * 3 + k) * MODES + mg * 8
                    ref[at : at + 8, :] = v2[pl.ds((j * MODES + mg * 8) * 8 + v0 + k, 8, stride=8), :]
        for k in range(2):
            x = x0 + c0 + k
            sc = base_ref[0, x : x + 1, :]
            fr = base_ref[1, x : x + 1, :]
            at = VROWS + k * QPAD
            for qg in range(10):
                t = t2[pl.ds(qg * 64 + c0 + k, 8, stride=8), :]
                ref[at + qg * 8 : at + qg * 8 + 8, :] = diagonal(qg * 8, sub, fr) - sc * t
            t = t2[640 + c0 + k : 641 + c0 + k, :]
            ref[at + 80 : at + QPAD, :] = jnp.where(sub == 0, -sc * t, 0.0)


def prepare_kernel(v_ref, t_ref, base_ref, vt_ref, ct_ref, pack_ref):
    rid = row_of_lane()
    v2 = v_ref.reshape(3 * MODES * ROWS, COLS)
    t2 = t_ref.reshape(81 * ROWS, COLS)
    sub = lax.broadcasted_iota(jnp.int32, (8, COLS), 0)

    def modes_part(n, _):
        j = n // MGS
        mg8 = pl.multiple_of((n % MGS) * 8, 8)
        acc = [jnp.zeros((8, COLS), F32)] * 3
        for x in range(ROWS):
            v = v2[pl.ds(n * 8 * ROWS + x, 8, stride=ROWS), :]
            vt_ref[j, x, pl.ds(mg8, 8), :] = v
            for c in range(3):
                acc[c] = jnp.where(rid == x + 3, pick_lanes(v, COLS - 3 + c, 2 - c), acc[c])
        for c in range(3):
            pack_ref[pl.ds(pl.multiple_of((j * 3 + c) * MODES + mg8, 8), 8), :] = acc[c]
        return 0

    lax.fori_loop(0, 3 * MGS, modes_part, 0)

    def coefs(qg, last):
        q8 = pl.multiple_of(qg * 8, 8)
        acc = [jnp.zeros((8, COLS), F32)] * 2
        for x in range(ROWS):
            sc = base_ref[0, x : x + 1, :]
            fr = base_ref[1, x : x + 1, :]
            if last:
                v = jnp.where(sub == 0, -sc * t2[80 * ROWS + x : 80 * ROWS + x + 1, :], 0.0)
            else:
                v = diagonal(q8, sub, fr) - sc * t2[pl.ds(qg * 8 * ROWS + x, 8, stride=ROWS), :]
            ct_ref[x, pl.ds(q8, 8), :] = v
            for c in range(2):
                acc[c] = jnp.where(rid == x + 3, pick_lanes(v, COLS - 2 + c, 1 - c), acc[c])
        for c in range(2):
            pack_ref[pl.ds(pl.multiple_of(VROWS + c * QPAD + q8, 8), 8), :] = acc[c]
        return 0

    lax.fori_loop(0, 10, lambda qg, _: coefs(qg, False), 0)
    coefs(10, True)


def halo_row(ru_ref, rd_ref, b, at_up, at_down, rows):
    if b < 3:
        return ru_ref[pl.ds(pl.multiple_of(at_up, 8), rows), :]
    return rd_ref[pl.ds(pl.multiple_of(at_down, 8), rows), :]


MODE_HALO = (0, 1, 2, ROWS + 3, ROWS + 4, ROWS + 5)
COEF_HALO = (1, 2, ROWS + 3, ROWS + 4)
HALF = MSG // 2


def finish_kernel(pack_ref, ru_ref, rd_ref, right_ref, left_ref, full):
    rid = row_of_lane()

    def modes_part(n, _):
        j = n // MGS
        mg8 = (n % MGS) * 8
        ats = [pl.multiple_of((j * 3 + c) * MODES + mg8, 8) for c in range(3)]
        acc = [pack_ref[pl.ds(at, 8), :] for at in ats]
        for b in MODE_HALO:
            v = halo_row(ru_ref, rd_ref, b, (j * 3 + b) * MODES + mg8, (j * 3 + b - ROWS - 3) * MODES + mg8, 8)
            for c in range(3):
                acc[c] = jnp.where(rid == b, pick_lanes(v, COLS - 3 + c, 2 - c), acc[c])
        for c in range(3):
            full[pl.ds(ats[c], 8), :] = acc[c]
        return 0

    lax.fori_loop(0, 3 * MGS, modes_part, 0)

    def coef_part(qg, _):
        q8 = qg * 8
        ats = [pl.multiple_of(VROWS + c * QPAD + q8, 8) for c in range(2)]
        acc = [pack_ref[pl.ds(at, 8), :] for at in ats]
        for b in COEF_HALO:
            v = halo_row(ru_ref, rd_ref, b, VROWS + (b - 1) * QPAD + q8, VROWS + (b - ROWS - 3) * QPAD + q8, 8)
            for c in range(2):
                acc[c] = jnp.where(rid == b, pick_lanes(v, COLS - 2 + c, 1 - c), acc[c])
        for c in range(2):
            full[pl.ds(ats[c], 8), :] = acc[c]
        return 0

    lax.fori_loop(0, QPAD // 8, coef_part, 0)
    even = lane_of() % 2 == 0
    for n in range(HALF // 8):
        a = full[n * 8 : n * 8 + 8, :]
        b = full[HALF + n * 8 : HALF + n * 8 + 8, :]
        right_ref[n * 8 : n * 8 + 8, :] = jnp.where(even, a, pltpu.roll(b, 1, 1))
        left_ref[n * 8 : n * 8 + 8, :] = jnp.where(even, pltpu.roll(b, COLS - 1, 1), a)


OWN = 6 * MODES + QPAD
OWN_COEFS = 6 * MODES


def own_kernel(vt_ref, ct_ref, ru_ref, rd_ref, out_ref):
    rid = row_of_lane()

    def modes_part(n, _):
        j = n // MGS
        mg8 = pl.multiple_of((n % MGS) * 8, 8)
        acc = [jnp.zeros((8, COLS), F32)] * 2
        for b in range(ROWS + 6):
            if b in MODE_HALO:
                v = halo_row(ru_ref, rd_ref, b, (j * 3 + b) * MODES + mg8, (j * 3 + b - ROWS - 3) * MODES + mg8, 8)
            else:
                v = vt_ref[j, b - 3, pl.ds(mg8, 8), :]
            for c in range(2):
                acc[c] = jnp.where(rid == b, pick_lanes(v, c, COLS - 1 - c), acc[c])
        for c in range(2):
            out_ref[pl.ds(pl.multiple_of((j * 2 + c) * MODES + mg8, 8), 8), :] = acc[c]
        return 0

    lax.fori_loop(0, 3 * MGS, modes_part, 0)

    def coef_part(qg, _):
        q8 = pl.multiple_of(qg * 8, 8)
        acc = jnp.zeros((8, COLS), F32)
        for b in range(1, ROWS + 5):
            if b in COEF_HALO:
                v = halo_row(ru_ref, rd_ref, b, VROWS + (b - 1) * QPAD + q8, VROWS + (b - ROWS - 3) * QPAD + q8, 8)
            else:
                v = ct_ref[b - 3, pl.ds(q8, 8), :]
            acc = jnp.where(rid == b, pick_lanes(v, 0, COLS - 1), acc)
        out_ref[pl.ds(pl.multiple_of(OWN_COEFS + q8, 8), 8), :] = acc
        return 0

    lax.fori_loop(0, QPAD // 8, coef_part, 0)


def taps():
    for dx in range(3):
        for dy in range(3):
            for j in range(3):
                yield dx, dy, j, (dx * 3 + dy) * 9 + j


def split(value):
    high = value.astype(BF16)
    return high, (value - high.astype(F32)).astype(BF16)


def row_at(field, r, t):
    return field[r % 4].at[t + r // 4]


def put_row(field, r, t, edge_at, keep=None):
    row = row_at(field, r, t)
    lane = lane_of()
    turn = (4 * COLS - 2 * r - 8 * t) % COLS
    for j in range(3):
        for mg in range(MGS):
            v = row[1, j, group(mg), :]
            e = pltpu.roll(edge_at(j, mg), turn, 1)
            row[0, j, group(mg), :] = jnp.where(lane == 0, e, pltpu.roll(v, 1, 1))
            row[2, j, group(mg), :] = jnp.where(lane == COLS - 1, e, pltpu.roll(v, COLS - 1, 1))
    if keep is not None:
        for j in range(3):
            keep(j, row[1, j])


def main_stencil(field, coefs, r, t):
    acc = [[None] * MGS for _ in range(3)]
    rows = [row_at(field, r + d, t) for d in (-1, 0, 1)]
    for dx, dy, j, q in taps():
        vs = [rows[dx][dy, j, group(mg), :] for mg in range(MGS)]
        for i in range(3):
            c = coefs[r - 1 + 4 * t, pl.ds(q + 3 * i, 1), :]
            for mg in range(MGS):
                term = c * vs[mg]
                acc[i][mg] = term if acc[i][mg] is None else acc[i][mg] + term
    return acc


def edge_stencil(rolled, left_at, right_at, c):
    even = lane_of((1, COLS)) % 2 == 0
    acc = [[None] * MGS for _ in range(3)]
    for dx, dy, j, q in taps():
        mirror = (dx * 3 + 2 - dy) * 9 + j
        vs = [rolled[dx, j, c + dy - 1, group(mg), :] for mg in range(MGS)]
        for i in range(3):
            k = jnp.where(even, left_at(q + 3 * i), right_at(mirror + 3 * i))
            for mg in range(MGS):
                term = k * vs[mg]
                acc[i][mg] = term if acc[i][mg] is None else acc[i][mg] + term
    return acc


def roll_edges(edges, rolled, cs):
    for j in range(3):
        for c in cs:
            for mg in range(MGS):
                v = edges[j, c, group(mg), :]
                rolled[0, j, c, group(mg), :] = pltpu.roll(v, 2, 1)
                rolled[1, j, c, group(mg), :] = v
                rolled[2, j, c, group(mg), :] = pltpu.roll(v, COLS - 2, 1)


def keep_in(ref, at, x):
    lanes = pl.ds(pl.multiple_of(x * COLS, COLS), COLS)

    def keep(j, value):
        ref[j, at : at + MODES, lanes], ref[j, at + MODES : at + 2 * MODES, lanes] = split(value)

    return keep


def iterate_kernel(
    vt_ref, ct_ref, ru_ref, rd_ref, own_ref, pl_ref, pr_ref, mass_ref, x_ref, q_ref,
    a0, a1, a2, a3, b0, b1, b2, b3, coefs, edges_a, edges_b, edges_c, outer, rolled, first, masses, image_0, image_1,
):
    field_a, field_b, images = (a0, a1, a2, a3), (b0, b1, b2, b3), (image_0, image_1)
    even = lane_of() % 2 == 0
    for n in range(HALF // 8):
        a = pl_ref[n * 8 : n * 8 + 8, :]
        b = pr_ref[n * 8 : n * 8 + 8, :]
        outer[n * 8 : n * 8 + 8, :] = jnp.where(even, a, b)
        outer[HALF + n * 8 : HALF + n * 8 + 8, :] = jnp.where(even, pltpu.roll(a, COLS - 1, 1), pltpu.roll(b, 1, 1))
    for k in range(2):
        coefs[k] = ru_ref[VROWS + k * QPAD : VROWS + (k + 1) * QPAD, :]
        coefs[ROWS + 2 + k] = rd_ref[VROWS + k * QPAD : VROWS + (k + 1) * QPAD, :]
    for j in range(3):
        for k in range(3):
            at = (j * 3 + k) * MODES
            row_at(field_a, k, 0)[1, j] = ru_ref[at : at + MODES, :]
            row_at(field_a, ROWS + 3 + k, 0)[1, j] = rd_ref[at : at + MODES, :]
            edges_a[j, k] = outer[at : at + MODES, :]
        for k in range(2):
            at = (j * 2 + k) * MODES
            edges_a[j, 3 + k] = own_ref[at : at + MODES, :]

    def copy_rows(t, _):
        for k in range(4):
            coefs[4 * t + k + 2] = ct_ref[4 * t + k]
            for j in range(3):
                row_at(field_a, k + 3, t)[1, j] = vt_ref[j, 4 * t + k]
        return 0

    lax.fori_loop(0, ROWS // 4, copy_rows, 0)

    def outer_coefs(c):
        if c == 3:
            at, ref = OWN_COEFS, own_ref
        else:
            at, ref = VROWS + (c - 1) * QPAD, outer
        return lambda q: ref[at + q : at + q + 1, :]

    roll_edges(edges_a, rolled, range(5))
    for c in (1, 2, 3):
        acc = edge_stencil(rolled, outer_coefs(c), outer_coefs(c), c)
        for i in range(3):
            for mg in range(MGS):
                edges_b[i, c, group(mg), :] = acc[i][mg]
    roll_edges(edges_b, rolled, (1, 2, 3))
    acc = edge_stencil(rolled, outer_coefs(2), outer_coefs(2), 2)
    for i in range(3):
        for mg in range(MGS):
            edges_c[i, group(mg), :] = acc[i][mg]

    def edge_a(j, mg):
        return edges_a[j, 2, group(mg), :]

    def edge_b(j, mg):
        return edges_b[j, 2, group(mg), :]

    def edge_c(j, mg):
        return edges_c[j, group(mg), :]

    def store(row, acc):
        for i in range(3):
            for mg in range(MGS):
                row[1, i, group(mg), :] = acc[i][mg]

    for b in range(3):
        put_row(field_a, b, 0, edge_a)

    def first_rows(t, _):
        for r in range(1, 5):
            put_row(field_a, r + 2, t, edge_a)
            store(row_at(field_b, r, t), main_stencil(field_a, coefs, r, t))
        return 0

    lax.fori_loop(0, ROWS // 4 + 1, first_rows, 0)
    for b in range(1, 4):
        put_row(field_b, b, 0, edge_b, keep_in(first, 0, max(b - 3, 0)))

    def second_rows(t, _):
        for r in range(2, 6):
            put_row(field_b, r + 2, t, edge_b, keep_in(first, 0, 4 * t + r - 1))
            store(row_at(field_a, r, t), main_stencil(field_b, coefs, r, t))
        return 0

    lax.fori_loop(0, ROWS // 4 + 1, second_rows, 0)
    for b in range(2, 5):
        put_row(field_a, b, 0, edge_c, keep_in(x_ref, 0, max(b - 3, 0)))

    sub = lax.broadcasted_iota(jnp.int32, (16, COLS), 0)

    def keep_image(r, t, x):
        for i in range(3):
            keep_in(x_ref, 2 * MODES, x)(i, 16.0 * row_at(field_a, r, t)[1, i] - images[r % 2][i])

    def third_rows(t, _):
        for r in range(3, 7):
            put_row(field_a, r + 2, t, edge_c, keep_in(x_ref, 0, 4 * t + r - 1))
            keep_image(r - 1, t, jnp.maximum(4 * t + r - 4, 0))
            x = 4 * t + r - 3
            w = jnp.zeros((16, COLS), F32)
            for n in range(3):
                w = jnp.where(sub == n, mass_ref[n, pl.ds(x, 1), :], w)
            lanes = pl.ds(pl.multiple_of(x * COLS, COLS), COLS)
            masses[0:16, lanes], masses[16:32, lanes] = split(w)
            acc = main_stencil(field_a, coefs, r, t)
            for i in range(3):
                for mg in range(MGS):
                    images[r % 2][i, group(mg), :] = acc[i][mg]
        return 0

    lax.fori_loop(0, ROWS // 4, third_rows, 0)
    keep_image(ROWS + 2, 0, ROWS - 1)

    def contract(a, b):
        return lax.dot_general(a, b, (((1,), (1,)), ((), ())), preferred_element_type=F32)

    g1 = jnp.zeros((2 * MODES, 2 * MODES), F32)
    g2 = jnp.zeros((2 * MODES, 4 * MODES), F32)
    sums = []
    for j in range(3):
        u = x_ref[j, 0 : 2 * MODES, : ROWS * COLS]
        f = first[j, :, : ROWS * COLS]
        g1 = g1 + contract(f, f)
        g2 = g2 + contract(u, x_ref[j, :, : ROWS * COLS])
        p = contract(u, masses[...])
        p = p[:MODES] + p[MODES:]
        sums.append(p[:, 0:3] + p[:, 16:19])
    g1 = g1[:MODES] + g1[MODES:]
    g2 = g2[:MODES] + g2[MODES:]
    q_ref[...] = jnp.zeros((MODES, COLS), F32)
    q_ref[:, 0:32] = g1[:, 0:32] + g1[:, 32:64]
    q_ref[:, 32:64] = g2[:, 0:32] + g2[:, 32:64]
    q_ref[:, 64:96] = g2[:, 64:96] + g2[:, 96:128]
    for j in range(3):
        q_ref[:, 96 + 3 * j : 99 + 3 * j] = sums[j]


def inverse_factor(gram):
    shape = (MODES, 2 * MODES)
    lane = lax.broadcasted_iota(jnp.int32, shape, 1)
    sub = lax.broadcasted_iota(jnp.int32, shape, 0)
    eye = jnp.where(lax.broadcasted_iota(jnp.int32, (MODES, MODES), 0) == lax.broadcasted_iota(jnp.int32, (MODES, MODES), 1), 1.0, 0.0)
    a = jnp.concatenate([gram, eye], axis=1)
    for k in range(MODES):
        f = jnp.where(sub > k, a[:, k : k + 1] / a[k : k + 1, k : k + 1], 0.0)
        a = a - f * a[k : k + 1, :]
    pivots = jnp.sum(jnp.where(lane == sub, a, 0.0), axis=1, keepdims=True)
    return a[:, MODES:] / jnp.sqrt(pivots)


def product(a, b, transposed=False):
    dims = (((1,), (1 if transposed else 0,)), ((), ()))
    return lax.dot_general(a, b, dims, precision=lax.Precision.HIGHEST, preferred_element_type=F32)


def combine_kernel(nodes, q_ref, x_ref, gid_ref, design_ref, modes_ref, send_ref, reduced_ref, part_ref, weight, bins):
    q = q_ref[...]
    w1 = inverse_factor(q[:, 0:32])
    gram = nodes * product(product(w1, q[:, 32:64]), w1, True)
    w = nodes * product(inverse_factor(gram), w1)
    reduced_ref[...] = product(product(w, q[:, 64:96]), w, True) / nodes
    s = lax.dot_general(
        q[:, 96:112], w, (((0,), (1,)), ((), ())), precision=lax.Precision.HIGHEST, preferred_element_type=F32
    ) / (nodes**0.5)
    for k, row in enumerate((s[0:1], s[3:4], s[6:7], s[8:9], -s[7:8], s[4:5] - s[2:3])):
        part_ref[k : k + 1, :] = row
    high = w.astype(BF16)
    low = (w - high.astype(F32)).astype(BF16)
    mix = jnp.concatenate([jnp.concatenate([high, high], axis=1), jnp.concatenate([low, low], axis=1)], axis=0)
    m2 = modes_ref.reshape(3 * MODES * ROWS, COLS)
    s2 = send_ref.reshape(MODES * PIECE, COLS)
    step = 4

    def chunk(n, _):
        lanes = pl.ds(pl.multiple_of(n * step * COLS, step * COLS), step * COLS)
        total = jnp.zeros((8, step * COLS), F32)
        for j in range(3):
            v = jnp.dot(mix, x_ref[j, 0 : 2 * MODES, lanes], preferred_element_type=F32)
            z = jnp.dot(mix, x_ref[j, 2 * MODES : 4 * MODES, lanes], preferred_element_type=F32)
            v = v[:MODES] + v[MODES:]
            z = z[:MODES] + z[MODES:]
            vz = v * z
            for mg in range(MGS):
                total = total + vz[group(mg)]
                for k in range(step):
                    piece = v[group(mg), k * COLS : (k + 1) * COLS]
                    x = n * step + k
                    m2[pl.ds((j * MODES + mg * 8) * ROWS + x, 8, stride=ROWS), :] = piece
                    s2[pl.ds(mg * 8 * PIECE + j * ROWS + x, 8, stride=PIECE), :] = piece
        total = jnp.sum(total, axis=0, keepdims=True)
        for k in range(step):
            weight[pl.ds(n * step + k, 1), :] = total[:, k * COLS : (k + 1) * COLS]
        return 0

    lax.fori_loop(0, ROWS // step, chunk, 0)
    gid = gid_ref[...]
    wgt = weight[...]
    for g in range(GROUPS):
        scale = 1.0 / (design_ref[g] * nodes)
        bins[g : g + 1, :] = jnp.sum(jnp.where(gid == g, wgt, 0.0), axis=0, keepdims=True) * scale
    adjoint = product(jnp.ones((8, COLS), F32), bins[...], True)
    adjoint = jnp.concatenate([adjoint, jnp.zeros((8, COLS - GROUPS), F32)], axis=1)

    def put(k, _):
        send_ref[k, 3 * ROWS : PIECE, :] = adjoint
        return 0

    lax.fori_loop(0, MODES, put, 0)


def spread_kernel(columns, recv_ref, out_ref):
    for n in range(columns):
        for i in range(3):
            out_ref[i, :, n * COLS : (n + 1) * COLS] = recv_ref[n, i * ROWS : (i + 1) * ROWS, :]


def call(kernel, outs, scratch, cost, *args, smem=(), hbm=()):
    flops, size = cost
    return pl.pallas_call(
        kernel,
        out_shape=[jax.ShapeDtypeStruct(s, d) for s, d in outs],
        in_specs=[
            pl.BlockSpec(memory_space=pltpu.SMEM if k in smem else pl.ANY if k in hbm else pltpu.VMEM)
            for k in range(len(args))
        ],
        out_specs=[pl.BlockSpec(memory_space=pltpu.VMEM) for _ in outs],
        scratch_shapes=[pltpu.VMEM(*s) if isinstance(s, tuple) else s for s in scratch],
        compiler_params=pltpu.CompilerParams(vmem_limit_bytes=VMEM),
        cost_estimate=pl.CostEstimate(flops=flops, bytes_accessed=size, transcendentals=0),
    )(*args)


def swap(x, axis, k):
    n = lax.axis_size(axis)
    return lax.ppermute(x, axis, [(i, i ^ k) for i in range(n)])


def sum_group(x, axis, generators):
    combos = [0]
    for k in generators:
        combos = combos + [c ^ k for c in combos]
    level = [x if c == 0 else swap(x, axis, c) for c in combos]
    while len(level) > 1:
        level = [level[2 * i] + level[2 * i + 1] for i in range(len(level) // 2)]
    return level[0]


def sum_devices(x):
    x = sum_group(x, "region", (1,))
    x = sum_group(x, "region", (2,))
    columns = lax.axis_size("node")
    copies = jnp.broadcast_to(x[None], (columns,) + x.shape)
    return jnp.sum(lax.all_to_all(copies, "node", 0, 0, tiled=True), axis=0)


def shift(x, axis, step):
    n = lax.axis_size(axis)
    return lax.ppermute(x, axis, [(i, i + step) for i in range(n) if 0 <= i + step < n])


def per_device(start_modes, stiffness_tiles, free_mask, group_ids, design, node_mass):
    regions = lax.axis_size("region")
    columns = lax.axis_size("node")
    total_x = ROWS * regions
    total_y = COLS * columns
    nodes = float(total_x * total_y)
    region = lax.axis_index("region")
    column = lax.axis_index("node")

    tiles = stiffness_tiles.reshape(81, ROWS, COLS)
    message = ((MSG, COLS), F32)
    half = ((HALF, COLS), F32)
    base, up, dn = call(
        rows_kernel,
        [((2, ROWS, COLS), F32), message, message],
        [
            ((3, MODES, 8, COLS), F32), ((3, MODES, 8, COLS), F32), ((81, 8, COLS), F32), ((81, 8, COLS), F32),
            pltpu.SemaphoreType.DMA((4,)),
        ],
        (1000000, 2000000),
        start_modes, tiles, free_mask, group_ids, design, smem=(4,), hbm=(0, 1),
    )
    ru = shift(dn, "region", 1)
    rd = shift(up, "region", -1)
    vt, ct, packed = call(
        prepare_kernel,
        [((3, ROWS, MODES, COLS), F32), ((ROWS, QPAD, COLS), F32), message],
        [],
        (10000000, 6000000),
        start_modes, tiles, base,
    )
    to_right, to_left = call(finish_kernel, [half, half], [message], (1000000, 1500000), packed, ru, rd)
    left = shift(to_right, "node", 1)
    right = shift(to_left, "node", -1)
    (own,) = call(own_kernel, [((OWN, COLS), F32)], [], (10000000, 4000000), vt, ct, ru, rd)

    mass = lax.dynamic_slice(node_mass, (0, column * COLS), (ROWS, COLS))
    xs = (region * ROWS + jnp.arange(ROWS, dtype=jnp.int32)).astype(F32)
    ys = (column * COLS + jnp.arange(COLS, dtype=jnp.int32)).astype(F32)
    pos_x = 2.0 * (xs + 0.5) / total_x - 1.0
    pos_y = 2.0 * (ys + 0.5) / total_y - 1.0
    weights = jnp.stack([mass, mass * pos_x[:, None], mass * pos_y[None, :]])

    rows = ((ROWS // 4 + 2, 3, 3, MODES, COLS), F32)
    edge = (3, 5, MODES, COLS)
    wide = (ROWS + 8) * COLS
    x, q = call(
        iterate_kernel,
        [((3, 4 * MODES, wide), BF16), ((MODES, COLS), F32)],
        [rows] * 8 + [
            ((ROWS + 8, QPAD, COLS), F32), (edge, F32), (edge, F32), ((3, MODES, COLS), F32), message,
            ((3,) + edge, F32), ((3, 2 * MODES, wide), BF16), ((32, ROWS * COLS), BF16),
            ((3, MODES, COLS), F32), ((3, MODES, COLS), F32),
        ],
        (100000000, 20000000),
        vt, ct, ru, rd, own, left, right, weights,
    )
    q = sum_devices(q)
    modes, send, reduced, part = call(
        lambda *refs: combine_kernel(nodes, *refs),
        [((3, MODES, ROWS, COLS), F32), ((MODES, PIECE, COLS), F32), ((MODES, MODES), F32), ((6, MODES), F32)],
        [((ROWS, COLS), F32), ((GROUPS, COLS), F32)],
        (10000000, 10000000),
        q, x, group_ids, design, smem=(3,),
    )
    participation = lax.dynamic_slice(part, (0, column), (6, 1))
    recv = lax.all_to_all(send, "node", 0, 0, tiled=True)
    extra = jnp.sum(recv[:, 3 * ROWS :, :], axis=0)
    (by_column,) = call(
        lambda *refs: spread_kernel(columns, *refs), [((3, ROWS, total_y), F32)], [], (10000, 6000000), recv
    )
    extra = sum_group(sum_group(extra, "region", (1,)), "region", (2,))
    adjoint = extra[0, :GROUPS]
    return (modes, by_column[:, None], reduced, participation, adjoint)


def solution(mesh):
    placed = (
        P(None, None, "region", "node"),
        P(None, None, None, "region", "node"),
        P("region", "node"),
        P("region", "node"),
        P(),
        P("region", None),
    )
    return jax.shard_map(
        per_device,
        mesh=mesh,
        in_specs=placed,
        out_specs=(
            P(None, None, "region", "node"),
            P(None, "node", "region", None),
            P(),
            P(None, "node"),
            P(),
        ),
        check_vma=False,
    )
```

time: 150 us -> 126 us (0.84)
  blocking collectives: 0 us -> 44.9 us
  waiting for transfers between devices: 36.3 us -> 3.14 us
  starting transfers between devices: 48.6 us -> 23.5 us
  Pallas kernels: 50.7 us -> 45.1 us
  between operations: 2.77 us -> 0.78 us
    all_to_all x0 -> x2, blocking collectives: none -> 44.9 us  [the longest x1 25.6 us: per_device(): recv = lax.all_to_all(send, 'node', 0, 0, tiled=True)]
    ppermute x13 -> x4, starting transfers between devices: 28.2 us -> 10.7 us  [swap(): return lax.ppermute(x, axis, [(i, i ^ k) for i in range(n)])]
    all_to_all x1 -> x0, waiting for transfers between devices: 17.5 us -> none  [per_device(): recv = lax.all_to_all(send, 'node', 0, 0, tiled=True)]
    ppermute x4, waiting for transfers between devices: 9.18 us -> 0.01 us  [shift(): lax.ppermute(x, axis, [(i, i + step) for i in range(n) if 0 <= i + step <...]
    all_to_all x1 -> x0, starting transfers between devices: 6.99 us -> none  [per_device(): recv = lax.all_to_all(send, 'node', 0, 0, tiled=True)]
    ppermute x13 -> x4, waiting for transfers between devices: 9.61 us -> 3.13 us  [swap(): return lax.ppermute(x, axis, [(i, i ^ k) for i in range(n)])]
    pallas_call x5 -> x7, Pallas kernels: 50.7 us -> 45.1 us  [call(): pl.pallas_call(kernel, out_shape=[jax.ShapeDtypeStruct(s, d) for s, d in...]
    another operation x1 -> x0, local copies, waits for them, and re-layouts: 2.96 us -> none  [per_device(): jnp.stack([s[0], s[3], s[6], s[8], -s[7], s[4] - s[2]])[:, None]]
  transfers between devices with their start and end apart: 18 -> 8, of which waited for: 12 -> 3; matrix products, arithmetic and copies ran while one was open for 4% -> 1% of each run, Pallas kernels for 0% -> 10%
where the time goes in v3:
time: 126 us
  Pallas kernels  45.1 us (36%)
  blocking collectives  44.9 us (36%)
  starting transfers between devices  23.5 us (19%)
  local copies, waits for them, and re-layouts  7.47 us (6%)
  waiting for transfers between devices  3.14 us (2%)
    pallas_call x7, Pallas kernels, call(): pl.pallas_call(kernel, out_shape=[jax.ShapeDtypeStruct(s, d) for s, d in...  45.1 us
    all_to_all x1, blocking collectives, per_device(): recv = lax.all_to_all(send, 'node', 0, 0, tiled=True)  25.6 us
    all_to_all x1, blocking collectives, sum_devices(): return jnp.sum(lax.all_to_all(copies, 'node', 0, 0, tiled=True), axis=0)  19.3 us
    ppermute x4, starting transfers between devices, shift(): lax.ppermute(x, axis, [(i, i + step) for i in range(n) if 0 <= i + step <...  12.8 us
    ppermute x4, starting transfers between devices, swap(): return lax.ppermute(x, axis, [(i, i ^ k) for i in range(n)])  10.7 us
    unnamed x19, local copies, waits for them, and re-layouts  6.83 us
    ppermute x4, waiting for transfers between devices, swap(): return lax.ppermute(x, axis, [(i, i ^ k) for i in range(n)])  3.13 us
  transfers between devices with their start and end apart: 8, of which 3 were waited for; matrix products, arithmetic and copies ran while one was open for 1% of the time, Pallas kernels for 10%

profile of v3, /device:TPU:1, one launch (start us, length us, event | category | flops | bytes accessed | tf_op | source)
XLA Modules:
  0.0 125.7 jit_solution(13474599216317374305)
XLA Ops:
  0.6 0.0 copy-start
  0.6 1.4 %copy-done = f32[3,32,32,128]{3,2,1,0:T(8,128)S(1)} copy-done((f32[3,32,32,128]{3,2,1,0:T(8,128)S(1)}, f32[3,32,32,128]{3,2,1,0:T(8,128)}, u32[]{:S(2)}) %copy-start) | copy-done | bytes 1572888
  2.0 1.3 %copy-done.2 = f32[9,3,3,32,128]{4,3,2,1,0:T(8,128)S(1)} copy-done((f32[9,3,3,32,128]{4,3,2,1,0:T(8,128)S(1)}, f32[9,3,3,32,128]{4,3,2,1,0:T(8,128)}, u32[]{:S(2)}) %copy-start.2) | copy-done | bytes 1327128
  3.4 0.7 copy-done.4
  4.1 0.7 copy-done.6
  4.8 0.7 copy-done.7
  5.5 1.0 shard_map.101
  6.4 6.0 %collective-permute-start = (f32[464,128]{1,0:T(8,128)S(1)}, f32[464,128]{1,0:T(8,128)S(1)}, u32[]{:S(2)}, u32[]{:S(2)}) collective-permute-start(f32[464,128]{1,0:T(8,128)S(1)} %get-tuple-element.22), channel_id=1, source_target_pairs={{0,32},{32,64},{64,96},{1,33},{33,65},{65,97},{2,34},{34,66},{66,9... | collective-permute-start | bytes 712712 | tf_op jit(solution)/shard_map/ppermute | solution.py:551
  12.5 1.9 %collective-permute-start.1 = (f32[464,128]{1,0:T(8,128)S(1)}, f32[464,128]{1,0:T(8,128)S(1)}, u32[]{:S(2)}, u32[]{:S(2)}) collective-permute-start(f32[464,128]{1,0:T(8,128)S(1)} %get-tuple-element.23), channel_id=1, source_target_pairs={{32,0},{64,32},{96,64},{33,1},{65,33},{97,65},{34,2},{66,34},{98,6... | collective-permute-start | bytes 712712 | tf_op jit(solution)/shard_map/ppermute | solution.py:551
  14.4 8.1 %shard_map.102 = (f32[3,32,32,128]{3,2,1,0:T(8,128)}, f32[32,88,128]{2,1,0:T(8,128)S(1)}, f32[464,128]{1,0:T(8,128)S(1)}) custom-call(f32[3,32,32,128]{3,2,1,0:T(8,128)} %v_ref.1, f32[81,32,128]{2,1,0:T(8,128)S(1)} %bitcast.13, f32[2,32,128]{2,1,0:T(8,128)S(1)} %get-tuple-element.19.base_ref), custom_call_target="tpu_custom_call" | custom-call | flops 10000000 | bytes 6000000 | tf_op jit(solution)/shard_map/pallas_call | solution.py:512
  22.6 0.0 collective-permute-done.1.rd_ref
  22.6 2.4 %shard_map.104 = (f32[232,128]{1,0:T(8,128)S(1)}, f32[232,128]{1,0:T(8,128)S(1)}) custom-call(f32[464,128]{1,0:T(8,128)S(1)} %get-tuple-element.24.pack_ref, f32[464,128]{1,0:T(8,128)S(1)} %collective-permute-done.ru_ref, f32[464,128]{1,0:T(8,128)S(1)} %collective-permute-done.1.rd_ref), custom_call_target="tpu_custom_call" | custom-call | flops 1000000 | bytes 1500000 | tf_op jit(solution)/shard_map/pallas_call | solution.py:512
  25.0 3.5 %collective-permute-start.2 = (f32[232,128]{1,0:T(8,128)S(1)}, f32[232,128]{1,0:T(8,128)S(1)}, u32[]{:S(2)}, u32[]{:S(2)}) collective-permute-start(f32[232,128]{1,0:T(8,128)S(1)} %get-tuple-element.25), channel_id=1, source_target_pairs={{0,1},{1,2},{2,3},{3,4},{4,5},{5,6},{6,7},{7,8},{8,9},{9,10},{10,1... | collective-permute-start | bytes 356360 | tf_op jit(solution)/shard_map/ppermute | solution.py:551
  28.6 1.3 %collective-permute-start.3 = (f32[232,128]{1,0:T(8,128)S(1)}, f32[232,128]{1,0:T(8,128)S(1)}, u32[]{:S(2)}, u32[]{:S(2)}) collective-permute-start(f32[232,128]{1,0:T(8,128)S(1)} %get-tuple-element.26), channel_id=1, source_target_pairs={{1,0},{2,1},{3,2},{4,3},{5,4},{6,5},{7,6},{8,7},{9,8},{10,9},{11,1... | collective-permute-start | bytes 356360 | tf_op jit(solution)/shard_map/ppermute | solution.py:551
  29.9 0.8 dynamic-slice_bitcast_fusion
  30.7 1.4 %copy-done.1 = f32[3,32,32,128]{3,2,1,0:T(8,128)S(1)} copy-done((f32[3,32,32,128]{3,2,1,0:T(8,128)S(1)}, f32[3,32,32,128]{3,2,1,0:T(8,128)}, u32[]{:S(2)}) %copy-start.1) | copy-done | bytes 1572888
  32.1 3.0 %shard_map.103.own_ref = f32[280,128]{1,0:T(8,128)S(1)} custom-call(f32[3,32,32,128]{3,2,1,0:T(8,128)S(1)} %copy-done.1, f32[32,88,128]{2,1,0:T(8,128)S(1)} %get-tuple-element.21.ct_ref, f32[464,128]{1,0:T(8,128)S(1)} %collective-permute-done.ru_ref, f32[464,128]{1,0:T(8,128)S(1)} %collective-permute-done.1.rd_ref), custom_call_target="tpu_custom_call" | custom-call | flops 10000000 | bytes 4000000 | tf_op jit(solution)/shard_map/pallas_call | solution.py:512
  35.1 16.6 %shard_map.105 = (bf16[3,128,5120]{2,1,0:T(8,128)(2,1)}, f32[32,128]{1,0:T(8,128)S(1)}) custom-call(f32[3,32,32,128]{3,2,1,0:T(8,128)S(1)} %copy-done.1, f32[32,88,128]{2,1,0:T(8,128)S(1)} %get-tuple-element.21.ct_ref, f32[464,128]{1,0:T(8,128)S(1)} %collective-permute-done.ru_ref, f32[464,128]{1,0:T(8,128)S(1)} %collective-permute-done.1.rd_ref, ...), custom_call_target="tpu_custom_call" | custom-call | flops 100000000 | bytes 20000000 | tf_op jit(solution)/shard_map/pallas_call | solution.py:512
  51.8 1.2 collective-permute-done.4
  53.0 3.4 %collective-permute-start.5 = (f32[32,128]{1,0:T(8,128)S(1)}, f32[32,128]{1,0:T(8,128)S(1)}, u32[]{:S(2)}, u32[]{:S(2)}) collective-permute-start(f32[32,128]{1,0:T(8,128)S(1)} %add.77), channel_id=1, source_target_pairs={{0,64},{32,96},{64,0},{96,32},{1,65},{33,97},{65,1},{97,33},{2,66}... | collective-permute-start | bytes 49160 | tf_op jit(solution)/shard_map/ppermute | solution.py:528
  56.4 1.1 collective-permute-done.5
  57.5 0.1 broadcast_in_dim.4
  57.6 19.3 %all_to_all.10 = f32[32,32,128]{2,1,0:T(8,128)S(1)} all-to-all(f32[32,32,128]{2,1,0:T(8,128)S(1)} %broadcast_in_dim.4), channel_id=1, replica_groups=mesh['region'=4,'node'=32] {'node'}, dimensions={0} | all-to-all | bytes 1048576 | tf_op jit(solution)/shard_map/all_to_all | solution.py:546
  77.0 12.6 %shard_map.106 = (f32[3,32,32,128]{3,2,1,0:T(8,128)}, f32[32,104,128]{2,1,0:T(8,128)S(1)}, f32[32,32]{1,0:T(8,128)}, f32[6,32]{1,0:T(8,128)S(1)}) custom-call(f32[32,128]{1,0:T(8,128)S(1)} %reduce_sum.18.refs_0_, bf16[3,128,5120]{2,1,0:T(8,128)(2,1)} %get-tuple-element.28.refs_1_, s32[32,128]{1,0:T(8,128)S(1)} %copy-done.5, f32[64]{0:T(128)S(1)} %copy-done.8), custom_call_target="tpu_custom_call" | custom-call | flops 10000000 | bytes 10000000 | tf_op jit(solution)/shard_map/pallas_call | solution.py:512
  89.6 25.6 %all_to_all.11.refs_0_ = f32[32,104,128]{2,1,0:T(8,128)S(1)} all-to-all(f32[32,104,128]{2,1,0:T(8,128)S(1)} %get-tuple-element.30), channel_id=1, replica_groups=mesh['region'=4,'node'=32] {'node'}, dimensions={0} | all-to-all | bytes 3407872 | tf_op jit(solution)/shard_map/all_to_all | solution.py:620
  115.2 4.3 %collective-permute-start.6 = (f32[8,128]{1,0:T(8,128)S(1)}, f32[8,128]{1,0:T(8,128)S(1)}, u32[]{:S(2)}, u32[]{:S(2)}) collective-permute-start(f32[8,128]{1,0:T(8,128)S(1)} %slice_reduce_fusion), channel_id=1, source_target_pairs={{0,32},{32,0},{64,96},{96,64},{1,33},{33,1},{65,97},{97,65},{2,34}... | collective-permute-start | bytes 12296 | tf_op jit(solution)/shard_map/ppermute | solution.py:528
  119.4 0.8 collective-permute-done.6
  120.3 3.0 %collective-permute-start.7 = (f32[8,128]{1,0:T(8,128)S(1)}, f32[8,128]{1,0:T(8,128)S(1)}, u32[]{:S(2)}, u32[]{:S(2)}) collective-permute-start(f32[8,128]{1,0:T(8,128)S(1)} %add.80), channel_id=1, source_target_pairs={{0,64},{32,96},{64,0},{96,32},{1,65},{33,97},{65,1},{97,33},{2,66}... | collective-permute-start | bytes 12296 | tf_op jit(solution)/shard_map/ppermute | solution.py:528
  123.2 0.1 constant_dynamic-slice_fusion
  123.3 0.6 copy.14
  123.9 1.3 %shard_map.107 = f32[3,32,4096]{2,1,0:T(8,128)} custom-call(f32[32,104,128]{2,1,0:T(8,128)S(1)} %all_to_all.11.refs_0_), custom_call_target="tpu_custom_call" | custom-call | flops 10000 | bytes 6000000 | tf_op jit(solution)/shard_map/pallas_call | solution.py:512
  125.2 0.5 slice_bitcast_fusion
  (25 shorter events, 0.1 us)
Async XLA Ops:
  0.6 1.4 %copy-start = (f32[3,32,32,128]{3,2,1,0:T(8,128)S(1)}, f32[3,32,32,128]{3,2,1,0:T(8,128)}, u32[]{:S(2)}) copy-start(f32[3,32,32,128]{3,2,1,0:T(8,128)} %v_ref.1) | copy-start | bytes 4718596
  2.0 1.3 %copy-start.2 = (f32[9,3,3,32,128]{4,3,2,1,0:T(8,128)S(1)}, f32[9,3,3,32,128]{4,3,2,1,0:T(8,128)}, u32[]{:S(2)}) copy-start(f32[9,3,3,32,128]{4,3,2,1,0:T(8,128)} %param.7) | copy-start | bytes 3981316
  3.4 0.7 copy-start.4
  4.1 0.7 copy-start.6
  4.8 0.7 copy-start.7
  5.5 9.0 %copy-start.3 = (f32[9,3,3,32,128]{4,3,2,1,0:T(8,128)S(1)}, f32[9,3,3,32,128]{4,3,2,1,0:T(8,128)}, u32[]{:S(2)}) copy-start(f32[9,3,3,32,128]{4,3,2,1,0:T(8,128)} %param.7) | copy-start | bytes 3981316
  6.4 16.1 %collective-permute-start = (f32[464,128]{1,0:T(8,128)S(1)}, f32[464,128]{1,0:T(8,128)S(1)}, u32[]{:S(2)}, u32[]{:S(2)}) collective-permute-start(f32[464,128]{1,0:T(8,128)S(1)} %get-tuple-element.22), channel_id=1, source_target_pairs={{0,32},{32,64},{64,96},{1,33},{33,65},{65,97},{2,34},{34,66},{66,9... | collective-permute-start | bytes 712712 | tf_op jit(solution)/shard_map/ppermute | solution.py:551
  12.5 10.1 %collective-permute-start.1 = (f32[464,128]{1,0:T(8,128)S(1)}, f32[464,128]{1,0:T(8,128)S(1)}, u32[]{:S(2)}, u32[]{:S(2)}) collective-permute-start(f32[464,128]{1,0:T(8,128)S(1)} %get-tuple-element.23), channel_id=1, source_target_pairs={{32,0},{64,32},{96,64},{33,1},{65,33},{97,65},{34,2},{66,34},{98,6... | collective-permute-start | bytes 712712 | tf_op jit(solution)/shard_map/ppermute | solution.py:551
  25.0 10.1 %collective-permute-start.2 = (f32[232,128]{1,0:T(8,128)S(1)}, f32[232,128]{1,0:T(8,128)S(1)}, u32[]{:S(2)}, u32[]{:S(2)}) collective-permute-start(f32[232,128]{1,0:T(8,128)S(1)} %get-tuple-element.25), channel_id=1, source_target_pairs={{0,1},{1,2},{2,3},{3,4},{4,5},{5,6},{6,7},{7,8},{8,9},{9,10},{10,1... | collective-permute-start | bytes 356360 | tf_op jit(solution)/shard_map/ppermute | solution.py:551
  28.6 6.6 %collective-permute-start.3 = (f32[232,128]{1,0:T(8,128)S(1)}, f32[232,128]{1,0:T(8,128)S(1)}, u32[]{:S(2)}, u32[]{:S(2)}) collective-permute-start(f32[232,128]{1,0:T(8,128)S(1)} %get-tuple-element.26), channel_id=1, source_target_pairs={{1,0},{2,1},{3,2},{4,3},{5,4},{6,5},{7,6},{8,7},{9,8},{10,9},{11,1... | collective-permute-start | bytes 356360 | tf_op jit(solution)/shard_map/ppermute | solution.py:551
  30.7 1.4 %copy-start.1 = (f32[3,32,32,128]{3,2,1,0:T(8,128)S(1)}, f32[3,32,32,128]{3,2,1,0:T(8,128)}, u32[]{:S(2)}) copy-start(f32[3,32,32,128]{3,2,1,0:T(8,128)} %get-tuple-element.20.vt_ref) | copy-start | bytes 4718596
  51.8 25.2 %copy-start.5 = (s32[32,128]{1,0:T(8,128)S(1)}, s32[32,128]{1,0:T(8,128)}, u32[]{:S(2)}) copy-start(s32[32,128]{1,0:T(8,128)} %refs_2_.1) | copy-start | bytes 49156
  51.8 25.2 %copy-start.8 = (f32[64]{0:T(128)S(1)}, f32[64]{0:T(128)}, u32[]{:S(2)}) copy-start(f32[64]{0:T(128)} %refs_3_.1) | copy-start | bytes 772
  51.8 1.2 collective-permute-start.4
  53.0 4.6 %collective-permute-start.5 = (f32[32,128]{1,0:T(8,128)S(1)}, f32[32,128]{1,0:T(8,128)S(1)}, u32[]{:S(2)}, u32[]{:S(2)}) collective-permute-start(f32[32,128]{1,0:T(8,128)S(1)} %add.77), channel_id=1, source_target_pairs={{0,64},{32,96},{64,0},{96,32},{1,65},{33,97},{65,1},{97,33},{2,66}... | collective-permute-start | bytes 49160 | tf_op jit(solution)/shard_map/ppermute | solution.py:528
  115.2 5.1 %collective-permute-start.6 = (f32[8,128]{1,0:T(8,128)S(1)}, f32[8,128]{1,0:T(8,128)S(1)}, u32[]{:S(2)}, u32[]{:S(2)}) collective-permute-start(f32[8,128]{1,0:T(8,128)S(1)} %slice_reduce_fusion), channel_id=1, source_target_pairs={{0,32},{32,0},{64,96},{96,64},{1,33},{33,1},{65,97},{97,65},{2,34}... | collective-permute-start | bytes 12296 | tf_op jit(solution)/shard_map/ppermute | solution.py:528
  120.3 4.9 %collective-permute-start.7 = (f32[8,128]{1,0:T(8,128)S(1)}, f32[8,128]{1,0:T(8,128)S(1)}, u32[]{:S(2)}, u32[]{:S(2)}) collective-permute-start(f32[8,128]{1,0:T(8,128)S(1)} %add.80), channel_id=1, source_target_pairs={{0,64},{32,96},{64,0},{96,32},{1,65},{33,97},{65,1},{97,33},{2,66}... | collective-permute-start | bytes 12296 | tf_op jit(solution)/shard_map/ppermute | solution.py:528

commit v4 on v3

--- a/solution.py
+++ b/solution.py
@@ -12,7 +12,6 @@
 VROWS = 9 * MODES
 MSG = VROWS + 2 * QPAD
 MGS = MODES // 8
-VMEM = 100 * 1024 * 1024 // 2
 EXTRA = 8
 PIECE = 3 * ROWS + EXTRA
 
@@ -41,17 +40,24 @@
 
 
 def rows_kernel(
-    v_hbm, t_hbm, free_ref, gid_ref, design_ref, base_ref, up_ref, dn_ref, v_top, v_end, t_top, t_end, sems
+    v_hbm, t_hbm, free_hbm, gid_hbm, design_hbm, base_ref, up_ref, dn_ref,
+    v_top, v_end, t_top, t_end, free_ref, gid_ref, design_ref, sems,
 ):
     top, end = pl.ds(0, 8), pl.ds(ROWS - 8, 8)
-    copies = [
-        pltpu.make_async_copy(v_hbm.at[:, :, top, :], v_top, sems.at[0]),
-        pltpu.make_async_copy(t_hbm.at[:, top, :], t_top, sems.at[1]),
-        pltpu.make_async_copy(v_hbm.at[:, :, end, :], v_end, sems.at[2]),
-        pltpu.make_async_copy(t_hbm.at[:, end, :], t_end, sems.at[3]),
-    ]
+    pairs = (
+        (design_hbm, design_ref),
+        (gid_hbm, gid_ref),
+        (free_hbm, free_ref),
+        (v_hbm.at[:, :, top, :], v_top),
+        (t_hbm.at[:, top, :], t_top),
+        (v_hbm.at[:, :, end, :], v_end),
+        (t_hbm.at[:, end, :], t_end),
+    )
+    copies = [pltpu.make_async_copy(src, dst, sems.at[k]) for k, (src, dst) in enumerate(pairs)]
     for copy in copies:
         copy.start()
+    for copy in copies[:3]:
+        copy.wait()
     free = free_ref[...].astype(F32)
     gid = gid_ref[...]
     factor = jnp.zeros((ROWS, COLS), F32)
@@ -59,7 +65,7 @@
         factor = jnp.where(gid == g, design_ref[g], factor)
     base_ref[0] = free * factor
     base_ref[1] = 16.0 * free
-    for copy in copies:
+    for copy in copies[3:]:
         copy.wait()
     sub = lax.broadcasted_iota(jnp.int32, (8, COLS), 0)
     for ref, vv, tt, x0, v0, c0 in ((up_ref, v_top, t_top, 0, 0, 0), (dn_ref, v_end, t_end, ROWS - 8, 5, 6)):
@@ -82,135 +88,116 @@
             ref[at + 80 : at + QPAD, :] = jnp.where(sub == 0, -sc * t, 0.0)
 
 
-def prepare_kernel(v_ref, t_ref, base_ref, vt_ref, ct_ref, pack_ref):
-    rid = row_of_lane()
+EDGE_ROWS = 3 * MODES + QPAD
+
+
+def pick_near():
+    k = lane_of() % 8
+    return jnp.where(k < 3, k, jnp.where(k < 6, COLS - 6 + k, 0))
+
+
+def take(value, index):
+    return jnp.take_along_axis(value, index, axis=1, mode="promise_in_bounds")
+
+
+def prepare_kernel(v_ref, t_ref, base_ref, ct_ref, near_ref):
     v2 = v_ref.reshape(3 * MODES * ROWS, COLS)
     t2 = t_ref.reshape(81 * ROWS, COLS)
     sub = lax.broadcasted_iota(jnp.int32, (8, COLS), 0)
+    near = pick_near()
+    slot = lane_of() // 8
 
     def modes_part(n, _):
-        j = n // MGS
-        mg8 = pl.multiple_of((n % MGS) * 8, 8)
-        acc = [jnp.zeros((8, COLS), F32)] * 3
-        for x in range(ROWS):
-            v = v2[pl.ds(n * 8 * ROWS + x, 8, stride=ROWS), :]
-            vt_ref[j, x, pl.ds(mg8, 8), :] = v
-            for c in range(3):
-                acc[c] = jnp.where(rid == x + 3, pick_lanes(v, COLS - 3 + c, 2 - c), acc[c])
-        for c in range(3):
-            pack_ref[pl.ds(pl.multiple_of((j * 3 + c) * MODES + mg8, 8), 8), :] = acc[c]
+        for half in range(2):
+            acc = jnp.zeros((8, COLS), F32)
+            for s in range(16):
+                v = v2[pl.ds(n * 8 * ROWS + half * 16 + s, 8, stride=ROWS), :]
+                acc = jnp.where(slot == s, take(v, near), acc)
+            near_ref[half, pl.ds(pl.multiple_of(n * 8, 8), 8), :] = acc
         return 0
 
     lax.fori_loop(0, 3 * MGS, modes_part, 0)
 
     def coefs(qg, last):
         q8 = pl.multiple_of(qg * 8, 8)
-        acc = [jnp.zeros((8, COLS), F32)] * 2
-        for x in range(ROWS):
-            sc = base_ref[0, x : x + 1, :]
-            fr = base_ref[1, x : x + 1, :]
-            if last:
-                v = jnp.where(sub == 0, -sc * t2[80 * ROWS + x : 80 * ROWS + x + 1, :], 0.0)
-            else:
-                v = diagonal(q8, sub, fr) - sc * t2[pl.ds(qg * 8 * ROWS + x, 8, stride=ROWS), :]
-            ct_ref[x, pl.ds(q8, 8), :] = v
-            for c in range(2):
-                acc[c] = jnp.where(rid == x + 3, pick_lanes(v, COLS - 2 + c, 1 - c), acc[c])
-        for c in range(2):
-            pack_ref[pl.ds(pl.multiple_of(VROWS + c * QPAD + q8, 8), 8), :] = acc[c]
+        for half in range(2):
+            acc = jnp.zeros((8, COLS), F32)
+            for s in range(16):
+                x = half * 16 + s
+                sc = base_ref[0, x : x + 1, :]
+                fr = base_ref[1, x : x + 1, :]
+                if last:
+                    v = jnp.where(sub == 0, -sc * t2[80 * ROWS + x : 80 * ROWS + x + 1, :], 0.0)
+                else:
+                    v = diagonal(q8, sub, fr) - sc * t2[pl.ds(qg * 8 * ROWS + x, 8, stride=ROWS), :]
+                ct_ref[x, pl.ds(q8, 8), :] = v
+                acc = jnp.where(slot == s, take(v, near), acc)
+            near_ref[half, pl.ds(pl.multiple_of(3 * MODES + q8, 8), 8), :] = acc
         return 0
 
     lax.fori_loop(0, 10, lambda qg, _: coefs(qg, False), 0)
     coefs(10, True)
-
-
-def halo_row(ru_ref, rd_ref, b, at_up, at_down, rows):
-    if b < 3:
-        return ru_ref[pl.ds(pl.multiple_of(at_up, 8), rows), :]
-    return rd_ref[pl.ds(pl.multiple_of(at_down, 8), rows), :]
 
 
 MODE_HALO = (0, 1, 2, ROWS + 3, ROWS + 4, ROWS + 5)
 COEF_HALO = (1, 2, ROWS + 3, ROWS + 4)
 HALF = MSG // 2
-
-
-def finish_kernel(pack_ref, ru_ref, rd_ref, right_ref, left_ref, full):
-    rid = row_of_lane()
-
-    def modes_part(n, _):
+FIRST_VMEM = 60
+
+
+def edge_column(c, low, high, halo):
+    b = row_of_lane()
+    even = lane_of() % 2 == 0
+    k = jnp.where(even, 3 + c, 2 - c) if c < 3 else jnp.where(even, c - 3, 8 - c)
+    outer = (b < 3) | (b >= ROWS + 3)
+    at = jnp.where(b < 3, b, jnp.where(b < 19, b - 3, jnp.where(b < ROWS + 3, b - 19, b - ROWS)))
+    index = (at * 8 + k) & (COLS - 1)
+    return jnp.where(outer, take(halo, index), jnp.where(b < 19, take(low, index), take(high, index)))
+
+
+def finish_kernel(near_ref, ru_ref, rd_ref, right_ref, left_ref, halo_ref, full):
+    near = pick_near()
+    slot = lane_of() // 8
+
+    def gather_halo(rows, at_of, at):
+        acc = jnp.zeros((8, COLS), F32)
+        for b in rows:
+            ref = ru_ref if b < 3 else rd_ref
+            v = ref[pl.ds(at_of(b), 8), :]
+            acc = jnp.where(slot == (b if b < 3 else b - ROWS), take(v, near), acc)
+        halo_ref[pl.ds(at, 8), :] = acc
+        return near_ref[0, pl.ds(at, 8), :], near_ref[1, pl.ds(at, 8), :], acc
+
+    def modes_part(n):
         j = n // MGS
         mg8 = (n % MGS) * 8
-        ats = [pl.multiple_of((j * 3 + c) * MODES + mg8, 8) for c in range(3)]
-        acc = [pack_ref[pl.ds(at, 8), :] for at in ats]
-        for b in MODE_HALO:
-            v = halo_row(ru_ref, rd_ref, b, (j * 3 + b) * MODES + mg8, (j * 3 + b - ROWS - 3) * MODES + mg8, 8)
-            for c in range(3):
-                acc[c] = jnp.where(rid == b, pick_lanes(v, COLS - 3 + c, 2 - c), acc[c])
+        parts = gather_halo(
+            MODE_HALO, lambda b: (j * 3 + (b if b < 3 else b - ROWS - 3)) * MODES + mg8, n * 8
+        )
         for c in range(3):
-            full[pl.ds(ats[c], 8), :] = acc[c]
-        return 0
-
-    lax.fori_loop(0, 3 * MGS, modes_part, 0)
-
-    def coef_part(qg, _):
+            full[pl.ds((j * 3 + c) * MODES + mg8, 8), :] = edge_column(c, *parts)
+
+    for n in range(3 * MGS):
+        modes_part(n)
+
+    def coef_part(qg):
         q8 = qg * 8
-        ats = [pl.multiple_of(VROWS + c * QPAD + q8, 8) for c in range(2)]
-        acc = [pack_ref[pl.ds(at, 8), :] for at in ats]
-        for b in COEF_HALO:
-            v = halo_row(ru_ref, rd_ref, b, VROWS + (b - 1) * QPAD + q8, VROWS + (b - ROWS - 3) * QPAD + q8, 8)
-            for c in range(2):
-                acc[c] = jnp.where(rid == b, pick_lanes(v, COLS - 2 + c, 1 - c), acc[c])
-        for c in range(2):
-            full[pl.ds(ats[c], 8), :] = acc[c]
-        return 0
-
-    lax.fori_loop(0, QPAD // 8, coef_part, 0)
+        parts = gather_halo(
+            COEF_HALO,
+            lambda b: VROWS + (b - 1 if b < 3 else b - ROWS - 3) * QPAD + q8,
+            3 * MODES + q8,
+        )
+        for c in (1, 2):
+            full[pl.ds(VROWS + (c - 1) * QPAD + q8, 8), :] = edge_column(c, *parts)
+
+    for qg in range(QPAD // 8):
+        coef_part(qg)
     even = lane_of() % 2 == 0
     for n in range(HALF // 8):
         a = full[n * 8 : n * 8 + 8, :]
         b = full[HALF + n * 8 : HALF + n * 8 + 8, :]
         right_ref[n * 8 : n * 8 + 8, :] = jnp.where(even, a, pltpu.roll(b, 1, 1))
         left_ref[n * 8 : n * 8 + 8, :] = jnp.where(even, pltpu.roll(b, COLS - 1, 1), a)
-
-
-OWN = 6 * MODES + QPAD
-OWN_COEFS = 6 * MODES
-
-
-def own_kernel(vt_ref, ct_ref, ru_ref, rd_ref, out_ref):
-    rid = row_of_lane()
-
-    def modes_part(n, _):
-        j = n // MGS
-        mg8 = pl.multiple_of((n % MGS) * 8, 8)
-        acc = [jnp.zeros((8, COLS), F32)] * 2
-        for b in range(ROWS + 6):
-            if b in MODE_HALO:
-                v = halo_row(ru_ref, rd_ref, b, (j * 3 + b) * MODES + mg8, (j * 3 + b - ROWS - 3) * MODES + mg8, 8)
-            else:
-                v = vt_ref[j, b - 3, pl.ds(mg8, 8), :]
-            for c in range(2):
-                acc[c] = jnp.where(rid == b, pick_lanes(v, c, COLS - 1 - c), acc[c])
-        for c in range(2):
-            out_ref[pl.ds(pl.multiple_of((j * 2 + c) * MODES + mg8, 8), 8), :] = acc[c]
-        return 0
-
-    lax.fori_loop(0, 3 * MGS, modes_part, 0)
-
-    def coef_part(qg, _):
-        q8 = pl.multiple_of(qg * 8, 8)
-        acc = jnp.zeros((8, COLS), F32)
-        for b in range(1, ROWS + 5):
-            if b in COEF_HALO:
-                v = halo_row(ru_ref, rd_ref, b, VROWS + (b - 1) * QPAD + q8, VROWS + (b - ROWS - 3) * QPAD + q8, 8)
-            else:
-                v = ct_ref[b - 3, pl.ds(q8, 8), :]
-            acc = jnp.where(rid == b, pick_lanes(v, 0, COLS - 1), acc)
-        out_ref[pl.ds(pl.multiple_of(OWN_COEFS + q8, 8), 8), :] = acc
-        return 0
-
-    lax.fori_loop(0, QPAD // 8, coef_part, 0)
 
 
 def taps():
@@ -291,9 +278,18 @@
 
 
 def iterate_kernel(
-    vt_ref, ct_ref, ru_ref, rd_ref, own_ref, pl_ref, pr_ref, mass_ref, x_ref, q_ref,
-    a0, a1, a2, a3, b0, b1, b2, b3, coefs, edges_a, edges_b, edges_c, outer, rolled, first, masses, image_0, image_1,
+    v_ref, ct_ref, ru_ref, rd_ref, near_ref, halo_ref, pl_ref, pr_ref, mass_hbm, x_ref, q_ref,
+    a0, a1, a2, a3, b0, b1, b2, b3, coefs, edges_a, edges_b, edges_c, outer, own, rolled, first, masses,
+    image_0, image_1, mass_ref, sem,
 ):
+    region = lax.axis_index("region")
+    column = lax.axis_index("node")
+    total_x = ROWS * lax.axis_size("region")
+    total_y = COLS * lax.axis_size("node")
+    mass_copy = pltpu.make_async_copy(
+        mass_hbm.at[:, pl.ds(pl.multiple_of(column * COLS, COLS), COLS)], mass_ref, sem.at[0]
+    )
+    mass_copy.start()
     field_a, field_b, images = (a0, a1, a2, a3), (b0, b1, b2, b3), (image_0, image_1)
     even = lane_of() % 2 == 0
     for n in range(HALF // 8):
@@ -310,24 +306,32 @@
             row_at(field_a, k, 0)[1, j] = ru_ref[at : at + MODES, :]
             row_at(field_a, ROWS + 3 + k, 0)[1, j] = rd_ref[at : at + MODES, :]
             edges_a[j, k] = outer[at : at + MODES, :]
-        for k in range(2):
-            at = (j * 2 + k) * MODES
-            edges_a[j, 3 + k] = own_ref[at : at + MODES, :]
+
+    def near(at):
+        return near_ref[0, pl.ds(at, 8), :], near_ref[1, pl.ds(at, 8), :], halo_ref[pl.ds(at, 8), :]
+
+    for j in range(3):
+        for mg in range(MGS):
+            for c in (3, 4):
+                edges_a[j, c, group(mg), :] = edge_column(c, *near(j * MODES + mg * 8))
+    for qg in range(QPAD // 8):
+        own[group(qg), :] = edge_column(3, *near(3 * MODES + qg * 8))
+
+    v2 = v_ref.reshape(3 * MODES * ROWS, COLS)
 
     def copy_rows(t, _):
         for k in range(4):
             coefs[4 * t + k + 2] = ct_ref[4 * t + k]
             for j in range(3):
-                row_at(field_a, k + 3, t)[1, j] = vt_ref[j, 4 * t + k]
+                for mg in range(MGS):
+                    at = (j * MODES + mg * 8) * ROWS + 4 * t + k
+                    row_at(field_a, k + 3, t)[1, j, group(mg), :] = v2[pl.ds(at, 8, stride=ROWS), :]
         return 0
 
     lax.fori_loop(0, ROWS // 4, copy_rows, 0)
 
     def outer_coefs(c):
-        if c == 3:
-            at, ref = OWN_COEFS, own_ref
-        else:
-            at, ref = VROWS + (c - 1) * QPAD, outer
+        at, ref = (0, own) if c == 3 else (VROWS + (c - 1) * QPAD, outer)
         return lambda q: ref[at + q : at + q + 1, :]
 
     roll_edges(edges_a, rolled, range(5))
@@ -380,6 +384,9 @@
         put_row(field_a, b, 0, edge_c, keep_in(x_ref, 0, max(b - 3, 0)))
 
     sub = lax.broadcasted_iota(jnp.int32, (16, COLS), 0)
+    mass_copy.wait()
+    ys = (column * COLS + lax.broadcasted_iota(jnp.int32, (16, COLS), 1)).astype(F32)
+    pos_y = 2.0 * (ys + 0.5) / total_y - 1.0
 
     def keep_image(r, t, x):
         for i in range(3):
@@ -390,9 +397,10 @@
             put_row(field_a, r + 2, t, edge_c, keep_in(x_ref, 0, 4 * t + r - 1))
             keep_image(r - 1, t, jnp.maximum(4 * t + r - 4, 0))
             x = 4 * t + r - 3
-            w = jnp.zeros((16, COLS), F32)
-            for n in range(3):
-                w = jnp.where(sub == n, mass_ref[n, pl.ds(x, 1), :], w)
+            xs = jnp.full((16, COLS), region * ROWS + x, jnp.int32).astype(F32)
+            pos_x = 2.0 * (xs + 0.5) / total_x - 1.0
+            place = jnp.where(sub == 0, 1.0, jnp.where(sub == 1, pos_x, jnp.where(sub == 2, pos_y, 0.0)))
+            w = mass_ref[pl.ds(x, 1), :] * place
             lanes = pl.ds(pl.multiple_of(x * COLS, COLS), COLS)
             masses[0:16, lanes], masses[16:32, lanes] = split(w)
             acc = main_stencil(field_a, coefs, r, t)
@@ -428,17 +436,34 @@
         q_ref[:, 96 + 3 * j : 99 + 3 * j] = sums[j]
 
 
-def inverse_factor(gram):
-    shape = (MODES, 2 * MODES)
-    lane = lax.broadcasted_iota(jnp.int32, shape, 1)
-    sub = lax.broadcasted_iota(jnp.int32, shape, 0)
-    eye = jnp.where(lax.broadcasted_iota(jnp.int32, (MODES, MODES), 0) == lax.broadcasted_iota(jnp.int32, (MODES, MODES), 1), 1.0, 0.0)
-    a = jnp.concatenate([gram, eye], axis=1)
+def reciprocal(x):
+    y = pl.reciprocal(x, approx=True)
+    y = y * (2.0 - x * y)
+    return y * (2.0 - x * y)
+
+
+def inverse_factor(gram, column, out):
+    lane = lane_of()
+    rows = [
+        [None if mg < i // 8 else jnp.broadcast_to(gram[group(mg), i : i + 1], (8, COLS)) for mg in range(MGS)]
+        for i in range(MODES)
+    ]
+    inverse = [jnp.where(lane == i, 1.0, 0.0) for i in range(MODES)]
     for k in range(MODES):
-        f = jnp.where(sub > k, a[:, k : k + 1] / a[k : k + 1, k : k + 1], 0.0)
-        a = a - f * a[k : k + 1, :]
-    pivots = jnp.sum(jnp.where(lane == sub, a, 0.0), axis=1, keepdims=True)
-    return a[:, MODES:] / jnp.sqrt(pivots)
+        at = k % 2
+        for mg in range(k // 8, MGS):
+            column[at, group(mg), :] = rows[k][mg]
+        pivot = jnp.broadcast_to(column[at, k : k + 1, :], (8, COLS))
+        over = reciprocal(pivot)
+        scaled = [None if v is None else v * over for v in rows[k]]
+        mine = inverse[k] * over
+        for i in range(k + 1, MODES):
+            f = column[at, i : i + 1, :]
+            for mg in range(i // 8, MGS):
+                rows[i][mg] = rows[i][mg] - f * scaled[mg]
+            inverse[i] = inverse[i] - f * mine
+        out[k : k + 1, :] = (inverse[k] / jnp.sqrt(pivot))[0:1, :]
+    return out[:, 0:MODES]
 
 
 def product(a, b, transposed=False):
@@ -446,26 +471,31 @@
     return lax.dot_general(a, b, dims, precision=lax.Precision.HIGHEST, preferred_element_type=F32)
 
 
-def combine_kernel(nodes, q_ref, x_ref, gid_ref, design_ref, modes_ref, send_ref, reduced_ref, part_ref, weight, bins):
+def combine_kernel(nodes, q_ref, x_ref, gid_ref, design_ref, modes_hbm, send_ref, reduced_ref, part_ref, weight, bins, modes_ref, column, factor, sems):
     q = q_ref[...]
-    w1 = inverse_factor(q[:, 0:32])
+    w1 = inverse_factor(q[:, 0:32], column, factor)
     gram = nodes * product(product(w1, q[:, 32:64]), w1, True)
-    w = nodes * product(inverse_factor(gram), w1)
+    w = nodes * product(inverse_factor(gram, column, factor), w1)
     reduced_ref[...] = product(product(w, q[:, 64:96]), w, True) / nodes
     s = lax.dot_general(
         q[:, 96:112], w, (((0,), (1,)), ((), ())), precision=lax.Precision.HIGHEST, preferred_element_type=F32
     ) / (nodes**0.5)
-    for k, row in enumerate((s[0:1], s[3:4], s[6:7], s[8:9], -s[7:8], s[4:5] - s[2:3])):
-        part_ref[k : k + 1, :] = row
+    part = jnp.concatenate([s[0:1], s[3:4], s[6:7], s[8:9], -s[7:8], s[4:5] - s[2:3]], axis=0)
+    mine = lax.broadcasted_iota(jnp.int32, part.shape, 1) == lax.axis_index("node")
+    part_ref[...] = jnp.sum(jnp.where(mine, part, 0.0), axis=1, keepdims=True)
     high = w.astype(BF16)
     low = (w - high.astype(F32)).astype(BF16)
     mix = jnp.concatenate([jnp.concatenate([high, high], axis=1), jnp.concatenate([low, low], axis=1)], axis=0)
     m2 = modes_ref.reshape(3 * MODES * ROWS, COLS)
     s2 = send_ref.reshape(MODES * PIECE, COLS)
-    step = 4
-
-    def chunk(n, _):
-        lanes = pl.ds(pl.multiple_of(n * step * COLS, step * COLS), step * COLS)
+    step = 8
+
+    def out_copy(n):
+        at = pl.ds(n * step, step)
+        return pltpu.make_async_copy(modes_ref.at[:, :, at, :], modes_hbm.at[:, :, at, :], sems.at[n])
+
+    def chunk(n):
+        lanes = pl.ds(n * step * COLS, step * COLS)
         total = jnp.zeros((8, step * COLS), F32)
         for j in range(3):
             v = jnp.dot(mix, x_ref[j, 0 : 2 * MODES, lanes], preferred_element_type=F32)
@@ -482,10 +512,11 @@
                     s2[pl.ds(mg * 8 * PIECE + j * ROWS + x, 8, stride=PIECE), :] = piece
         total = jnp.sum(total, axis=0, keepdims=True)
         for k in range(step):
-            weight[pl.ds(n * step + k, 1), :] = total[:, k * COLS : (k + 1) * COLS]
-        return 0
-
-    lax.fori_loop(0, ROWS // step, chunk, 0)
+            weight[n * step + k : n * step + k + 1, :] = total[:, k * COLS : (k + 1) * COLS]
+        out_copy(n).start()
+
+    for n in range(ROWS // step):
+        chunk(n)
     gid = gid_ref[...]
     wgt = weight[...]
     for g in range(GROUPS):
@@ -499,6 +530,8 @@
         return 0
 
     lax.fori_loop(0, MODES, put, 0)
+    for n in range(ROWS // step):
+        out_copy(n).wait()
 
 
 def spread_kernel(columns, recv_ref, out_ref):
@@ -507,7 +540,7 @@
             out_ref[i, :, n * COLS : (n + 1) * COLS] = recv_ref[n, i * ROWS : (i + 1) * ROWS, :]
 
 
-def call(kernel, outs, scratch, cost, *args, smem=(), hbm=()):
+def call(kernel, outs, scratch, cost, *args, smem=(), hbm=(), hbm_outs=(), vmem=16):
     flops, size = cost
     return pl.pallas_call(
         kernel,
@@ -516,9 +549,9 @@
             pl.BlockSpec(memory_space=pltpu.SMEM if k in smem else pl.ANY if k in hbm else pltpu.VMEM)
             for k in range(len(args))
         ],
-        out_specs=[pl.BlockSpec(memory_space=pltpu.VMEM) for _ in outs],
+        out_specs=[pl.BlockSpec(memory_space=pl.ANY if k in hbm_outs else pltpu.VMEM) for k in range(len(outs))],
         scratch_shapes=[pltpu.VMEM(*s) if isinstance(s, tuple) else s for s in scratch],
-        compiler_params=pltpu.CompilerParams(vmem_limit_bytes=VMEM),
+        compiler_params=pltpu.CompilerParams(vmem_limit_bytes=vmem * 1024 * 1024),
         cost_estimate=pl.CostEstimate(flops=flops, bytes_accessed=size, transcendentals=0),
     )(*args)
 
@@ -539,11 +572,9 @@
 
 
 def sum_devices(x):
-    x = sum_group(x, "region", (1,))
-    x = sum_group(x, "region", (2,))
-    columns = lax.axis_size("node")
-    copies = jnp.broadcast_to(x[None], (columns,) + x.shape)
-    return jnp.sum(lax.all_to_all(copies, "node", 0, 0, tiled=True), axis=0)
+    for axis, generators in (("region", (1,)), ("node", (1, 2)), ("node", (4, 8)), ("node", (16,)), ("region", (2,))):
+        x = sum_group(x, axis, generators)
+    return x
 
 
 def shift(x, axis, step):
@@ -554,11 +585,8 @@
 def per_device(start_modes, stiffness_tiles, free_mask, group_ids, design, node_mass):
     regions = lax.axis_size("region")
     columns = lax.axis_size("node")
-    total_x = ROWS * regions
     total_y = COLS * columns
-    nodes = float(total_x * total_y)
-    region = lax.axis_index("region")
-    column = lax.axis_index("node")
+    nodes = float(ROWS * regions * total_y)
 
     tiles = stiffness_tiles.reshape(81, ROWS, COLS)
     message = ((MSG, COLS), F32)
@@ -568,31 +596,27 @@
         [((2, ROWS, COLS), F32), message, message],
         [
             ((3, MODES, 8, COLS), F32), ((3, MODES, 8, COLS), F32), ((81, 8, COLS), F32), ((81, 8, COLS), F32),
-            pltpu.SemaphoreType.DMA((4,)),
+            ((ROWS, COLS), jnp.int32), ((ROWS, COLS), jnp.int32), pltpu.SMEM((GROUPS,), F32),
+            pltpu.SemaphoreType.DMA((7,)),
         ],
         (1000000, 2000000),
-        start_modes, tiles, free_mask, group_ids, design, smem=(4,), hbm=(0, 1),
+        start_modes, tiles, free_mask, group_ids, design, hbm=(0, 1, 2, 3, 4), vmem=FIRST_VMEM,
     )
     ru = shift(dn, "region", 1)
     rd = shift(up, "region", -1)
-    vt, ct, packed = call(
+    edge_rows = ((EDGE_ROWS, COLS), F32)
+    ct, near = call(
         prepare_kernel,
-        [((3, ROWS, MODES, COLS), F32), ((ROWS, QPAD, COLS), F32), message],
+        [((ROWS, QPAD, COLS), F32), ((2, EDGE_ROWS, COLS), F32)],
         [],
         (10000000, 6000000),
         start_modes, tiles, base,
     )
-    to_right, to_left = call(finish_kernel, [half, half], [message], (1000000, 1500000), packed, ru, rd)
+    to_right, to_left, halo = call(
+        finish_kernel, [half, half, edge_rows], [message], (1000000, 1500000), near, ru, rd
+    )
     left = shift(to_right, "node", 1)
     right = shift(to_left, "node", -1)
-    (own,) = call(own_kernel, [((OWN, COLS), F32)], [], (10000000, 4000000), vt, ct, ru, rd)
-
-    mass = lax.dynamic_slice(node_mass, (0, column * COLS), (ROWS, COLS))
-    xs = (region * ROWS + jnp.arange(ROWS, dtype=jnp.int32)).astype(F32)
-    ys = (column * COLS + jnp.arange(COLS, dtype=jnp.int32)).astype(F32)
-    pos_x = 2.0 * (xs + 0.5) / total_x - 1.0
-    pos_y = 2.0 * (ys + 0.5) / total_y - 1.0
-    weights = jnp.stack([mass, mass * pos_x[:, None], mass * pos_y[None, :]])
 
     rows = ((ROWS // 4 + 2, 3, 3, MODES, COLS), F32)
     edge = (3, 5, MODES, COLS)
@@ -602,21 +626,23 @@
         [((3, 4 * MODES, wide), BF16), ((MODES, COLS), F32)],
         [rows] * 8 + [
             ((ROWS + 8, QPAD, COLS), F32), (edge, F32), (edge, F32), ((3, MODES, COLS), F32), message,
-            ((3,) + edge, F32), ((3, 2 * MODES, wide), BF16), ((32, ROWS * COLS), BF16),
-            ((3, MODES, COLS), F32), ((3, MODES, COLS), F32),
+            ((QPAD, COLS), F32), ((3,) + edge, F32), ((3, 2 * MODES, wide), BF16), ((32, ROWS * COLS), BF16),
+            ((3, MODES, COLS), F32), ((3, MODES, COLS), F32), ((ROWS, COLS), F32), pltpu.SemaphoreType.DMA((1,)),
         ],
         (100000000, 20000000),
-        vt, ct, ru, rd, own, left, right, weights,
+        start_modes, ct, ru, rd, near, halo, left, right, node_mass, hbm=(8,), vmem=34,
     )
     q = sum_devices(q)
-    modes, send, reduced, part = call(
+    modes, send, reduced, participation = call(
         lambda *refs: combine_kernel(nodes, *refs),
-        [((3, MODES, ROWS, COLS), F32), ((MODES, PIECE, COLS), F32), ((MODES, MODES), F32), ((6, MODES), F32)],
-        [((ROWS, COLS), F32), ((GROUPS, COLS), F32)],
+        [((3, MODES, ROWS, COLS), F32), ((MODES, PIECE, COLS), F32), ((MODES, MODES), F32), ((6, 1), F32)],
+        [
+            ((ROWS, COLS), F32), ((GROUPS, COLS), F32), ((3, MODES, ROWS, COLS), F32),
+            ((2, MODES, COLS), F32), ((MODES, COLS), F32), pltpu.SemaphoreType.DMA((ROWS // 8,)),
+        ],
         (10000000, 10000000),
-        q, x, group_ids, design, smem=(3,),
-    )
-    participation = lax.dynamic_slice(part, (0, column), (6, 1))
+        q, x, group_ids, design, smem=(3,), hbm_outs=(0,),
+    )
     recv = lax.all_to_all(send, "node", 0, 0, tiled=True)
     extra = jnp.sum(recv[:, 3 * ROWS :, :], axis=0)
     (by_column,) = call(

time: 126 us -> 112 us (0.89)
  blocking collectives: 44.9 us -> 21.8 us
  waiting for transfers between devices: 3.14 us -> 22.3 us
  Pallas kernels: 45.1 us -> 31.3 us
  starting transfers between devices: 23.5 us -> 33.3 us
  local copies, waits for them, and re-layouts: 7.47 us -> 1.88 us
    all_to_all x1 -> x0, blocking collectives: 19.3 us -> none  [sum_devices(): return jnp.sum(lax.all_to_all(copies, 'node', 0, 0, tiled=True), axis=0)]
    pallas_call x7 -> x6, Pallas kernels: 45.1 us -> 31.3 us  [call(): pl.pallas_call(kernel, out_shape=[jax.ShapeDtypeStruct(s, d) for s, d in...]
    ppermute x4 -> x11, waiting for transfers between devices: 3.13 us -> 14.9 us  [swap(): return lax.ppermute(x, axis, [(i, i ^ k) for i in range(n)])]
    ppermute x4 -> x11, starting transfers between devices: 10.7 us -> 20.5 us  [swap(): return lax.ppermute(x, axis, [(i, i ^ k) for i in range(n)])]
    ppermute x4, waiting for transfers between devices: 0.01 us -> 7.43 us  [shift(): lax.ppermute(x, axis, [(i, i + step) for i in range(n) if 0 <= i + step <...]
    unnamed x19 -> x13, local copies, waits for them, and re-layouts: 6.83 us -> 1.37 us
    all_to_all x1, blocking collectives: 25.6 us -> 21.8 us  [per_device(): recv = lax.all_to_all(send, 'node', 0, 0, tiled=True)]
  transfers between devices with their start and end apart: 8 -> 15, of which waited for: 3 -> 12; matrix products, arithmetic and copies ran while one was open for 1% -> 1% of each run, Pallas kernels for 10% -> 4%
where the time goes in v4:
time: 112 us; the launch traced here: 111 us
  starting transfers between devices  33.3 us (30%)
  Pallas kernels  31.3 us (28%)
  waiting for transfers between devices  22.3 us (20%)
  blocking collectives  21.8 us (19%)
  local copies, waits for them, and re-layouts  1.88 us (2%)
    pallas_call x6, Pallas kernels, call(): pl.pallas_call(kernel, out_shape=[jax.ShapeDtypeStruct(s, d) for s, d in...  31.3 us
    all_to_all x1, blocking collectives, per_device(): recv = lax.all_to_all(send, 'node', 0, 0, tiled=True)  21.8 us
    ppermute x11, starting transfers between devices, swap(): return lax.ppermute(x, axis, [(i, i ^ k) for i in range(n)])  20.5 us
    ppermute x11, waiting for transfers between devices, swap(): return lax.ppermute(x, axis, [(i, i ^ k) for i in range(n)])  14.9 us
    ppermute x4, starting transfers between devices, shift(): lax.ppermute(x, axis, [(i, i + step) for i in range(n) if 0 <= i + step <...  12.8 us
    ppermute x4, waiting for transfers between devices, shift(): lax.ppermute(x, axis, [(i, i + step) for i in range(n) if 0 <= i + step <...  7.43 us
  transfers between devices with their start and end apart: 15, of which 12 were waited for; matrix products, arithmetic and copies ran while one was open for 1% of the time, Pallas kernels for 4%

profile of v4, /device:TPU:1, one launch (start us, length us, event | category | flops | bytes accessed | tf_op | source)
XLA Modules:
  0.0 111.4 jit_solution(14294224144033578212)
XLA Ops:
  0.7 2.4 %shard_map.101 = (f32[2,32,128]{2,1,0:T(8,128)}, f32[464,128]{1,0:T(8,128)}, f32[464,128]{1,0:T(8,128)}) custom-call(f32[3,32,32,128]{3,2,1,0:T(8,128)} %v_ref.3, f32[81,32,128]{2,1,0:T(8,128)} %bitcast.6, s32[32,128]{1,0:T(8,128)} %free_hbm.1, s32[32,128]{1,0:T(8,128)} %refs_2_.1, f32[64]{0:T(128)} %refs_3_.1), custom_call_target="tpu_custom_call" | custom-call | flops 1000000 | bytes 2000000 | tf_op jit(solution)/shard_map/pallas_call | solution.py:545
  3.0 6.0 %collective-permute-start = (f32[464,128]{1,0:T(8,128)}, f32[464,128]{1,0:T(8,128)S(1)}, u32[]{:S(2)}, u32[]{:S(2)}) collective-permute-start(f32[464,128]{1,0:T(8,128)} %get-tuple-element.21), channel_id=1, source_target_pairs={{0,32},{32,64},{64,96},{1,33},{33,65},{65,97},{2,34},{34,66},{66,9... | collective-permute-start | bytes 712712 | tf_op jit(solution)/shard_map/ppermute | solution.py:582
  9.1 1.9 %collective-permute-start.1 = (f32[464,128]{1,0:T(8,128)}, f32[464,128]{1,0:T(8,128)S(1)}, u32[]{:S(2)}, u32[]{:S(2)}) collective-permute-start(f32[464,128]{1,0:T(8,128)} %get-tuple-element.22), channel_id=1, source_target_pairs={{32,0},{64,32},{96,64},{33,1},{65,33},{97,65},{34,2},{66,34},{98,6... | collective-permute-start | bytes 712712 | tf_op jit(solution)/shard_map/ppermute | solution.py:582
  11.1 0.7 copy-done.4
  11.8 3.5 %shard_map.102 = (f32[32,88,128]{2,1,0:T(8,128)S(1)}, f32[2,184,128]{2,1,0:T(8,128)S(1)}) custom-call(f32[3,32,32,128]{3,2,1,0:T(8,128)S(1)} %copy-done, f32[81,32,128]{2,1,0:T(8,128)S(1)} %bitcast.7, f32[2,32,128]{2,1,0:T(8,128)S(1)} %copy-done.4), custom_call_target="tpu_custom_call" | custom-call | flops 10000000 | bytes 6000000 | tf_op jit(solution)/shard_map/pallas_call | solution.py:545
  15.3 3.0 %collective-permute-done.1.rd_ref = f32[464,128]{1,0:T(8,128)S(1)} collective-permute-done((f32[464,128]{1,0:T(8,128)}, f32[464,128]{1,0:T(8,128)S(1)}, u32[]{:S(2)}, u32[]{:S(2)}) %collective-permute-start.1) | collective-permute-done | bytes 237600 | tf_op jit(solution)/shard_map/ppermute | solution.py:582
  18.2 1.4 %shard_map.103 = (f32[232,128]{1,0:T(8,128)S(1)}, f32[232,128]{1,0:T(8,128)S(1)}, f32[184,128]{1,0:T(8,128)S(1)}) custom-call(f32[2,184,128]{2,1,0:T(8,128)S(1)} %get-tuple-element.23.near_ref, f32[464,128]{1,0:T(8,128)S(1)} %collective-permute-done.ru_ref, f32[464,128]{1,0:T(8,128)S(1)} %collective-permute-done.1.rd_ref), custom_call_target="tpu_custom_call" | custom-call | flops 1000000 | bytes 1500000 | tf_op jit(solution)/shard_map/pallas_call | solution.py:545
  19.6 3.5 %collective-permute-start.2 = (f32[232,128]{1,0:T(8,128)S(1)}, f32[232,128]{1,0:T(8,128)S(1)}, u32[]{:S(2)}, u32[]{:S(2)}) collective-permute-start(f32[232,128]{1,0:T(8,128)S(1)} %get-tuple-element.25), channel_id=1, source_target_pairs={{0,1},{1,2},{2,3},{3,4},{4,5},{5,6},{6,7},{7,8},{8,9},{9,10},{10,1... | collective-permute-start | bytes 356360 | tf_op jit(solution)/shard_map/ppermute | solution.py:582
  23.2 1.3 %collective-permute-start.3 = (f32[232,128]{1,0:T(8,128)S(1)}, f32[232,128]{1,0:T(8,128)S(1)}, u32[]{:S(2)}, u32[]{:S(2)}) collective-permute-start(f32[232,128]{1,0:T(8,128)S(1)} %get-tuple-element.26), channel_id=1, source_target_pairs={{1,0},{2,1},{3,2},{4,3},{5,4},{6,5},{7,6},{8,7},{9,8},{10,9},{11,1... | collective-permute-start | bytes 356360 | tf_op jit(solution)/shard_map/ppermute | solution.py:582
  24.5 0.5 collective-permute-done.2.pl_ref
  25.0 4.0 %collective-permute-done.3.pr_ref = f32[232,128]{1,0:T(8,128)S(1)} collective-permute-done((f32[232,128]{1,0:T(8,128)S(1)}, f32[232,128]{1,0:T(8,128)S(1)}, u32[]{:S(2)}, u32[]{:S(2)}) %collective-permute-start.3) | collective-permute-done | bytes 118816 | tf_op jit(solution)/shard_map/ppermute | solution.py:582
  28.9 16.6 %shard_map.104 = (bf16[3,128,5120]{2,1,0:T(8,128)(2,1)S(1)}, f32[32,128]{1,0:T(8,128)S(1)}) custom-call(f32[3,32,32,128]{3,2,1,0:T(8,128)S(1)} %copy-done, f32[32,88,128]{2,1,0:T(8,128)S(1)} %get-tuple-element.20.ct_ref, f32[464,128]{1,0:T(8,128)S(1)} %collective-permute-done.ru_ref, f32[464,128]{1,0:T(8,128)S(1)} %collective-permute-done.1.rd_ref, ...), custom_call_target="tpu_custom_call" | custom-call | flops 100000000 | bytes 20000000 | tf_op jit(solution)/shard_map/pallas_call | solution.py:545
  45.7 1.2 %collective-permute-done.4 = f32[32,128]{1,0:T(8,128)S(1)} collective-permute-done((f32[32,128]{1,0:T(8,128)S(1)}, f32[32,128]{1,0:T(8,128)S(1)}, u32[]{:S(2)}, u32[]{:S(2)}) %collective-permute-start.4) | collective-permute-done | bytes 16416 | tf_op jit(solution)/shard_map/ppermute | solution.py:561
  46.8 4.1 %collective-permute-start.7 = (f32[32,128]{1,0:T(8,128)S(1)}, f32[32,128]{1,0:T(8,128)S(1)}, u32[]{:S(2)}, u32[]{:S(2)}) collective-permute-start(f32[32,128]{1,0:T(8,128)S(1)} %add.33), channel_id=1, source_target_pairs={{0,3},{1,2},{2,1},{3,0},{4,7},{5,6},{6,5},{7,4},{8,11},{9,10},{10,... | collective-permute-start | bytes 49160 | tf_op jit(solution)/shard_map/ppermute | solution.py:561
  50.9 0.7 collective-permute-start.5
  51.6 0.5 collective-permute-done.7
  52.0 3.0 %collective-permute-done.6 = f32[32,128]{1,0:T(8,128)S(1)} collective-permute-done((f32[32,128]{1,0:T(8,128)S(1)}, f32[32,128]{1,0:T(8,128)S(1)}, u32[]{:S(2)}, u32[]{:S(2)}) %collective-permute-start.6) | collective-permute-done | bytes 16416 | tf_op jit(solution)/shard_map/ppermute | solution.py:561
  55.0 4.9 %collective-permute-start.10 = (f32[32,128]{1,0:T(8,128)S(1)}, f32[32,128]{1,0:T(8,128)S(1)}, u32[]{:S(2)}, u32[]{:S(2)}) collective-permute-start(f32[32,128]{1,0:T(8,128)S(1)} %add_add_fusion.1), channel_id=1, source_target_pairs={{0,12},{1,13},{2,14},{3,15},{4,8},{5,9},{6,10},{7,11},{8,4},{9,5},... | collective-permute-start | bytes 49160 | tf_op jit(solution)/shard_map/ppermute | solution.py:561
  59.9 0.7 collective-permute-start.8
  61.1 3.0 %collective-permute-done.9 = f32[32,128]{1,0:T(8,128)S(1)} collective-permute-done((f32[32,128]{1,0:T(8,128)S(1)}, f32[32,128]{1,0:T(8,128)S(1)}, u32[]{:S(2)}, u32[]{:S(2)}) %collective-permute-start.9) | collective-permute-done | bytes 16416 | tf_op jit(solution)/shard_map/ppermute | solution.py:561
  64.1 2.6 %collective-permute-done.11 = f32[32,128]{1,0:T(8,128)S(1)} collective-permute-done((f32[32,128]{1,0:T(8,128)S(1)}, f32[32,128]{1,0:T(8,128)S(1)}, u32[]{:S(2)}, u32[]{:S(2)}) %collective-permute-start.11) | collective-permute-done | bytes 16416 | tf_op jit(solution)/shard_map/ppermute | solution.py:561
  66.7 1.3 %collective-permute-start.12 = (f32[32,128]{1,0:T(8,128)S(1)}, f32[32,128]{1,0:T(8,128)S(1)}, u32[]{:S(2)}, u32[]{:S(2)}) collective-permute-start(f32[32,128]{1,0:T(8,128)S(1)} %add.40), channel_id=1, source_target_pairs={{0,64},{32,96},{64,0},{96,32},{1,65},{33,97},{65,1},{97,33},{2,66}... | collective-permute-start | bytes 49160 | tf_op jit(solution)/shard_map/ppermute | solution.py:561
  68.1 2.8 %collective-permute-done.12 = f32[32,128]{1,0:T(8,128)S(1)} collective-permute-done((f32[32,128]{1,0:T(8,128)S(1)}, f32[32,128]{1,0:T(8,128)S(1)}, u32[]{:S(2)}, u32[]{:S(2)}) %collective-permute-start.12) | collective-permute-done | bytes 16416 | tf_op jit(solution)/shard_map/ppermute | solution.py:561
  70.8 6.1 %shard_map.105 = (f32[3,32,32,128]{3,2,1,0:T(8,128)}, f32[32,104,128]{2,1,0:T(8,128)S(1)}, f32[32,32]{1,0:T(8,128)}, f32[6,1]{1,0:T(8,128)S(1)}) custom-call(f32[32,128]{1,0:T(8,128)S(1)} %add.41.refs_0_, bf16[3,128,5120]{2,1,0:T(8,128)(2,1)S(1)} %get-tuple-element.28.refs_1_, s32[32,128]{1,0:T(8,128)S(1)} %copy-done.3, f32[64]{0:T(128)S(1)} %copy-done.5), custom_call_target="tpu_custom_call" | custom-call | flops 10000000 | bytes 10000000 | tf_op jit(solution)/shard_map/pallas_call | solution.py:545
  77.0 21.8 %all_to_all.5.refs_0_ = f32[32,104,128]{2,1,0:T(8,128)S(1)} all-to-all(f32[32,104,128]{2,1,0:T(8,128)S(1)} %get-tuple-element.30), channel_id=1, replica_groups=mesh['region'=4,'node'=32] {'node'}, dimensions={0} | all-to-all | bytes 3407872 | tf_op jit(solution)/shard_map/all_to_all | solution.py:646
  98.8 7.3 %collective-permute-start.13 = (f32[8,128]{1,0:T(8,128)S(1)}, f32[8,128]{1,0:T(8,128)S(1)}, u32[]{:S(2)}, u32[]{:S(2)}) collective-permute-start(f32[8,128]{1,0:T(8,128)S(1)} %slice_reduce_fusion), channel_id=1, source_target_pairs={{0,32},{32,0},{64,96},{96,64},{1,33},{33,1},{65,97},{97,65},{2,34}... | collective-permute-start | bytes 12296 | tf_op jit(solution)/shard_map/ppermute | solution.py:561
  106.1 0.8 collective-permute-done.13
  106.9 1.3 %collective-permute-start.14 = (f32[8,128]{1,0:T(8,128)S(1)}, f32[8,128]{1,0:T(8,128)S(1)}, u32[]{:S(2)}, u32[]{:S(2)}) collective-permute-start(f32[8,128]{1,0:T(8,128)S(1)} %add.42), channel_id=1, source_target_pairs={{0,64},{32,96},{64,0},{96,32},{1,65},{33,97},{65,1},{97,33},{2,66}... | collective-permute-start | bytes 12296 | tf_op jit(solution)/shard_map/ppermute | solution.py:561
  108.3 0.6 copy.12
  108.9 1.3 %shard_map.106 = f32[3,32,4096]{2,1,0:T(8,128)} custom-call(f32[32,104,128]{2,1,0:T(8,128)S(1)} %all_to_all.5.refs_0_), custom_call_target="tpu_custom_call" | custom-call | flops 10000 | bytes 6000000 | tf_op jit(solution)/shard_map/pallas_call | solution.py:545
  110.1 0.7 collective-permute-done.14
  110.9 0.5 slice_bitcast_fusion
  (27 shorter events, 0.7 us)
Async XLA Ops:
  0.6 10.4 %copy-start = (f32[3,32,32,128]{3,2,1,0:T(8,128)S(1)}, f32[3,32,32,128]{3,2,1,0:T(8,128)}, u32[]{:S(2)}) copy-start(f32[3,32,32,128]{3,2,1,0:T(8,128)} %v_ref.3) | copy-start | bytes 4718596
  0.6 10.4 %copy-start.1 = (f32[9,3,3,32,128]{4,3,2,1,0:T(8,128)S(1)}, f32[9,3,3,32,128]{4,3,2,1,0:T(8,128)}, u32[]{:S(2)}) copy-start(f32[9,3,3,32,128]{4,3,2,1,0:T(8,128)} %param.7) | copy-start | bytes 3981316
  3.0 12.2 %collective-permute-start = (f32[464,128]{1,0:T(8,128)}, f32[464,128]{1,0:T(8,128)S(1)}, u32[]{:S(2)}, u32[]{:S(2)}) collective-permute-start(f32[464,128]{1,0:T(8,128)} %get-tuple-element.21), channel_id=1, source_target_pairs={{0,32},{32,64},{64,96},{1,33},{33,65},{65,97},{2,34},{34,66},{66,9... | collective-permute-start | bytes 712712 | tf_op jit(solution)/shard_map/ppermute | solution.py:582
  9.1 9.1 %collective-permute-start.1 = (f32[464,128]{1,0:T(8,128)}, f32[464,128]{1,0:T(8,128)S(1)}, u32[]{:S(2)}, u32[]{:S(2)}) collective-permute-start(f32[464,128]{1,0:T(8,128)} %get-tuple-element.22), channel_id=1, source_target_pairs={{32,0},{64,32},{96,64},{33,1},{65,33},{97,65},{34,2},{66,34},{98,6... | collective-permute-start | bytes 712712 | tf_op jit(solution)/shard_map/ppermute | solution.py:582
  11.0 0.8 copy-start.4
  11.8 17.1 %copy-start.2 = (f32[32,4096]{1,0:T(8,128)S(1)}, f32[32,4096]{1,0:T(8,128)}, u32[]{:S(2)}) copy-start(f32[32,4096]{1,0:T(8,128)} %mass_hbm.1) | copy-start | bytes 1572868
  19.6 5.4 %collective-permute-start.2 = (f32[232,128]{1,0:T(8,128)S(1)}, f32[232,128]{1,0:T(8,128)S(1)}, u32[]{:S(2)}, u32[]{:S(2)}) collective-permute-start(f32[232,128]{1,0:T(8,128)S(1)} %get-tuple-element.25), channel_id=1, source_target_pairs={{0,1},{1,2},{2,3},{3,4},{4,5},{5,6},{6,7},{7,8},{8,9},{9,10},{10,1... | collective-permute-start | bytes 356360 | tf_op jit(solution)/shard_map/ppermute | solution.py:582
  23.2 5.8 %collective-permute-start.3 = (f32[232,128]{1,0:T(8,128)S(1)}, f32[232,128]{1,0:T(8,128)S(1)}, u32[]{:S(2)}, u32[]{:S(2)}) collective-permute-start(f32[232,128]{1,0:T(8,128)S(1)} %get-tuple-element.26), channel_id=1, source_target_pairs={{1,0},{2,1},{3,2},{4,3},{5,4},{6,5},{7,6},{8,7},{9,8},{10,9},{11,1... | collective-permute-start | bytes 356360 | tf_op jit(solution)/shard_map/ppermute | solution.py:582
  28.9 41.9 %copy-start.3 = (s32[32,128]{1,0:T(8,128)S(1)}, s32[32,128]{1,0:T(8,128)}, u32[]{:S(2)}) copy-start(s32[32,128]{1,0:T(8,128)} %refs_2_.1) | copy-start | bytes 49156
  28.9 41.9 %copy-start.5 = (f32[64]{0:T(128)S(1)}, f32[64]{0:T(128)}, u32[]{:S(2)}) copy-start(f32[64]{0:T(128)} %refs_3_.1) | copy-start | bytes 772
  45.6 1.3 %collective-permute-start.4 = (f32[32,128]{1,0:T(8,128)S(1)}, f32[32,128]{1,0:T(8,128)S(1)}, u32[]{:S(2)}, u32[]{:S(2)}) collective-permute-start(f32[32,128]{1,0:T(8,128)S(1)} %get-tuple-element.27), channel_id=1, source_target_pairs={{0,32},{32,0},{64,96},{96,64},{1,33},{33,1},{65,97},{97,65},{2,34}... | collective-permute-start | bytes 49160 | tf_op jit(solution)/shard_map/ppermute | solution.py:561
  46.8 5.2 %collective-permute-start.7 = (f32[32,128]{1,0:T(8,128)S(1)}, f32[32,128]{1,0:T(8,128)S(1)}, u32[]{:S(2)}, u32[]{:S(2)}) collective-permute-start(f32[32,128]{1,0:T(8,128)S(1)} %add.33), channel_id=1, source_target_pairs={{0,3},{1,2},{2,1},{3,0},{4,7},{5,6},{6,5},{7,4},{8,11},{9,10},{10,... | collective-permute-start | bytes 49160 | tf_op jit(solution)/shard_map/ppermute | solution.py:561
  50.9 4.1 %collective-permute-start.6 = (f32[32,128]{1,0:T(8,128)S(1)}, f32[32,128]{1,0:T(8,128)S(1)}, u32[]{:S(2)}, u32[]{:S(2)}) collective-permute-start(f32[32,128]{1,0:T(8,128)S(1)} %add.33), channel_id=1, source_target_pairs={{0,2},{1,3},{2,0},{3,1},{4,6},{5,7},{6,4},{7,5},{8,10},{9,11},{10,... | collective-permute-start | bytes 49160 | tf_op jit(solution)/shard_map/ppermute | solution.py:561
  50.9 4.1 %collective-permute-start.5 = (f32[32,128]{1,0:T(8,128)S(1)}, f32[32,128]{1,0:T(8,128)S(1)}, u32[]{:S(2)}, u32[]{:S(2)}) collective-permute-start(f32[32,128]{1,0:T(8,128)S(1)} %add.33), channel_id=1, source_target_pairs={{0,1},{1,0},{2,3},{3,2},{4,5},{5,4},{6,7},{7,6},{8,9},{9,8},{10,11... | collective-permute-start | bytes 49160 | tf_op jit(solution)/shard_map/ppermute | solution.py:561
  55.0 6.0 %collective-permute-start.10 = (f32[32,128]{1,0:T(8,128)S(1)}, f32[32,128]{1,0:T(8,128)S(1)}, u32[]{:S(2)}, u32[]{:S(2)}) collective-permute-start(f32[32,128]{1,0:T(8,128)S(1)} %add_add_fusion.1), channel_id=1, source_target_pairs={{0,12},{1,13},{2,14},{3,15},{4,8},{5,9},{6,10},{7,11},{8,4},{9,5},... | collective-permute-start | bytes 49160 | tf_op jit(solution)/shard_map/ppermute | solution.py:561
  59.9 4.1 %collective-permute-start.9 = (f32[32,128]{1,0:T(8,128)S(1)}, f32[32,128]{1,0:T(8,128)S(1)}, u32[]{:S(2)}, u32[]{:S(2)}) collective-permute-start(f32[32,128]{1,0:T(8,128)S(1)} %add_add_fusion.1), channel_id=1, source_target_pairs={{0,8},{1,9},{2,10},{3,11},{4,12},{5,13},{6,14},{7,15},{8,0},{9,1},... | collective-permute-start | bytes 49160 | tf_op jit(solution)/shard_map/ppermute | solution.py:561
  59.9 4.1 %collective-permute-start.8 = (f32[32,128]{1,0:T(8,128)S(1)}, f32[32,128]{1,0:T(8,128)S(1)}, u32[]{:S(2)}, u32[]{:S(2)}) collective-permute-start(f32[32,128]{1,0:T(8,128)S(1)} %add_add_fusion.1), channel_id=1, source_target_pairs={{0,4},{1,5},{2,6},{3,7},{4,0},{5,1},{6,2},{7,3},{8,12},{9,13},{10,... | collective-permute-start | bytes 49160 | tf_op jit(solution)/shard_map/ppermute | solution.py:561
  64.0 2.7 %collective-permute-start.11 = (f32[32,128]{1,0:T(8,128)S(1)}, f32[32,128]{1,0:T(8,128)S(1)}, u32[]{:S(2)}, u32[]{:S(2)}) collective-permute-start(f32[32,128]{1,0:T(8,128)S(1)} %add_add_fusion), channel_id=1, source_target_pairs={{0,16},{1,17},{2,18},{3,19},{4,20},{5,21},{6,22},{7,23},{8,24},{9,... | collective-permute-start | bytes 49160 | tf_op jit(solution)/shard_map/ppermute | solution.py:561
  66.7 4.1 %collective-permute-start.12 = (f32[32,128]{1,0:T(8,128)S(1)}, f32[32,128]{1,0:T(8,128)S(1)}, u32[]{:S(2)}, u32[]{:S(2)}) collective-permute-start(f32[32,128]{1,0:T(8,128)S(1)} %add.40), channel_id=1, source_target_pairs={{0,64},{32,96},{64,0},{96,32},{1,65},{33,97},{65,1},{97,33},{2,66}... | collective-permute-start | bytes 49160 | tf_op jit(solution)/shard_map/ppermute | solution.py:561
  98.8 8.1 %collective-permute-start.13 = (f32[8,128]{1,0:T(8,128)S(1)}, f32[8,128]{1,0:T(8,128)S(1)}, u32[]{:S(2)}, u32[]{:S(2)}) collective-permute-start(f32[8,128]{1,0:T(8,128)S(1)} %slice_reduce_fusion), channel_id=1, source_target_pairs={{0,32},{32,0},{64,96},{96,64},{1,33},{33,1},{65,97},{97,65},{2,34}... | collective-permute-start | bytes 12296 | tf_op jit(solution)/shard_map/ppermute | solution.py:561
  106.9 4.0 %collective-permute-start.14 = (f32[8,128]{1,0:T(8,128)S(1)}, f32[8,128]{1,0:T(8,128)S(1)}, u32[]{:S(2)}, u32[]{:S(2)}) collective-permute-start(f32[8,128]{1,0:T(8,128)S(1)} %add.42), channel_id=1, source_target_pairs={{0,64},{32,96},{64,0},{96,32},{1,65},{33,97},{65,1},{97,33},{2,66}... | collective-permute-start | bytes 12296 | tf_op jit(solution)/shard_map/ppermute | solution.py:561

commit v5 on v4

--- a/solution.py
+++ b/solution.py
@@ -216,19 +216,18 @@
     return field[r % 4].at[t + r // 4]
 
 
-def put_row(field, r, t, edge_at, keep=None):
+def put_row(field, r, t, edge_at, keep):
     row = row_at(field, r, t)
     lane = lane_of()
     turn = (4 * COLS - 2 * r - 8 * t) % COLS
     for j in range(3):
         for mg in range(MGS):
             v = row[1, j, group(mg), :]
-            e = pltpu.roll(edge_at(j, mg), turn, 1)
+            e = pltpu.roll(edge_at(j, 2, mg), turn, 1)
             row[0, j, group(mg), :] = jnp.where(lane == 0, e, pltpu.roll(v, 1, 1))
             row[2, j, group(mg), :] = jnp.where(lane == COLS - 1, e, pltpu.roll(v, COLS - 1, 1))
-    if keep is not None:
-        for j in range(3):
-            keep(j, row[1, j])
+    for j in range(3):
+        keep(j, row[1, j])
 
 
 def main_stencil(field, coefs, r, t):
@@ -277,9 +276,56 @@
     return keep
 
 
+def first_kernel(v_ref, ct_ref, ru_ref, rd_ref, u0, u1, u2, u3, coefs, a0, a1, a2, a3):
+    field, raw = (a0, a1, a2, a3), (u0, u1, u2, u3)
+    for k in range(2):
+        coefs[k] = ru_ref[VROWS + k * QPAD : VROWS + (k + 1) * QPAD, :]
+        coefs[ROWS + 2 + k] = rd_ref[VROWS + k * QPAD : VROWS + (k + 1) * QPAD, :]
+    v2 = v_ref.reshape(3 * MODES * ROWS, COLS)
+
+    def put(row, j, mg, v):
+        row[0, j, group(mg), :] = pltpu.roll(v, 1, 1)
+        row[1, j, group(mg), :] = v
+        row[2, j, group(mg), :] = pltpu.roll(v, COLS - 1, 1)
+
+    def put_own(r, t):
+        x = 4 * t + r - 3
+        coefs[x + 2] = ct_ref[x]
+        for j in range(3):
+            for mg in range(MGS):
+                at = (j * MODES + mg * 8) * ROWS + x
+                put(row_at(field, r, t), j, mg, v2[pl.ds(at, 8, stride=ROWS), :])
+
+    def put_halo(ref, r, k):
+        for j in range(3):
+            for mg in range(MGS):
+                at = (j * 3 + k) * MODES + mg * 8
+                put(row_at(field, r, 0), j, mg, ref[at : at + 8, :])
+
+    for k in range(3):
+        put_halo(ru_ref, k, k)
+        put_halo(rd_ref, ROWS + 3 + k, k)
+
+    def rows(t, _):
+        for r in range(1, 5):
+            put_own(r + 2, t)
+            acc = main_stencil(field, coefs, r, t)
+            for i in range(3):
+                for mg in range(MGS):
+                    raw[r % 4][t + r // 4, i, group(mg), :] = acc[i][mg]
+        return 0
+
+    lax.fori_loop(0, ROWS // 4, rows, 0)
+    for r in range(ROWS + 1, ROWS + 5):
+        acc = main_stencil(field, coefs, r, 0)
+        for i in range(3):
+            for mg in range(MGS):
+                raw[r % 4][r // 4, i, group(mg), :] = acc[i][mg]
+
+
 def iterate_kernel(
-    v_ref, ct_ref, ru_ref, rd_ref, near_ref, halo_ref, pl_ref, pr_ref, mass_hbm, x_ref, q_ref,
-    a0, a1, a2, a3, b0, b1, b2, b3, coefs, edges_a, edges_b, edges_c, outer, own, rolled, first, masses,
+    u0, u1, u2, u3, coefs, near_ref, halo_ref, pl_ref, pr_ref, mass_hbm, x_ref, q_ref,
+    a0, a1, a2, a3, b0, b1, b2, b3, edges_a, edges_b, edges_c, outer, own, rolled, first, masses,
     image_0, image_1, mass_ref, sem,
 ):
     region = lax.axis_index("region")
@@ -291,20 +337,16 @@
     )
     mass_copy.start()
     field_a, field_b, images = (a0, a1, a2, a3), (b0, b1, b2, b3), (image_0, image_1)
+    raw = (u0, u1, u2, u3)
     even = lane_of() % 2 == 0
     for n in range(HALF // 8):
         a = pl_ref[n * 8 : n * 8 + 8, :]
         b = pr_ref[n * 8 : n * 8 + 8, :]
         outer[n * 8 : n * 8 + 8, :] = jnp.where(even, a, b)
         outer[HALF + n * 8 : HALF + n * 8 + 8, :] = jnp.where(even, pltpu.roll(a, COLS - 1, 1), pltpu.roll(b, 1, 1))
-    for k in range(2):
-        coefs[k] = ru_ref[VROWS + k * QPAD : VROWS + (k + 1) * QPAD, :]
-        coefs[ROWS + 2 + k] = rd_ref[VROWS + k * QPAD : VROWS + (k + 1) * QPAD, :]
     for j in range(3):
         for k in range(3):
             at = (j * 3 + k) * MODES
-            row_at(field_a, k, 0)[1, j] = ru_ref[at : at + MODES, :]
-            row_at(field_a, ROWS + 3 + k, 0)[1, j] = rd_ref[at : at + MODES, :]
             edges_a[j, k] = outer[at : at + MODES, :]
 
     def near(at):
@@ -317,19 +359,6 @@
     for qg in range(QPAD // 8):
         own[group(qg), :] = edge_column(3, *near(3 * MODES + qg * 8))
 
-    v2 = v_ref.reshape(3 * MODES * ROWS, COLS)
-
-    def copy_rows(t, _):
-        for k in range(4):
-            coefs[4 * t + k + 2] = ct_ref[4 * t + k]
-            for j in range(3):
-                for mg in range(MGS):
-                    at = (j * MODES + mg * 8) * ROWS + 4 * t + k
-                    row_at(field_a, k + 3, t)[1, j, group(mg), :] = v2[pl.ds(at, 8, stride=ROWS), :]
-        return 0
-
-    lax.fori_loop(0, ROWS // 4, copy_rows, 0)
-
     def outer_coefs(c):
         at, ref = (0, own) if c == 3 else (VROWS + (c - 1) * QPAD, outer)
         return lambda q: ref[at + q : at + q + 1, :]
@@ -346,13 +375,10 @@
         for mg in range(MGS):
             edges_c[i, group(mg), :] = acc[i][mg]
 
-    def edge_a(j, mg):
-        return edges_a[j, 2, group(mg), :]
-
-    def edge_b(j, mg):
-        return edges_b[j, 2, group(mg), :]
-
-    def edge_c(j, mg):
+    def edge_b(j, c, mg):
+        return edges_b[j, c, group(mg), :]
+
+    def edge_c(j, c, mg):
         return edges_c[j, group(mg), :]
 
     def store(row, acc):
@@ -360,16 +386,20 @@
             for mg in range(MGS):
                 row[1, i, group(mg), :] = acc[i][mg]
 
-    for b in range(3):
-        put_row(field_a, b, 0, edge_a)
-
-    def first_rows(t, _):
+    side = (lane_of() == 0) | (lane_of() == COLS - 1)
+
+    def centre_rows(t, _):
         for r in range(1, 5):
-            put_row(field_a, r + 2, t, edge_a)
-            store(row_at(field_b, r, t), main_stencil(field_a, coefs, r, t))
+            turn = (4 * COLS - 2 * r - 8 * t) % COLS
+            for j in range(3):
+                for mg in range(MGS):
+                    v = raw[r % 4][t + r // 4, j, group(mg), :]
+                    row_at(field_b, r, t)[1, j, group(mg), :] = jnp.where(
+                        side, pltpu.roll(edge_b(j, 3, mg), turn, 1), v
+                    )
         return 0
 
-    lax.fori_loop(0, ROWS // 4 + 1, first_rows, 0)
+    lax.fori_loop(0, ROWS // 4 + 1, centre_rows, 0)
     for b in range(1, 4):
         put_row(field_b, b, 0, edge_b, keep_in(first, 0, max(b - 3, 0)))
 
@@ -620,17 +650,24 @@
 
     rows = ((ROWS // 4 + 2, 3, 3, MODES, COLS), F32)
     edge = (3, 5, MODES, COLS)
+    *u, coefs = call(
+        first_kernel,
+        [((ROWS // 4 + 2, 3, MODES, COLS), F32)] * 4 + [((ROWS + 8, QPAD, COLS), F32)],
+        [rows] * 4,
+        (20000000, 6000000),
+        start_modes, ct, ru, rd,
+    )
     wide = (ROWS + 8) * COLS
     x, q = call(
         iterate_kernel,
         [((3, 4 * MODES, wide), BF16), ((MODES, COLS), F32)],
         [rows] * 8 + [
-            ((ROWS + 8, QPAD, COLS), F32), (edge, F32), (edge, F32), ((3, MODES, COLS), F32), message,
+            (edge, F32), (edge, F32), ((3, MODES, COLS), F32), message,
             ((QPAD, COLS), F32), ((3,) + edge, F32), ((3, 2 * MODES, wide), BF16), ((32, ROWS * COLS), BF16),
             ((3, MODES, COLS), F32), ((3, MODES, COLS), F32), ((ROWS, COLS), F32), pltpu.SemaphoreType.DMA((1,)),
         ],
         (100000000, 20000000),
-        start_modes, ct, ru, rd, near, halo, left, right, node_mass, hbm=(8,), vmem=34,
+        *u, coefs, near, halo, left, right, node_mass, hbm=(9,), vmem=34,
     )
     q = sum_devices(q)
     modes, send, reduced, participation = call(

time: 112 us -> 109 us (0.973)
  waiting for transfers between devices: 22.3 us -> 18.4 us
  Pallas kernels: 31.3 us -> 32.9 us
  starting transfers between devices: 33.3 us -> 32.1 us
    ppermute x4, waiting for transfers between devices: 7.43 us -> 3.01 us  [shift(): lax.ppermute(x, axis, [(i, i + step) for i in range(n) if 0 <= i + step <...]
    pallas_call x6 -> x7, Pallas kernels: 31.3 us -> 32.9 us  [call(): pl.pallas_call(kernel, out_shape=[jax.ShapeDtypeStruct(s, d) for s, d in...]
    ppermute x11, starting transfers between devices: 20.5 us -> 19.3 us  [swap(): return lax.ppermute(x, axis, [(i, i ^ k) for i in range(n)])]
  transfers between devices with their start and end apart: 15 -> 15, of which waited for: 12 -> 10; matrix products, arithmetic and copies ran while one was open for 1% -> 1% of each run, Pallas kernels for 4% -> 9%
where the time goes in v5:
time: 109 us; the launch traced here: 108 us
  Pallas kernels  32.9 us (30%)
  starting transfers between devices  32.1 us (29%)
  blocking collectives  22.2 us (20%)
  waiting for transfers between devices  18.4 us (17%)
  local copies, waits for them, and re-layouts  1.89 us (2%)
    pallas_call x7, Pallas kernels, call(): pl.pallas_call(kernel, out_shape=[jax.ShapeDtypeStruct(s, d) for s, d in...  32.9 us
    all_to_all x1, blocking collectives, per_device(): recv = lax.all_to_all(send, 'node', 0, 0, tiled=True)  22.2 us
    ppermute x11, starting transfers between devices, swap(): return lax.ppermute(x, axis, [(i, i ^ k) for i in range(n)])  19.3 us
    ppermute x11, waiting for transfers between devices, swap(): return lax.ppermute(x, axis, [(i, i ^ k) for i in range(n)])  15.4 us
    ppermute x4, starting transfers between devices, shift(): lax.ppermute(x, axis, [(i, i + step) for i in range(n) if 0 <= i + step <...  12.8 us
    ppermute x4, waiting for transfers between devices, shift(): lax.ppermute(x, axis, [(i, i + step) for i in range(n) if 0 <= i + step <...  3.01 us
  transfers between devices with their start and end apart: 15, of which 10 were waited for; matrix products, arithmetic and copies ran while one was open for 1% of the time, Pallas kernels for 9%

profile of v5, /device:TPU:1, one launch (start us, length us, event | category | flops | bytes accessed | tf_op | source)
XLA Modules:
  0.0 108.4 jit_solution(3004594437740315222)
XLA Ops:
  0.7 2.4 %shard_map.101 = (f32[2,32,128]{2,1,0:T(8,128)}, f32[464,128]{1,0:T(8,128)}, f32[464,128]{1,0:T(8,128)}) custom-call(f32[3,32,32,128]{3,2,1,0:T(8,128)} %v_ref.3, f32[81,32,128]{2,1,0:T(8,128)} %bitcast.6, s32[32,128]{1,0:T(8,128)} %free_hbm.1, s32[32,128]{1,0:T(8,128)} %refs_2_.1, f32[64]{0:T(128)} %refs_3_.1), custom_call_target="tpu_custom_call" | custom-call | flops 1000000 | bytes 2000000 | tf_op jit(solution)/shard_map/pallas_call | solution.py:575
  3.0 6.0 %collective-permute-start = (f32[464,128]{1,0:T(8,128)}, f32[464,128]{1,0:T(8,128)S(1)}, u32[]{:S(2)}, u32[]{:S(2)}) collective-permute-start(f32[464,128]{1,0:T(8,128)} %get-tuple-element.26), channel_id=1, source_target_pairs={{0,32},{32,64},{64,96},{1,33},{33,65},{65,97},{2,34},{34,66},{66,9... | collective-permute-start | bytes 712712 | tf_op jit(solution)/shard_map/ppermute | solution.py:612
  9.1 1.9 %collective-permute-start.1 = (f32[464,128]{1,0:T(8,128)}, f32[464,128]{1,0:T(8,128)S(1)}, u32[]{:S(2)}, u32[]{:S(2)}) collective-permute-start(f32[464,128]{1,0:T(8,128)} %get-tuple-element.27), channel_id=1, source_target_pairs={{32,0},{64,32},{96,64},{33,1},{65,33},{97,65},{34,2},{66,34},{98,6... | collective-permute-start | bytes 712712 | tf_op jit(solution)/shard_map/ppermute | solution.py:612
  11.1 0.7 copy-done.4
  11.8 3.4 %shard_map.102 = (f32[32,88,128]{2,1,0:T(8,128)S(1)}, f32[2,184,128]{2,1,0:T(8,128)S(1)}) custom-call(f32[3,32,32,128]{3,2,1,0:T(8,128)S(1)} %copy-done, f32[81,32,128]{2,1,0:T(8,128)S(1)} %bitcast.7, f32[2,32,128]{2,1,0:T(8,128)S(1)} %copy-done.4), custom_call_target="tpu_custom_call" | custom-call | flops 10000000 | bytes 6000000 | tf_op jit(solution)/shard_map/pallas_call | solution.py:575
  15.2 3.0 %collective-permute-done.1.rd_ref = f32[464,128]{1,0:T(8,128)S(1)} collective-permute-done((f32[464,128]{1,0:T(8,128)}, f32[464,128]{1,0:T(8,128)S(1)}, u32[]{:S(2)}, u32[]{:S(2)}) %collective-permute-start.1) | collective-permute-done | bytes 237600 | tf_op jit(solution)/shard_map/ppermute | solution.py:612
  18.2 1.4 %shard_map.104 = (f32[232,128]{1,0:T(8,128)S(1)}, f32[232,128]{1,0:T(8,128)S(1)}, f32[184,128]{1,0:T(8,128)S(1)}) custom-call(f32[2,184,128]{2,1,0:T(8,128)S(1)} %get-tuple-element.33.near_ref, f32[464,128]{1,0:T(8,128)S(1)} %collective-permute-done.ru_ref, f32[464,128]{1,0:T(8,128)S(1)} %collective-permute-done.1.rd_ref), custom_call_target="tpu_custom_call" | custom-call | flops 1000000 | bytes 1500000 | tf_op jit(solution)/shard_map/pallas_call | solution.py:575
  19.6 3.5 %collective-permute-start.2 = (f32[232,128]{1,0:T(8,128)S(1)}, f32[232,128]{1,0:T(8,128)S(1)}, u32[]{:S(2)}, u32[]{:S(2)}) collective-permute-start(f32[232,128]{1,0:T(8,128)S(1)} %get-tuple-element.35), channel_id=1, source_target_pairs={{0,1},{1,2},{2,3},{3,4},{4,5},{5,6},{6,7},{7,8},{8,9},{9,10},{10,1... | collective-permute-start | bytes 356360 | tf_op jit(solution)/shard_map/ppermute | solution.py:612
  23.2 1.3 %collective-permute-start.3 = (f32[232,128]{1,0:T(8,128)S(1)}, f32[232,128]{1,0:T(8,128)S(1)}, u32[]{:S(2)}, u32[]{:S(2)}) collective-permute-start(f32[232,128]{1,0:T(8,128)S(1)} %get-tuple-element.36), channel_id=1, source_target_pairs={{1,0},{2,1},{3,2},{4,3},{5,4},{6,5},{7,6},{8,7},{9,8},{10,9},{11,1... | collective-permute-start | bytes 356360 | tf_op jit(solution)/shard_map/ppermute | solution.py:612
  24.5 5.2 %shard_map.103 = (f32[10,3,32,128]{3,2,1,0:T(8,128)S(1)}, f32[10,3,32,128]{3,2,1,0:T(8,128)S(1)}, f32[10,3,32,128]{3,2,1,0:T(8,128)S(1)}, f32[10,3,32,128]{3,2,1,0:T(8,128)S(1)}, f32[40,88,128]{2,1,0:T(8,128)S(1)}) custom-call(f32[3,32,32,128]{3,2,1,0:T(8,128)S(1)} %copy-done, f32[32,88,128]{2,1,0:T(8,128)S(1)} %get-tuple-element.25.ct_ref, ...), custom_call_target="tpu_custom_call" | custom-call | flops 20000000 | bytes 6000000 | tf_op jit(solution)/shard_map/pallas_call | solution.py:575
  29.7 13.1 %shard_map.105 = (bf16[3,128,5120]{2,1,0:T(8,128)(2,1)S(1)}, f32[32,128]{1,0:T(8,128)S(1)}) custom-call(f32[10,3,32,128]{3,2,1,0:T(8,128)S(1)} %get-tuple-element.28.u0, f32[10,3,32,128]{3,2,1,0:T(8,128)S(1)} %get-tuple-element.29.u1, f32[10,3,32,128]{3,2,1,0:T(8,128)S(1)} %get-tuple-element.30.u2, f32[10,3,32,128]{3,2,1,0:T(8,128)S(1)} %get-tuple-element.31.u3, ...), custom_call_target="tpu_custom_call" | custom-call | flops 100000000 | bytes 20000000 | tf_op jit(solution)/shard_map/pallas_call | solution.py:575
  42.9 1.2 %collective-permute-done.4 = f32[32,128]{1,0:T(8,128)S(1)} collective-permute-done((f32[32,128]{1,0:T(8,128)S(1)}, f32[32,128]{1,0:T(8,128)S(1)}, u32[]{:S(2)}, u32[]{:S(2)}) %collective-permute-start.4) | collective-permute-done | bytes 16416 | tf_op jit(solution)/shard_map/ppermute | solution.py:591
  44.1 4.2 %collective-permute-start.7 = (f32[32,128]{1,0:T(8,128)S(1)}, f32[32,128]{1,0:T(8,128)S(1)}, u32[]{:S(2)}, u32[]{:S(2)}) collective-permute-start(f32[32,128]{1,0:T(8,128)S(1)} %add.33), channel_id=1, source_target_pairs={{0,3},{1,2},{2,1},{3,0},{4,7},{5,6},{6,5},{7,4},{8,11},{9,10},{10,... | collective-permute-start | bytes 49160 | tf_op jit(solution)/shard_map/ppermute | solution.py:591
  48.3 0.7 collective-permute-start.5
  49.0 0.5 collective-permute-done.7
  49.4 3.0 %collective-permute-done.6 = f32[32,128]{1,0:T(8,128)S(1)} collective-permute-done((f32[32,128]{1,0:T(8,128)S(1)}, f32[32,128]{1,0:T(8,128)S(1)}, u32[]{:S(2)}, u32[]{:S(2)}) %collective-permute-start.6) | collective-permute-done | bytes 16416 | tf_op jit(solution)/shard_map/ppermute | solution.py:591
  52.4 4.0 %collective-permute-start.10 = (f32[32,128]{1,0:T(8,128)S(1)}, f32[32,128]{1,0:T(8,128)S(1)}, u32[]{:S(2)}, u32[]{:S(2)}) collective-permute-start(f32[32,128]{1,0:T(8,128)S(1)} %add_add_fusion.1), channel_id=1, source_target_pairs={{0,12},{1,13},{2,14},{3,15},{4,8},{5,9},{6,10},{7,11},{8,4},{9,5},... | collective-permute-start | bytes 49160 | tf_op jit(solution)/shard_map/ppermute | solution.py:591
  56.4 0.7 collective-permute-start.8
  57.1 0.5 collective-permute-done.10
  57.5 3.0 %collective-permute-done.9 = f32[32,128]{1,0:T(8,128)S(1)} collective-permute-done((f32[32,128]{1,0:T(8,128)S(1)}, f32[32,128]{1,0:T(8,128)S(1)}, u32[]{:S(2)}, u32[]{:S(2)}) %collective-permute-start.9) | collective-permute-done | bytes 16416 | tf_op jit(solution)/shard_map/ppermute | solution.py:591
  60.6 2.6 %collective-permute-done.11 = f32[32,128]{1,0:T(8,128)S(1)} collective-permute-done((f32[32,128]{1,0:T(8,128)S(1)}, f32[32,128]{1,0:T(8,128)S(1)}, u32[]{:S(2)}, u32[]{:S(2)}) %collective-permute-start.11) | collective-permute-done | bytes 16416 | tf_op jit(solution)/shard_map/ppermute | solution.py:591
  63.2 1.3 %collective-permute-start.12 = (f32[32,128]{1,0:T(8,128)S(1)}, f32[32,128]{1,0:T(8,128)S(1)}, u32[]{:S(2)}, u32[]{:S(2)}) collective-permute-start(f32[32,128]{1,0:T(8,128)S(1)} %add.40), channel_id=1, source_target_pairs={{0,64},{32,96},{64,0},{96,32},{1,65},{33,97},{65,1},{97,33},{2,66}... | collective-permute-start | bytes 49160 | tf_op jit(solution)/shard_map/ppermute | solution.py:591
  64.5 2.8 %collective-permute-done.12 = f32[32,128]{1,0:T(8,128)S(1)} collective-permute-done((f32[32,128]{1,0:T(8,128)S(1)}, f32[32,128]{1,0:T(8,128)S(1)}, u32[]{:S(2)}, u32[]{:S(2)}) %collective-permute-start.12) | collective-permute-done | bytes 16416 | tf_op jit(solution)/shard_map/ppermute | solution.py:591
  67.3 6.1 %shard_map.106 = (f32[3,32,32,128]{3,2,1,0:T(8,128)}, f32[32,104,128]{2,1,0:T(8,128)S(1)}, f32[32,32]{1,0:T(8,128)}, f32[6,1]{1,0:T(8,128)S(1)}) custom-call(f32[32,128]{1,0:T(8,128)S(1)} %add.41.refs_0_, bf16[3,128,5120]{2,1,0:T(8,128)(2,1)S(1)} %get-tuple-element.38.refs_1_, s32[32,128]{1,0:T(8,128)S(1)} %copy-done.3, f32[64]{0:T(128)S(1)} %copy-done.5), custom_call_target="tpu_custom_call" | custom-call | flops 10000000 | bytes 10000000 | tf_op jit(solution)/shard_map/pallas_call | solution.py:575
  73.4 22.2 %all_to_all.5.refs_0_ = f32[32,104,128]{2,1,0:T(8,128)S(1)} all-to-all(f32[32,104,128]{2,1,0:T(8,128)S(1)} %get-tuple-element.40), channel_id=1, replica_groups=mesh['region'=4,'node'=32] {'node'}, dimensions={0} | all-to-all | bytes 3407872 | tf_op jit(solution)/shard_map/all_to_all | solution.py:683
  95.6 7.4 %collective-permute-start.13 = (f32[8,128]{1,0:T(8,128)S(1)}, f32[8,128]{1,0:T(8,128)S(1)}, u32[]{:S(2)}, u32[]{:S(2)}) collective-permute-start(f32[8,128]{1,0:T(8,128)S(1)} %slice_reduce_fusion), channel_id=1, source_target_pairs={{0,32},{32,0},{64,96},{96,64},{1,33},{33,1},{65,97},{97,65},{2,34}... | collective-permute-start | bytes 12296 | tf_op jit(solution)/shard_map/ppermute | solution.py:591
  103.0 0.8 collective-permute-done.13
  103.9 0.9 collective-permute-start.14
  104.7 0.6 copy.12
  105.3 1.3 %shard_map.107 = f32[3,32,4096]{2,1,0:T(8,128)} custom-call(f32[32,104,128]{2,1,0:T(8,128)S(1)} %all_to_all.5.refs_0_), custom_call_target="tpu_custom_call" | custom-call | flops 10000 | bytes 6000000 | tf_op jit(solution)/shard_map/pallas_call | solution.py:575
  106.6 1.2 %collective-permute-done.14 = f32[8,128]{1,0:T(8,128)S(1)} collective-permute-done((f32[8,128]{1,0:T(8,128)S(1)}, f32[8,128]{1,0:T(8,128)S(1)}, u32[]{:S(2)}, u32[]{:S(2)}) %collective-permute-start.14) | collective-permute-done | bytes 4128 | tf_op jit(solution)/shard_map/ppermute | solution.py:591
  107.8 0.5 slice_bitcast_fusion
  (28 shorter events, 0.3 us)
Async XLA Ops:
  0.6 10.4 %copy-start = (f32[3,32,32,128]{3,2,1,0:T(8,128)S(1)}, f32[3,32,32,128]{3,2,1,0:T(8,128)}, u32[]{:S(2)}) copy-start(f32[3,32,32,128]{3,2,1,0:T(8,128)} %v_ref.3) | copy-start | bytes 4718596
  0.6 10.4 %copy-start.1 = (f32[9,3,3,32,128]{4,3,2,1,0:T(8,128)S(1)}, f32[9,3,3,32,128]{4,3,2,1,0:T(8,128)}, u32[]{:S(2)}) copy-start(f32[9,3,3,32,128]{4,3,2,1,0:T(8,128)} %param.7) | copy-start | bytes 3981316
  3.0 12.2 %collective-permute-start = (f32[464,128]{1,0:T(8,128)}, f32[464,128]{1,0:T(8,128)S(1)}, u32[]{:S(2)}, u32[]{:S(2)}) collective-permute-start(f32[464,128]{1,0:T(8,128)} %get-tuple-element.26), channel_id=1, source_target_pairs={{0,32},{32,64},{64,96},{1,33},{33,65},{65,97},{2,34},{34,66},{66,9... | collective-permute-start | bytes 712712 | tf_op jit(solution)/shard_map/ppermute | solution.py:612
  9.1 9.1 %collective-permute-start.1 = (f32[464,128]{1,0:T(8,128)}, f32[464,128]{1,0:T(8,128)S(1)}, u32[]{:S(2)}, u32[]{:S(2)}) collective-permute-start(f32[464,128]{1,0:T(8,128)} %get-tuple-element.27), channel_id=1, source_target_pairs={{32,0},{64,32},{96,64},{33,1},{65,33},{97,65},{34,2},{66,34},{98,6... | collective-permute-start | bytes 712712 | tf_op jit(solution)/shard_map/ppermute | solution.py:612
  11.0 0.8 copy-start.4
  19.6 10.1 %collective-permute-start.2 = (f32[232,128]{1,0:T(8,128)S(1)}, f32[232,128]{1,0:T(8,128)S(1)}, u32[]{:S(2)}, u32[]{:S(2)}) collective-permute-start(f32[232,128]{1,0:T(8,128)S(1)} %get-tuple-element.35), channel_id=1, source_target_pairs={{0,1},{1,2},{2,3},{3,4},{4,5},{5,6},{6,7},{7,8},{8,9},{9,10},{10,1... | collective-permute-start | bytes 356360 | tf_op jit(solution)/shard_map/ppermute | solution.py:612
  23.2 6.5 %collective-permute-start.3 = (f32[232,128]{1,0:T(8,128)S(1)}, f32[232,128]{1,0:T(8,128)S(1)}, u32[]{:S(2)}, u32[]{:S(2)}) collective-permute-start(f32[232,128]{1,0:T(8,128)S(1)} %get-tuple-element.36), channel_id=1, source_target_pairs={{1,0},{2,1},{3,2},{4,3},{5,4},{6,5},{7,6},{8,7},{9,8},{10,9},{11,1... | collective-permute-start | bytes 356360 | tf_op jit(solution)/shard_map/ppermute | solution.py:612
  24.5 5.2 %copy-start.2 = (f32[32,4096]{1,0:T(8,128)S(1)}, f32[32,4096]{1,0:T(8,128)}, u32[]{:S(2)}) copy-start(f32[32,4096]{1,0:T(8,128)} %mass_hbm.1) | copy-start | bytes 1572868
  29.7 37.6 %copy-start.3 = (s32[32,128]{1,0:T(8,128)S(1)}, s32[32,128]{1,0:T(8,128)}, u32[]{:S(2)}) copy-start(s32[32,128]{1,0:T(8,128)} %refs_2_.1) | copy-start | bytes 49156
  29.7 37.6 %copy-start.5 = (f32[64]{0:T(128)S(1)}, f32[64]{0:T(128)}, u32[]{:S(2)}) copy-start(f32[64]{0:T(128)} %refs_3_.1) | copy-start | bytes 772
  42.8 1.3 %collective-permute-start.4 = (f32[32,128]{1,0:T(8,128)S(1)}, f32[32,128]{1,0:T(8,128)S(1)}, u32[]{:S(2)}, u32[]{:S(2)}) collective-permute-start(f32[32,128]{1,0:T(8,128)S(1)} %get-tuple-element.37), channel_id=1, source_target_pairs={{0,32},{32,0},{64,96},{96,64},{1,33},{33,1},{65,97},{97,65},{2,34}... | collective-permute-start | bytes 49160 | tf_op jit(solution)/shard_map/ppermute | solution.py:591
  44.1 5.3 %collective-permute-start.7 = (f32[32,128]{1,0:T(8,128)S(1)}, f32[32,128]{1,0:T(8,128)S(1)}, u32[]{:S(2)}, u32[]{:S(2)}) collective-permute-start(f32[32,128]{1,0:T(8,128)S(1)} %add.33), channel_id=1, source_target_pairs={{0,3},{1,2},{2,1},{3,0},{4,7},{5,6},{6,5},{7,4},{8,11},{9,10},{10,... | collective-permute-start | bytes 49160 | tf_op jit(solution)/shard_map/ppermute | solution.py:591
  48.3 4.1 %collective-permute-start.6 = (f32[32,128]{1,0:T(8,128)S(1)}, f32[32,128]{1,0:T(8,128)S(1)}, u32[]{:S(2)}, u32[]{:S(2)}) collective-permute-start(f32[32,128]{1,0:T(8,128)S(1)} %add.33), channel_id=1, source_target_pairs={{0,2},{1,3},{2,0},{3,1},{4,6},{5,7},{6,4},{7,5},{8,10},{9,11},{10,... | collective-permute-start | bytes 49160 | tf_op jit(solution)/shard_map/ppermute | solution.py:591
  48.3 4.1 %collective-permute-start.5 = (f32[32,128]{1,0:T(8,128)S(1)}, f32[32,128]{1,0:T(8,128)S(1)}, u32[]{:S(2)}, u32[]{:S(2)}) collective-permute-start(f32[32,128]{1,0:T(8,128)S(1)} %add.33), channel_id=1, source_target_pairs={{0,1},{1,0},{2,3},{3,2},{4,5},{5,4},{6,7},{7,6},{8,9},{9,8},{10,11... | collective-permute-start | bytes 49160 | tf_op jit(solution)/shard_map/ppermute | solution.py:591
  52.4 5.1 %collective-permute-start.10 = (f32[32,128]{1,0:T(8,128)S(1)}, f32[32,128]{1,0:T(8,128)S(1)}, u32[]{:S(2)}, u32[]{:S(2)}) collective-permute-start(f32[32,128]{1,0:T(8,128)S(1)} %add_add_fusion.1), channel_id=1, source_target_pairs={{0,12},{1,13},{2,14},{3,15},{4,8},{5,9},{6,10},{7,11},{8,4},{9,5},... | collective-permute-start | bytes 49160 | tf_op jit(solution)/shard_map/ppermute | solution.py:591
  56.4 4.1 %collective-permute-start.9 = (f32[32,128]{1,0:T(8,128)S(1)}, f32[32,128]{1,0:T(8,128)S(1)}, u32[]{:S(2)}, u32[]{:S(2)}) collective-permute-start(f32[32,128]{1,0:T(8,128)S(1)} %add_add_fusion.1), channel_id=1, source_target_pairs={{0,8},{1,9},{2,10},{3,11},{4,12},{5,13},{6,14},{7,15},{8,0},{9,1},... | collective-permute-start | bytes 49160 | tf_op jit(solution)/shard_map/ppermute | solution.py:591
  56.4 4.1 %collective-permute-start.8 = (f32[32,128]{1,0:T(8,128)S(1)}, f32[32,128]{1,0:T(8,128)S(1)}, u32[]{:S(2)}, u32[]{:S(2)}) collective-permute-start(f32[32,128]{1,0:T(8,128)S(1)} %add_add_fusion.1), channel_id=1, source_target_pairs={{0,4},{1,5},{2,6},{3,7},{4,0},{5,1},{6,2},{7,3},{8,12},{9,13},{10,... | collective-permute-start | bytes 49160 | tf_op jit(solution)/shard_map/ppermute | solution.py:591
  60.5 2.7 %collective-permute-start.11 = (f32[32,128]{1,0:T(8,128)S(1)}, f32[32,128]{1,0:T(8,128)S(1)}, u32[]{:S(2)}, u32[]{:S(2)}) collective-permute-start(f32[32,128]{1,0:T(8,128)S(1)} %add_add_fusion), channel_id=1, source_target_pairs={{0,16},{1,17},{2,18},{3,19},{4,20},{5,21},{6,22},{7,23},{8,24},{9,... | collective-permute-start | bytes 49160 | tf_op jit(solution)/shard_map/ppermute | solution.py:591
  63.2 4.1 %collective-permute-start.12 = (f32[32,128]{1,0:T(8,128)S(1)}, f32[32,128]{1,0:T(8,128)S(1)}, u32[]{:S(2)}, u32[]{:S(2)}) collective-permute-start(f32[32,128]{1,0:T(8,128)S(1)} %add.40), channel_id=1, source_target_pairs={{0,64},{32,96},{64,0},{96,32},{1,65},{33,97},{65,1},{97,33},{2,66}... | collective-permute-start | bytes 49160 | tf_op jit(solution)/shard_map/ppermute | solution.py:591
  95.6 8.2 %collective-permute-start.13 = (f32[8,128]{1,0:T(8,128)S(1)}, f32[8,128]{1,0:T(8,128)S(1)}, u32[]{:S(2)}, u32[]{:S(2)}) collective-permute-start(f32[8,128]{1,0:T(8,128)S(1)} %slice_reduce_fusion), channel_id=1, source_target_pairs={{0,32},{32,0},{64,96},{96,64},{1,33},{33,1},{65,97},{97,65},{2,34}... | collective-permute-start | bytes 12296 | tf_op jit(solution)/shard_map/ppermute | solution.py:591
  103.9 4.0 %collective-permute-start.14 = (f32[8,128]{1,0:T(8,128)S(1)}, f32[8,128]{1,0:T(8,128)S(1)}, u32[]{:S(2)}, u32[]{:S(2)}) collective-permute-start(f32[8,128]{1,0:T(8,128)S(1)} %add.42), channel_id=1, source_target_pairs={{0,64},{32,96},{64,0},{96,32},{1,65},{33,97},{65,1},{97,33},{2,66}... | collective-permute-start | bytes 12296 | tf_op jit(solution)/shard_map/ppermute | solution.py:591

commit v6 on v5

--- a/solution.py
+++ b/solution.py
@@ -14,6 +14,7 @@
 MGS = MODES // 8
 EXTRA = 8
 PIECE = 3 * ROWS + EXTRA
+SPREAD_LIMIT = 64.0
 
 
 def lane_of(shape=(8, COLS)):
@@ -501,11 +502,16 @@
     return lax.dot_general(a, b, dims, precision=lax.Precision.HIGHEST, preferred_element_type=F32)
 
 
-def combine_kernel(nodes, q_ref, x_ref, gid_ref, design_ref, modes_hbm, send_ref, reduced_ref, part_ref, weight, bins, modes_ref, column, factor, sems):
+def combine_kernel(nodes, q_ref, x_ref, gid_ref, design_ref, modes_hbm, send_ref, reduced_ref, part_ref, bad_ref, weight, bins, modes_ref, column, factor, sems):
     q = q_ref[...]
     w1 = inverse_factor(q[:, 0:32], column, factor)
     gram = nodes * product(product(w1, q[:, 32:64]), w1, True)
     w = nodes * product(inverse_factor(gram, column, factor), w1)
+    same = lax.broadcasted_iota(jnp.int32, gram.shape, 0) == lax.broadcasted_iota(jnp.int32, gram.shape, 1)
+    norms = jnp.sum(jnp.where(same, q[:, 32:64], 0.0), axis=0, keepdims=True)
+    spread = norms * jnp.sum(w * w, axis=0, keepdims=True) / nodes
+    bad = jnp.sum(jnp.where(spread < SPREAD_LIMIT, 0.0, 1.0), axis=1, keepdims=True)
+    bad_ref[...] = jnp.broadcast_to(bad, (8, COLS))
     reduced_ref[...] = product(product(w, q[:, 64:96]), w, True) / nodes
     s = lax.dot_general(
         q[:, 96:112], w, (((0,), (1,)), ((), ())), precision=lax.Precision.HIGHEST, preferred_element_type=F32
@@ -612,6 +618,104 @@
     return lax.ppermute(x, axis, [(i, i + step) for i in range(n) if 0 <= i + step < n])
 
 
+ITERS = 2
+HIGH = lax.Precision.HIGHEST
+
+
+def with_halo(array, sides, width):
+    for axis, dim in sides:
+        size, length = (lax.axis_size(axis), array.shape[dim])
+        up = [(i, (i + 1) % size) for i in range(size - 1)]
+        down = [(j, i) for i, j in up]
+        last = lax.slice_in_dim(array, length - width, length, axis=dim)
+        initial = lax.slice_in_dim(array, 0, width, axis=dim)
+        before = lax.ppermute(last, axis, up)
+        after = lax.ppermute(initial, axis, down)
+        array = jnp.concatenate([before, array, after], axis=dim)
+    return array
+
+
+def apply_operator(field, tiles, scale):
+    padded = with_halo(field, (("region", 2), ("node", 3)), 1)
+    rows = field.shape[2]
+    cols = field.shape[3]
+    parts = []
+    for i in range(3):
+        total = jnp.zeros(field.shape[1:], jnp.float32)
+        for s in range(9):
+            step_x = s // 3 - 1
+            step_y = s % 3 - 1
+            beside = padded[:, :, 1 + step_x : 1 + step_x + rows, 1 + step_y : 1 + step_y + cols]
+            for j in range(3):
+                total = total + tiles[s, i, j][None] * beside[j]
+        parts.append(total)
+    return jnp.stack(parts) * scale[None, None]
+
+
+def plain_inverse_factor(gram, width):
+    lower = jnp.linalg.cholesky(gram)
+    return jax.scipy.linalg.solve_triangular(lower, jnp.eye(width, dtype=jnp.float32), lower=True)
+
+
+def combine_modes(inverse, block, root):
+    return root * jnp.einsum("km,imxy->ikxy", inverse, block, precision=HIGH)
+
+
+def invariants(modes, mass, pos_x, pos_y):
+    weighted = modes * mass[None, None]
+    part_t = jnp.sum(weighted, axis=(2, 3))
+    rot_x = jnp.sum(weighted[2] * pos_y[None, None, :], axis=(1, 2))
+    rot_y = -jnp.sum(weighted[2] * pos_x[None, :, None], axis=(1, 2))
+    rot_z = jnp.sum(
+        weighted[1] * pos_x[None, :, None] - weighted[0] * pos_y[None, None, :], axis=(1, 2)
+    )
+    return jnp.concatenate([part_t, jnp.stack([rot_x, rot_y, rot_z])], axis=0)
+
+
+def step_by_step(start_modes, stiffness_tiles, free_mask, group_ids, design, node_mass):
+    rows = start_modes.shape[2]
+    cols = start_modes.shape[3]
+    width = start_modes.shape[1]
+    groups = design.shape[0]
+    regions = lax.axis_size("region")
+    columns = lax.axis_size("node")
+    total_x = rows * regions
+    total_y = cols * columns
+    nodes = jnp.float32(total_x * total_y)
+    root = jnp.sqrt(nodes)
+    freedom = free_mask.astype(jnp.float32)
+    onehot = (group_ids[None] == jnp.arange(groups, dtype=jnp.int32)[:, None, None]).astype(
+        jnp.float32
+    )
+    factor = jnp.sum(onehot * design[:, None, None], axis=0)
+    scale = freedom * factor
+    modes = start_modes
+    for step in range(ITERS):
+        iterated = 16.0 * freedom[None, None] * modes - apply_operator(
+            modes, stiffness_tiles, scale
+        )
+        gram_local = jnp.einsum("imxy,ikxy->mk", iterated, iterated, precision=HIGH)
+        gram = sum_devices(gram_local)
+        inverse = plain_inverse_factor(gram, width)
+        modes = combine_modes(inverse, iterated, root)
+    image = apply_operator(modes, stiffness_tiles, scale)
+    weight = jnp.sum(modes * image, axis=(0, 1)) / factor
+    reduced_local = jnp.einsum("imxy,ikxy->mk", modes, image, precision=HIGH)
+    reduced_sum = sum_devices(reduced_local)
+    adjoint_sum = sum_devices(jnp.sum(onehot * weight[None], axis=(1, 2)))
+    reduced = reduced_sum / nodes
+    adjoint = adjoint_sum / nodes
+    by_column = lax.all_to_all(modes, "node", split_axis=1, concat_axis=3, tiled=True)
+    start_x = lax.axis_index("region") * rows
+    pos_x = (
+        2.0 * ((start_x + jnp.arange(rows, dtype=jnp.int32)).astype(jnp.float32) + 0.5) / total_x
+        - 1.0
+    )
+    pos_y = 2.0 * (jnp.arange(total_y, dtype=jnp.int32).astype(jnp.float32) + 0.5) / total_y - 1.0
+    participation = sum_group(invariants(by_column, node_mass, pos_x, pos_y), "region", (1, 2)) / root
+    return (modes, by_column, reduced, participation, adjoint)
+
+
 def per_device(start_modes, stiffness_tiles, free_mask, group_ids, design, node_mass):
     regions = lax.axis_size("region")
     columns = lax.axis_size("node")
@@ -670,9 +774,9 @@
         *u, coefs, near, halo, left, right, node_mass, hbm=(9,), vmem=34,
     )
     q = sum_devices(q)
-    modes, send, reduced, participation = call(
+    modes, send, reduced, participation, bad = call(
         lambda *refs: combine_kernel(nodes, *refs),
-        [((3, MODES, ROWS, COLS), F32), ((MODES, PIECE, COLS), F32), ((MODES, MODES), F32), ((6, 1), F32)],
+        [((3, MODES, ROWS, COLS), F32), ((MODES, PIECE, COLS), F32), ((MODES, MODES), F32), ((6, 1), F32), ((8, COLS), F32)],
         [
             ((ROWS, COLS), F32), ((GROUPS, COLS), F32), ((3, MODES, ROWS, COLS), F32),
             ((2, MODES, COLS), F32), ((MODES, COLS), F32), pltpu.SemaphoreType.DMA((ROWS // 8,)),
@@ -687,7 +791,9 @@
     )
     extra = sum_group(sum_group(extra, "region", (1,)), "region", (2,))
     adjoint = extra[0, :GROUPS]
-    return (modes, by_column[:, None], reduced, participation, adjoint)
+    inputs = (start_modes, stiffness_tiles, free_mask, group_ids, design, node_mass)
+    results = (modes, by_column[:, None], reduced, participation, adjoint)
+    return lax.cond(bad[0, 0] == 0.0, lambda done, _: done, lambda _, given: step_by_step(*given), results, inputs)
 
 
 def solution(mesh):

time: 109 us -> 112 us (1.028)
  transfers between devices with their start and end apart: 15 -> 15, of which waited for: 10 -> 10; matrix products, arithmetic and copies ran while one was open for 1% -> 0% of each run, Pallas kernels for 9% -> 9%
where the time goes in v6:
time: 112 us; the launch traced here: 111 us
  Pallas kernels  33 us (29%)
  starting transfers between devices  32.9 us (29%)
  blocking collectives  22.1 us (20%)
  waiting for transfers between devices  19.3 us (17%)
  local copies, waits for them, and re-layouts  2.57 us (2%)
  between operations  1.49 us (1%)
    pallas_call x7, Pallas kernels, call(): pl.pallas_call(kernel, out_shape=[jax.ShapeDtypeStruct(s, d) for s, d in...  33 us
    all_to_all x1, blocking collectives, per_device(): recv = lax.all_to_all(send, 'node', 0, 0, tiled=True)  22.1 us
    ppermute x11, starting transfers between devices, swap(): return lax.ppermute(x, axis, [(i, i ^ k) for i in range(n)])  20.1 us
    ppermute x11, waiting for transfers between devices, swap(): return lax.ppermute(x, axis, [(i, i ^ k) for i in range(n)])  16.2 us
    ppermute x4, starting transfers between devices, shift(): lax.ppermute(x, axis, [(i, i + step) for i in range(n) if 0 <= i + step <...  12.8 us
    ppermute x4, waiting for transfers between devices, shift(): lax.ppermute(x, axis, [(i, i + step) for i in range(n) if 0 <= i + step <...  3.01 us
  transfers between devices with their start and end apart: 15, of which 10 were waited for; matrix products, arithmetic and copies ran while one was open for 0% of the time, Pallas kernels for 9%

profile of v6, /device:TPU:1, one launch (start us, length us, event | category | flops | bytes accessed | tf_op | source)
XLA Modules:
  0.0 111.4 jit_solution(11846492253723839970)
XLA Ops:
  0.7 2.4 %shard_map.109 = (f32[2,32,128]{2,1,0:T(8,128)}, f32[464,128]{1,0:T(8,128)}, f32[464,128]{1,0:T(8,128)}) custom-call(f32[3,32,32,128]{3,2,1,0:T(8,128)} %v_ref.3, f32[81,32,128]{2,1,0:T(8,128)} %bitcast.258, s32[32,128]{1,0:T(8,128)} %free_hbm.1, s32[32,128]{1,0:T(8,128)} %refs_2_.1, f32[64]{0:T(128)} %refs_3_.1), custom_call_target="tpu_custom_call" | custom-call | flops 1000000 | bytes 2000000 | tf_op jit(solution)/shard_map/pallas_call | solution.py:581
  3.0 6.0 %collective-permute-start.51 = (f32[464,128]{1,0:T(8,128)}, f32[464,128]{1,0:T(8,128)S(1)}, u32[]{:S(2)}, u32[]{:S(2)}) collective-permute-start(f32[464,128]{1,0:T(8,128)} %get-tuple-element.74), channel_id=1, source_target_pairs={{0,32},{32,64},{64,96},{1,33},{33,65},{65,97},{2,34},{34,66},{66,9... | collective-permute-start | bytes 712712 | tf_op jit(solution)/shard_map/ppermute | solution.py:618
  9.1 1.9 %collective-permute-start.52 = (f32[464,128]{1,0:T(8,128)}, f32[464,128]{1,0:T(8,128)S(1)}, u32[]{:S(2)}, u32[]{:S(2)}) collective-permute-start(f32[464,128]{1,0:T(8,128)} %get-tuple-element.75), channel_id=1, source_target_pairs={{32,0},{64,32},{96,64},{33,1},{65,33},{97,65},{34,2},{66,34},{98,6... | collective-permute-start | bytes 712712 | tf_op jit(solution)/shard_map/ppermute | solution.py:618
  11.1 0.7 copy-done
  11.8 3.4 %shard_map.110 = (f32[32,88,128]{2,1,0:T(8,128)S(1)}, f32[2,184,128]{2,1,0:T(8,128)S(1)}) custom-call(f32[3,32,32,128]{3,2,1,0:T(8,128)S(1)} %copy-done.1, f32[81,32,128]{2,1,0:T(8,128)S(1)} %bitcast.259, f32[2,32,128]{2,1,0:T(8,128)S(1)} %copy-done), custom_call_target="tpu_custom_call" | custom-call | flops 10000000 | bytes 6000000 | tf_op jit(solution)/shard_map/pallas_call | solution.py:581
  15.2 3.0 %collective-permute-done.52.rd_ref = f32[464,128]{1,0:T(8,128)S(1)} collective-permute-done((f32[464,128]{1,0:T(8,128)}, f32[464,128]{1,0:T(8,128)S(1)}, u32[]{:S(2)}, u32[]{:S(2)}) %collective-permute-start.52) | collective-permute-done | bytes 237600 | tf_op jit(solution)/shard_map/ppermute | solution.py:618
  18.2 1.4 %shard_map.112 = (f32[232,128]{1,0:T(8,128)S(1)}, f32[232,128]{1,0:T(8,128)S(1)}, f32[184,128]{1,0:T(8,128)S(1)}) custom-call(f32[2,184,128]{2,1,0:T(8,128)S(1)} %get-tuple-element.81.near_ref, f32[464,128]{1,0:T(8,128)S(1)} %collective-permute-done.51.ru_ref, f32[464,128]{1,0:T(8,128)S(1)} %collective-permute-done.52.rd_ref), custom_call_target="tpu_custom_call" | custom-call | flops 1000000 | bytes 1500000 | tf_op jit(solution)/shard_map/pallas_call | solution.py:581
  19.6 3.5 %collective-permute-start.53 = (f32[232,128]{1,0:T(8,128)S(1)}, f32[232,128]{1,0:T(8,128)S(1)}, u32[]{:S(2)}, u32[]{:S(2)}) collective-permute-start(f32[232,128]{1,0:T(8,128)S(1)} %get-tuple-element.83), channel_id=1, source_target_pairs={{0,1},{1,2},{2,3},{3,4},{4,5},{5,6},{6,7},{7,8},{8,9},{9,10},{10,1... | collective-permute-start | bytes 356360 | tf_op jit(solution)/shard_map/ppermute | solution.py:618
  23.2 1.3 %collective-permute-start.54 = (f32[232,128]{1,0:T(8,128)S(1)}, f32[232,128]{1,0:T(8,128)S(1)}, u32[]{:S(2)}, u32[]{:S(2)}) collective-permute-start(f32[232,128]{1,0:T(8,128)S(1)} %get-tuple-element.84), channel_id=1, source_target_pairs={{1,0},{2,1},{3,2},{4,3},{5,4},{6,5},{7,6},{8,7},{9,8},{10,9},{11,1... | collective-permute-start | bytes 356360 | tf_op jit(solution)/shard_map/ppermute | solution.py:618
  24.5 5.2 %shard_map.111 = (f32[10,3,32,128]{3,2,1,0:T(8,128)S(1)}, f32[10,3,32,128]{3,2,1,0:T(8,128)S(1)}, f32[10,3,32,128]{3,2,1,0:T(8,128)S(1)}, f32[10,3,32,128]{3,2,1,0:T(8,128)S(1)}, f32[40,88,128]{2,1,0:T(8,128)S(1)}) custom-call(f32[3,32,32,128]{3,2,1,0:T(8,128)S(1)} %copy-done.1, f32[32,88,128]{2,1,0:T(8,128)S(1)} %get-tuple-element.73.ct_ref, ...), custom_call_target="tpu_custom_call" | custom-call | flops 20000000 | bytes 6000000 | tf_op jit(solution)/shard_map/pallas_call | solution.py:581
  29.7 13.1 %shard_map.113 = (bf16[3,128,5120]{2,1,0:T(8,128)(2,1)S(1)}, f32[32,128]{1,0:T(8,128)S(1)}) custom-call(f32[10,3,32,128]{3,2,1,0:T(8,128)S(1)} %get-tuple-element.76.u0, f32[10,3,32,128]{3,2,1,0:T(8,128)S(1)} %get-tuple-element.77.u1, f32[10,3,32,128]{3,2,1,0:T(8,128)S(1)} %get-tuple-element.78.u2, f32[10,3,32,128]{3,2,1,0:T(8,128)S(1)} %get-tuple-element.79.u3, ...), custom_call_target="tpu_custom_call" | custom-call | flops 100000000 | bytes 20000000 | tf_op jit(solution)/shard_map/pallas_call | solution.py:581
  43.0 1.2 %collective-permute-done.55 = f32[32,128]{1,0:T(8,128)S(1)} collective-permute-done((f32[32,128]{1,0:T(8,128)S(1)}, f32[32,128]{1,0:T(8,128)S(1)}, u32[]{:S(2)}, u32[]{:S(2)}) %collective-permute-start.55) | collective-permute-done | bytes 16416 | tf_op jit(solution)/shard_map/ppermute | solution.py:597
  44.1 2.3 %collective-permute-start.56 = (f32[32,128]{1,0:T(8,128)S(1)}, f32[32,128]{1,0:T(8,128)S(1)}, u32[]{:S(2)}, u32[]{:S(2)}) collective-permute-start(f32[32,128]{1,0:T(8,128)S(1)} %add.1132), channel_id=1, source_target_pairs={{0,1},{1,0},{2,3},{3,2},{4,5},{5,4},{6,7},{7,6},{8,9},{9,8},{10,11... | collective-permute-start | bytes 49160 | tf_op jit(solution)/shard_map/ppermute | solution.py:597
  46.4 3.1 %collective-permute-start.57 = (f32[32,128]{1,0:T(8,128)S(1)}, f32[32,128]{1,0:T(8,128)S(1)}, u32[]{:S(2)}, u32[]{:S(2)}) collective-permute-start(f32[32,128]{1,0:T(8,128)S(1)} %add.1132), channel_id=1, source_target_pairs={{0,2},{1,3},{2,0},{3,1},{4,6},{5,7},{6,4},{7,5},{8,10},{9,11},{10,... | collective-permute-start | bytes 49160 | tf_op jit(solution)/shard_map/ppermute | solution.py:597
  49.5 1.3 %collective-permute-done.57 = f32[32,128]{1,0:T(8,128)S(1)} collective-permute-done((f32[32,128]{1,0:T(8,128)S(1)}, f32[32,128]{1,0:T(8,128)S(1)}, u32[]{:S(2)}, u32[]{:S(2)}) %collective-permute-start.57) | collective-permute-done | bytes 16416 | tf_op jit(solution)/shard_map/ppermute | solution.py:597
  50.8 2.5 %collective-permute-done.58 = f32[32,128]{1,0:T(8,128)S(1)} collective-permute-done((f32[32,128]{1,0:T(8,128)S(1)}, f32[32,128]{1,0:T(8,128)S(1)}, u32[]{:S(2)}, u32[]{:S(2)}) %collective-permute-start.58) | collective-permute-done | bytes 16416 | tf_op jit(solution)/shard_map/ppermute | solution.py:597
  53.3 1.4 %collective-permute-start.59 = (f32[32,128]{1,0:T(8,128)S(1)}, f32[32,128]{1,0:T(8,128)S(1)}, u32[]{:S(2)}, u32[]{:S(2)}) collective-permute-start(f32[32,128]{1,0:T(8,128)S(1)} %add_add_fusion.9), channel_id=1, source_target_pairs={{0,4},{1,5},{2,6},{3,7},{4,0},{5,1},{6,2},{7,3},{8,12},{9,13},{10,... | collective-permute-start | bytes 49160 | tf_op jit(solution)/shard_map/ppermute | solution.py:597
  54.7 3.8 %collective-permute-start.60 = (f32[32,128]{1,0:T(8,128)S(1)}, f32[32,128]{1,0:T(8,128)S(1)}, u32[]{:S(2)}, u32[]{:S(2)}) collective-permute-start(f32[32,128]{1,0:T(8,128)S(1)} %add_add_fusion.9), channel_id=1, source_target_pairs={{0,8},{1,9},{2,10},{3,11},{4,12},{5,13},{6,14},{7,15},{8,0},{9,1},... | collective-permute-start | bytes 49160 | tf_op jit(solution)/shard_map/ppermute | solution.py:597
  58.5 1.3 %collective-permute-done.60 = f32[32,128]{1,0:T(8,128)S(1)} collective-permute-done((f32[32,128]{1,0:T(8,128)S(1)}, f32[32,128]{1,0:T(8,128)S(1)}, u32[]{:S(2)}, u32[]{:S(2)}) %collective-permute-start.60) | collective-permute-done | bytes 16416 | tf_op jit(solution)/shard_map/ppermute | solution.py:597
  59.8 2.6 %collective-permute-done.61 = f32[32,128]{1,0:T(8,128)S(1)} collective-permute-done((f32[32,128]{1,0:T(8,128)S(1)}, f32[32,128]{1,0:T(8,128)S(1)}, u32[]{:S(2)}, u32[]{:S(2)}) %collective-permute-start.61) | collective-permute-done | bytes 16416 | tf_op jit(solution)/shard_map/ppermute | solution.py:597
  62.5 2.9 %collective-permute-done.62 = f32[32,128]{1,0:T(8,128)S(1)} collective-permute-done((f32[32,128]{1,0:T(8,128)S(1)}, f32[32,128]{1,0:T(8,128)S(1)}, u32[]{:S(2)}, u32[]{:S(2)}) %collective-permute-start.62) | collective-permute-done | bytes 16416 | tf_op jit(solution)/shard_map/ppermute | solution.py:597
  65.4 1.3 %collective-permute-start.63 = (f32[32,128]{1,0:T(8,128)S(1)}, f32[32,128]{1,0:T(8,128)S(1)}, u32[]{:S(2)}, u32[]{:S(2)}) collective-permute-start(f32[32,128]{1,0:T(8,128)S(1)} %add.1139), channel_id=1, source_target_pairs={{0,64},{32,96},{64,0},{96,32},{1,65},{33,97},{65,1},{97,33},{2,66}... | collective-permute-start | bytes 49160 | tf_op jit(solution)/shard_map/ppermute | solution.py:597
  66.8 2.7 %collective-permute-done.63 = f32[32,128]{1,0:T(8,128)S(1)} collective-permute-done((f32[32,128]{1,0:T(8,128)S(1)}, f32[32,128]{1,0:T(8,128)S(1)}, u32[]{:S(2)}, u32[]{:S(2)}) %collective-permute-start.63) | collective-permute-done | bytes 16416 | tf_op jit(solution)/shard_map/ppermute | solution.py:597
  69.5 6.2 %shard_map.114 = (f32[3,32,32,128]{3,2,1,0:T(8,128)}, f32[32,104,128]{2,1,0:T(8,128)S(1)}, f32[32,32]{1,0:T(8,128)}, f32[6,1]{1,0:T(8,128)}, f32[8,128]{1,0:T(8,128)S(1)}) custom-call(f32[32,128]{1,0:T(8,128)S(1)} %add.1140.refs_0_, bf16[3,128,5120]{2,1,0:T(8,128)(2,1)S(1)} %get-tuple-element.86.refs_1_, s32[32,128]{1,0:T(8,128)S(1)} %copy-done.49, ...), custom_call_target="tpu_custom_call" | custom-call | flops 10000000 | bytes 10000000 | tf_op jit(solution)/shard_map/pallas_call | solution.py:581
  75.8 22.1 %all_to_all.19.refs_0_ = f32[32,104,128]{2,1,0:T(8,128)S(1)} all-to-all(f32[32,104,128]{2,1,0:T(8,128)S(1)} %get-tuple-element.88), channel_id=1, replica_groups=mesh['region'=4,'node'=32] {'node'}, dimensions={0} | all-to-all | bytes 3407872 | tf_op jit(solution)/shard_map/all_to_all | solution.py:787
  97.9 7.4 %collective-permute-start.64 = (f32[8,128]{1,0:T(8,128)S(1)}, f32[8,128]{1,0:T(8,128)S(1)}, u32[]{:S(2)}, u32[]{:S(2)}) collective-permute-start(f32[8,128]{1,0:T(8,128)S(1)} %slice_reduce_fusion), channel_id=1, source_target_pairs={{0,32},{32,0},{64,96},{96,64},{1,33},{33,1},{65,97},{97,65},{2,34}... | collective-permute-start | bytes 12296 | tf_op jit(solution)/shard_map/ppermute | solution.py:597
  105.3 0.8 collective-permute-done.64
  106.1 0.6 collective-permute-start.65
  107.9 1.3 %shard_map.115 = f32[3,32,4096]{2,1,0:T(8,128)} custom-call(f32[32,104,128]{2,1,0:T(8,128)S(1)} %all_to_all.19.refs_0_), custom_call_target="tpu_custom_call" | custom-call | flops 10000 | bytes 6000000 | tf_op jit(solution)/shard_map/pallas_call | solution.py:581
  109.2 0.9 collective-permute-done.65
  110.1 0.8 conditional.1
  110.1 0.8 copy.107
  (34 shorter events, 1.3 us)
Async XLA Ops:
  0.6 10.4 %copy-start.10 = (f32[9,3,3,32,128]{4,3,2,1,0:T(8,128)S(1)}, f32[9,3,3,32,128]{4,3,2,1,0:T(8,128)}, u32[]{:S(2)}) copy-start(f32[9,3,3,32,128]{4,3,2,1,0:T(8,128)} %param.12) | copy-start | bytes 3981316
  0.6 10.4 %copy-start.1 = (f32[3,32,32,128]{3,2,1,0:T(8,128)S(1)}, f32[3,32,32,128]{3,2,1,0:T(8,128)}, u32[]{:S(2)}) copy-start(f32[3,32,32,128]{3,2,1,0:T(8,128)} %v_ref.3) | copy-start | bytes 4718596
  3.0 12.2 %collective-permute-start.51 = (f32[464,128]{1,0:T(8,128)}, f32[464,128]{1,0:T(8,128)S(1)}, u32[]{:S(2)}, u32[]{:S(2)}) collective-permute-start(f32[464,128]{1,0:T(8,128)} %get-tuple-element.74), channel_id=1, source_target_pairs={{0,32},{32,64},{64,96},{1,33},{33,65},{65,97},{2,34},{34,66},{66,9... | collective-permute-start | bytes 712712 | tf_op jit(solution)/shard_map/ppermute | solution.py:618
  9.1 9.1 %collective-permute-start.52 = (f32[464,128]{1,0:T(8,128)}, f32[464,128]{1,0:T(8,128)S(1)}, u32[]{:S(2)}, u32[]{:S(2)}) collective-permute-start(f32[464,128]{1,0:T(8,128)} %get-tuple-element.75), channel_id=1, source_target_pairs={{32,0},{64,32},{96,64},{33,1},{65,33},{97,65},{34,2},{66,34},{98,6... | collective-permute-start | bytes 712712 | tf_op jit(solution)/shard_map/ppermute | solution.py:618
  11.0 0.8 copy-start
  19.6 10.0 %collective-permute-start.53 = (f32[232,128]{1,0:T(8,128)S(1)}, f32[232,128]{1,0:T(8,128)S(1)}, u32[]{:S(2)}, u32[]{:S(2)}) collective-permute-start(f32[232,128]{1,0:T(8,128)S(1)} %get-tuple-element.83), channel_id=1, source_target_pairs={{0,1},{1,2},{2,3},{3,4},{4,5},{5,6},{6,7},{7,8},{8,9},{9,10},{10,1... | collective-permute-start | bytes 356360 | tf_op jit(solution)/shard_map/ppermute | solution.py:618
  23.2 6.5 %collective-permute-start.54 = (f32[232,128]{1,0:T(8,128)S(1)}, f32[232,128]{1,0:T(8,128)S(1)}, u32[]{:S(2)}, u32[]{:S(2)}) collective-permute-start(f32[232,128]{1,0:T(8,128)S(1)} %get-tuple-element.84), channel_id=1, source_target_pairs={{1,0},{2,1},{3,2},{4,3},{5,4},{6,5},{7,6},{8,7},{9,8},{10,9},{11,1... | collective-permute-start | bytes 356360 | tf_op jit(solution)/shard_map/ppermute | solution.py:618
  24.5 5.2 %copy-start.11 = (f32[32,4096]{1,0:T(8,128)S(1)}, f32[32,4096]{1,0:T(8,128)}, u32[]{:S(2)}) copy-start(f32[32,4096]{1,0:T(8,128)} %mass_hbm.1) | copy-start | bytes 1572868
  29.7 39.8 %copy-start.49 = (s32[32,128]{1,0:T(8,128)S(1)}, s32[32,128]{1,0:T(8,128)}, u32[]{:S(2)}) copy-start(s32[32,128]{1,0:T(8,128)} %refs_2_.1) | copy-start | bytes 49156
  29.7 39.8 %copy-start.172 = (f32[64]{0:T(128)S(1)}, f32[64]{0:T(128)}, u32[]{:S(2)}) copy-start(f32[64]{0:T(128)} %refs_3_.1) | copy-start | bytes 772
  42.9 1.3 %collective-permute-start.55 = (f32[32,128]{1,0:T(8,128)S(1)}, f32[32,128]{1,0:T(8,128)S(1)}, u32[]{:S(2)}, u32[]{:S(2)}) collective-permute-start(f32[32,128]{1,0:T(8,128)S(1)} %get-tuple-element.85), channel_id=1, source_target_pairs={{0,32},{32,0},{64,96},{96,64},{1,33},{33,1},{65,97},{97,65},{2,34}... | collective-permute-start | bytes 49160 | tf_op jit(solution)/shard_map/ppermute | solution.py:597
  44.1 5.4 %collective-permute-start.56 = (f32[32,128]{1,0:T(8,128)S(1)}, f32[32,128]{1,0:T(8,128)S(1)}, u32[]{:S(2)}, u32[]{:S(2)}) collective-permute-start(f32[32,128]{1,0:T(8,128)S(1)} %add.1132), channel_id=1, source_target_pairs={{0,1},{1,0},{2,3},{3,2},{4,5},{5,4},{6,7},{7,6},{8,9},{9,8},{10,11... | collective-permute-start | bytes 49160 | tf_op jit(solution)/shard_map/ppermute | solution.py:597
  46.4 4.4 %collective-permute-start.57 = (f32[32,128]{1,0:T(8,128)S(1)}, f32[32,128]{1,0:T(8,128)S(1)}, u32[]{:S(2)}, u32[]{:S(2)}) collective-permute-start(f32[32,128]{1,0:T(8,128)S(1)} %add.1132), channel_id=1, source_target_pairs={{0,2},{1,3},{2,0},{3,1},{4,6},{5,7},{6,4},{7,5},{8,10},{9,11},{10,... | collective-permute-start | bytes 49160 | tf_op jit(solution)/shard_map/ppermute | solution.py:597
  49.5 3.8 %collective-permute-start.58 = (f32[32,128]{1,0:T(8,128)S(1)}, f32[32,128]{1,0:T(8,128)S(1)}, u32[]{:S(2)}, u32[]{:S(2)}) collective-permute-start(f32[32,128]{1,0:T(8,128)S(1)} %add.1132), channel_id=1, source_target_pairs={{0,3},{1,2},{2,1},{3,0},{4,7},{5,6},{6,5},{7,4},{8,11},{9,10},{10,... | collective-permute-start | bytes 49160 | tf_op jit(solution)/shard_map/ppermute | solution.py:597
  53.3 5.2 %collective-permute-start.59 = (f32[32,128]{1,0:T(8,128)S(1)}, f32[32,128]{1,0:T(8,128)S(1)}, u32[]{:S(2)}, u32[]{:S(2)}) collective-permute-start(f32[32,128]{1,0:T(8,128)S(1)} %add_add_fusion.9), channel_id=1, source_target_pairs={{0,4},{1,5},{2,6},{3,7},{4,0},{5,1},{6,2},{7,3},{8,12},{9,13},{10,... | collective-permute-start | bytes 49160 | tf_op jit(solution)/shard_map/ppermute | solution.py:597
  54.7 5.1 %collective-permute-start.60 = (f32[32,128]{1,0:T(8,128)S(1)}, f32[32,128]{1,0:T(8,128)S(1)}, u32[]{:S(2)}, u32[]{:S(2)}) collective-permute-start(f32[32,128]{1,0:T(8,128)S(1)} %add_add_fusion.9), channel_id=1, source_target_pairs={{0,8},{1,9},{2,10},{3,11},{4,12},{5,13},{6,14},{7,15},{8,0},{9,1},... | collective-permute-start | bytes 49160 | tf_op jit(solution)/shard_map/ppermute | solution.py:597
  58.5 3.9 %collective-permute-start.61 = (f32[32,128]{1,0:T(8,128)S(1)}, f32[32,128]{1,0:T(8,128)S(1)}, u32[]{:S(2)}, u32[]{:S(2)}) collective-permute-start(f32[32,128]{1,0:T(8,128)S(1)} %add_add_fusion.9), channel_id=1, source_target_pairs={{0,12},{1,13},{2,14},{3,15},{4,8},{5,9},{6,10},{7,11},{8,4},{9,5},... | collective-permute-start | bytes 49160 | tf_op jit(solution)/shard_map/ppermute | solution.py:597
  62.4 3.0 %collective-permute-start.62 = (f32[32,128]{1,0:T(8,128)S(1)}, f32[32,128]{1,0:T(8,128)S(1)}, u32[]{:S(2)}, u32[]{:S(2)}) collective-permute-start(f32[32,128]{1,0:T(8,128)S(1)} %add_add_fusion.8), channel_id=1, source_target_pairs={{0,16},{1,17},{2,18},{3,19},{4,20},{5,21},{6,22},{7,23},{8,24},{9,... | collective-permute-start | bytes 49160 | tf_op jit(solution)/shard_map/ppermute | solution.py:597
  65.4 4.1 %collective-permute-start.63 = (f32[32,128]{1,0:T(8,128)S(1)}, f32[32,128]{1,0:T(8,128)S(1)}, u32[]{:S(2)}, u32[]{:S(2)}) collective-permute-start(f32[32,128]{1,0:T(8,128)S(1)} %add.1139), channel_id=1, source_target_pairs={{0,64},{32,96},{64,0},{96,32},{1,65},{33,97},{65,1},{97,33},{2,66}... | collective-permute-start | bytes 49160 | tf_op jit(solution)/shard_map/ppermute | solution.py:597
  97.9 8.2 %collective-permute-start.64 = (f32[8,128]{1,0:T(8,128)S(1)}, f32[8,128]{1,0:T(8,128)S(1)}, u32[]{:S(2)}, u32[]{:S(2)}) collective-permute-start(f32[8,128]{1,0:T(8,128)S(1)} %slice_reduce_fusion), channel_id=1, source_target_pairs={{0,32},{32,0},{64,96},{96,64},{1,33},{33,1},{65,97},{97,65},{2,34}... | collective-permute-start | bytes 12296 | tf_op jit(solution)/shard_map/ppermute | solution.py:597
  106.1 4.0 %collective-permute-start.65 = (f32[8,128]{1,0:T(8,128)S(1)}, f32[8,128]{1,0:T(8,128)S(1)}, u32[]{:S(2)}, u32[]{:S(2)}) collective-permute-start(f32[8,128]{1,0:T(8,128)S(1)} %add.1141), channel_id=1, source_target_pairs={{0,64},{32,96},{64,0},{96,32},{1,65},{33,97},{65,1},{97,33},{2,66}... | collective-permute-start | bytes 12296 | tf_op jit(solution)/shard_map/ppermute | solution.py:597
  110.9 0.5 copy-start.173
  110.9 0.5 copy-start.174

commit v7 on v6

--- a/solution.py
+++ b/solution.py
@@ -410,7 +410,10 @@
             store(row_at(field_a, r, t), main_stencil(field_b, coefs, r, t))
         return 0
 
-    lax.fori_loop(0, ROWS // 4 + 1, second_rows, 0)
+    lax.fori_loop(0, ROWS // 4, second_rows, 0)
+    put_row(field_b, ROWS + 4, 0, edge_b, keep_in(first, 0, ROWS + 1))
+    for b in (ROWS + 2, ROWS + 3):
+        store(row_at(field_a, b, 0), main_stencil(field_b, coefs, b, 0))
     for b in range(2, 5):
         put_row(field_a, b, 0, edge_c, keep_in(x_ref, 0, max(b - 3, 0)))
 

time: 112 us -> 111 us (level)
  no operation moved by 1% of the time
where the time goes in v7:
time: 111 us
  starting transfers between devices  32.9 us (30%)
  Pallas kernels  32.6 us (29%)
  blocking collectives  22.1 us (20%)
  waiting for transfers between devices  19.3 us (17%)
  local copies, waits for them, and re-layouts  2.57 us (2%)
  between operations  1.49 us (1%)
    pallas_call x7, Pallas kernels, call(): pl.pallas_call(kernel, out_shape=[jax.ShapeDtypeStruct(s, d) for s, d in...  32.6 us
    all_to_all x1, blocking collectives, per_device(): recv = lax.all_to_all(send, 'node', 0, 0, tiled=True)  22.1 us
    ppermute x11, starting transfers between devices, swap(): return lax.ppermute(x, axis, [(i, i ^ k) for i in range(n)])  20.1 us
    ppermute x11, waiting for transfers between devices, swap(): return lax.ppermute(x, axis, [(i, i ^ k) for i in range(n)])  16.3 us
    ppermute x4, starting transfers between devices, shift(): lax.ppermute(x, axis, [(i, i + step) for i in range(n) if 0 <= i + step <...  12.8 us
    ppermute x4, waiting for transfers between devices, shift(): lax.ppermute(x, axis, [(i, i + step) for i in range(n) if 0 <= i + step <...  3.01 us
  transfers between devices with their start and end apart: 15, of which 10 were waited for; matrix products, arithmetic and copies ran while one was open for 0% of the time, Pallas kernels for 9%

profile of v7, /device:TPU:1, one launch (start us, length us, event | category | flops | bytes accessed | tf_op | source)
XLA Modules:
  0.0 111.0 jit_solution(7444583445538066008)
XLA Ops:
  0.7 2.4 %shard_map.109 = (f32[2,32,128]{2,1,0:T(8,128)}, f32[464,128]{1,0:T(8,128)}, f32[464,128]{1,0:T(8,128)}) custom-call(f32[3,32,32,128]{3,2,1,0:T(8,128)} %v_ref.3, f32[81,32,128]{2,1,0:T(8,128)} %bitcast.258, s32[32,128]{1,0:T(8,128)} %free_hbm.1, s32[32,128]{1,0:T(8,128)} %refs_2_.1, f32[64]{0:T(128)} %refs_3_.1), custom_call_target="tpu_custom_call" | custom-call | flops 1000000 | bytes 2000000 | tf_op jit(solution)/shard_map/pallas_call | solution.py:584
  3.0 6.0 %collective-permute-start.51 = (f32[464,128]{1,0:T(8,128)}, f32[464,128]{1,0:T(8,128)S(1)}, u32[]{:S(2)}, u32[]{:S(2)}) collective-permute-start(f32[464,128]{1,0:T(8,128)} %get-tuple-element.74), channel_id=1, source_target_pairs={{0,32},{32,64},{64,96},{1,33},{33,65},{65,97},{2,34},{34,66},{66,9... | collective-permute-start | bytes 712712 | tf_op jit(solution)/shard_map/ppermute | solution.py:621
  9.1 1.9 %collective-permute-start.52 = (f32[464,128]{1,0:T(8,128)}, f32[464,128]{1,0:T(8,128)S(1)}, u32[]{:S(2)}, u32[]{:S(2)}) collective-permute-start(f32[464,128]{1,0:T(8,128)} %get-tuple-element.75), channel_id=1, source_target_pairs={{32,0},{64,32},{96,64},{33,1},{65,33},{97,65},{34,2},{66,34},{98,6... | collective-permute-start | bytes 712712 | tf_op jit(solution)/shard_map/ppermute | solution.py:621
  11.1 0.7 copy-done
  11.8 3.4 %shard_map.110 = (f32[32,88,128]{2,1,0:T(8,128)S(1)}, f32[2,184,128]{2,1,0:T(8,128)S(1)}) custom-call(f32[3,32,32,128]{3,2,1,0:T(8,128)S(1)} %copy-done.1, f32[81,32,128]{2,1,0:T(8,128)S(1)} %bitcast.259, f32[2,32,128]{2,1,0:T(8,128)S(1)} %copy-done), custom_call_target="tpu_custom_call" | custom-call | flops 10000000 | bytes 6000000 | tf_op jit(solution)/shard_map/pallas_call | solution.py:584
  15.2 3.0 %collective-permute-done.52.rd_ref = f32[464,128]{1,0:T(8,128)S(1)} collective-permute-done((f32[464,128]{1,0:T(8,128)}, f32[464,128]{1,0:T(8,128)S(1)}, u32[]{:S(2)}, u32[]{:S(2)}) %collective-permute-start.52) | collective-permute-done | bytes 237600 | tf_op jit(solution)/shard_map/ppermute | solution.py:621
  18.2 1.4 %shard_map.112 = (f32[232,128]{1,0:T(8,128)S(1)}, f32[232,128]{1,0:T(8,128)S(1)}, f32[184,128]{1,0:T(8,128)S(1)}) custom-call(f32[2,184,128]{2,1,0:T(8,128)S(1)} %get-tuple-element.81.near_ref, f32[464,128]{1,0:T(8,128)S(1)} %collective-permute-done.51.ru_ref, f32[464,128]{1,0:T(8,128)S(1)} %collective-permute-done.52.rd_ref), custom_call_target="tpu_custom_call" | custom-call | flops 1000000 | bytes 1500000 | tf_op jit(solution)/shard_map/pallas_call | solution.py:584
  19.6 3.5 %collective-permute-start.53 = (f32[232,128]{1,0:T(8,128)S(1)}, f32[232,128]{1,0:T(8,128)S(1)}, u32[]{:S(2)}, u32[]{:S(2)}) collective-permute-start(f32[232,128]{1,0:T(8,128)S(1)} %get-tuple-element.83), channel_id=1, source_target_pairs={{0,1},{1,2},{2,3},{3,4},{4,5},{5,6},{6,7},{7,8},{8,9},{9,10},{10,1... | collective-permute-start | bytes 356360 | tf_op jit(solution)/shard_map/ppermute | solution.py:621
  23.2 1.3 %collective-permute-start.54 = (f32[232,128]{1,0:T(8,128)S(1)}, f32[232,128]{1,0:T(8,128)S(1)}, u32[]{:S(2)}, u32[]{:S(2)}) collective-permute-start(f32[232,128]{1,0:T(8,128)S(1)} %get-tuple-element.84), channel_id=1, source_target_pairs={{1,0},{2,1},{3,2},{4,3},{5,4},{6,5},{7,6},{8,7},{9,8},{10,9},{11,1... | collective-permute-start | bytes 356360 | tf_op jit(solution)/shard_map/ppermute | solution.py:621
  24.5 5.2 %shard_map.111 = (f32[10,3,32,128]{3,2,1,0:T(8,128)S(1)}, f32[10,3,32,128]{3,2,1,0:T(8,128)S(1)}, f32[10,3,32,128]{3,2,1,0:T(8,128)S(1)}, f32[10,3,32,128]{3,2,1,0:T(8,128)S(1)}, f32[40,88,128]{2,1,0:T(8,128)S(1)}) custom-call(f32[3,32,32,128]{3,2,1,0:T(8,128)S(1)} %copy-done.1, f32[32,88,128]{2,1,0:T(8,128)S(1)} %get-tuple-element.73.ct_ref, ...), custom_call_target="tpu_custom_call" | custom-call | flops 20000000 | bytes 6000000 | tf_op jit(solution)/shard_map/pallas_call | solution.py:584
  29.7 12.8 %shard_map.113 = (bf16[3,128,5120]{2,1,0:T(8,128)(2,1)S(1)}, f32[32,128]{1,0:T(8,128)S(1)}) custom-call(f32[10,3,32,128]{3,2,1,0:T(8,128)S(1)} %get-tuple-element.76.u0, f32[10,3,32,128]{3,2,1,0:T(8,128)S(1)} %get-tuple-element.77.u1, f32[10,3,32,128]{3,2,1,0:T(8,128)S(1)} %get-tuple-element.78.u2, f32[10,3,32,128]{3,2,1,0:T(8,128)S(1)} %get-tuple-element.79.u3, ...), custom_call_target="tpu_custom_call" | custom-call | flops 100000000 | bytes 20000000 | tf_op jit(solution)/shard_map/pallas_call | solution.py:584
  42.6 1.2 %collective-permute-done.55 = f32[32,128]{1,0:T(8,128)S(1)} collective-permute-done((f32[32,128]{1,0:T(8,128)S(1)}, f32[32,128]{1,0:T(8,128)S(1)}, u32[]{:S(2)}, u32[]{:S(2)}) %collective-permute-start.55) | collective-permute-done | bytes 16416 | tf_op jit(solution)/shard_map/ppermute | solution.py:600
  43.8 2.3 %collective-permute-start.56 = (f32[32,128]{1,0:T(8,128)S(1)}, f32[32,128]{1,0:T(8,128)S(1)}, u32[]{:S(2)}, u32[]{:S(2)}) collective-permute-start(f32[32,128]{1,0:T(8,128)S(1)} %add.1132), channel_id=1, source_target_pairs={{0,1},{1,0},{2,3},{3,2},{4,5},{5,4},{6,7},{7,6},{8,9},{9,8},{10,11... | collective-permute-start | bytes 49160 | tf_op jit(solution)/shard_map/ppermute | solution.py:600
  46.0 3.1 %collective-permute-start.57 = (f32[32,128]{1,0:T(8,128)S(1)}, f32[32,128]{1,0:T(8,128)S(1)}, u32[]{:S(2)}, u32[]{:S(2)}) collective-permute-start(f32[32,128]{1,0:T(8,128)S(1)} %add.1132), channel_id=1, source_target_pairs={{0,2},{1,3},{2,0},{3,1},{4,6},{5,7},{6,4},{7,5},{8,10},{9,11},{10,... | collective-permute-start | bytes 49160 | tf_op jit(solution)/shard_map/ppermute | solution.py:600
  49.2 1.3 %collective-permute-done.57 = f32[32,128]{1,0:T(8,128)S(1)} collective-permute-done((f32[32,128]{1,0:T(8,128)S(1)}, f32[32,128]{1,0:T(8,128)S(1)}, u32[]{:S(2)}, u32[]{:S(2)}) %collective-permute-start.57) | collective-permute-done | bytes 16416 | tf_op jit(solution)/shard_map/ppermute | solution.py:600
  50.4 2.5 %collective-permute-done.58 = f32[32,128]{1,0:T(8,128)S(1)} collective-permute-done((f32[32,128]{1,0:T(8,128)S(1)}, f32[32,128]{1,0:T(8,128)S(1)}, u32[]{:S(2)}, u32[]{:S(2)}) %collective-permute-start.58) | collective-permute-done | bytes 16416 | tf_op jit(solution)/shard_map/ppermute | solution.py:600
  53.0 1.4 %collective-permute-start.59 = (f32[32,128]{1,0:T(8,128)S(1)}, f32[32,128]{1,0:T(8,128)S(1)}, u32[]{:S(2)}, u32[]{:S(2)}) collective-permute-start(f32[32,128]{1,0:T(8,128)S(1)} %add_add_fusion.9), channel_id=1, source_target_pairs={{0,4},{1,5},{2,6},{3,7},{4,0},{5,1},{6,2},{7,3},{8,12},{9,13},{10,... | collective-permute-start | bytes 49160 | tf_op jit(solution)/shard_map/ppermute | solution.py:600
  54.3 3.8 %collective-permute-start.60 = (f32[32,128]{1,0:T(8,128)S(1)}, f32[32,128]{1,0:T(8,128)S(1)}, u32[]{:S(2)}, u32[]{:S(2)}) collective-permute-start(f32[32,128]{1,0:T(8,128)S(1)} %add_add_fusion.9), channel_id=1, source_target_pairs={{0,8},{1,9},{2,10},{3,11},{4,12},{5,13},{6,14},{7,15},{8,0},{9,1},... | collective-permute-start | bytes 49160 | tf_op jit(solution)/shard_map/ppermute | solution.py:600
  58.1 1.3 %collective-permute-done.60 = f32[32,128]{1,0:T(8,128)S(1)} collective-permute-done((f32[32,128]{1,0:T(8,128)S(1)}, f32[32,128]{1,0:T(8,128)S(1)}, u32[]{:S(2)}, u32[]{:S(2)}) %collective-permute-start.60) | collective-permute-done | bytes 16416 | tf_op jit(solution)/shard_map/ppermute | solution.py:600
  59.4 2.6 %collective-permute-done.61 = f32[32,128]{1,0:T(8,128)S(1)} collective-permute-done((f32[32,128]{1,0:T(8,128)S(1)}, f32[32,128]{1,0:T(8,128)S(1)}, u32[]{:S(2)}, u32[]{:S(2)}) %collective-permute-start.61) | collective-permute-done | bytes 16416 | tf_op jit(solution)/shard_map/ppermute | solution.py:600
  62.1 2.9 %collective-permute-done.62 = f32[32,128]{1,0:T(8,128)S(1)} collective-permute-done((f32[32,128]{1,0:T(8,128)S(1)}, f32[32,128]{1,0:T(8,128)S(1)}, u32[]{:S(2)}, u32[]{:S(2)}) %collective-permute-start.62) | collective-permute-done | bytes 16416 | tf_op jit(solution)/shard_map/ppermute | solution.py:600
  65.0 1.3 %collective-permute-start.63 = (f32[32,128]{1,0:T(8,128)S(1)}, f32[32,128]{1,0:T(8,128)S(1)}, u32[]{:S(2)}, u32[]{:S(2)}) collective-permute-start(f32[32,128]{1,0:T(8,128)S(1)} %add.1139), channel_id=1, source_target_pairs={{0,64},{32,96},{64,0},{96,32},{1,65},{33,97},{65,1},{97,33},{2,66}... | collective-permute-start | bytes 49160 | tf_op jit(solution)/shard_map/ppermute | solution.py:600
  66.4 2.8 %collective-permute-done.63 = f32[32,128]{1,0:T(8,128)S(1)} collective-permute-done((f32[32,128]{1,0:T(8,128)S(1)}, f32[32,128]{1,0:T(8,128)S(1)}, u32[]{:S(2)}, u32[]{:S(2)}) %collective-permute-start.63) | collective-permute-done | bytes 16416 | tf_op jit(solution)/shard_map/ppermute | solution.py:600
  69.1 6.2 %shard_map.114 = (f32[3,32,32,128]{3,2,1,0:T(8,128)}, f32[32,104,128]{2,1,0:T(8,128)S(1)}, f32[32,32]{1,0:T(8,128)}, f32[6,1]{1,0:T(8,128)}, f32[8,128]{1,0:T(8,128)S(1)}) custom-call(f32[32,128]{1,0:T(8,128)S(1)} %add.1140.refs_0_, bf16[3,128,5120]{2,1,0:T(8,128)(2,1)S(1)} %get-tuple-element.86.refs_1_, s32[32,128]{1,0:T(8,128)S(1)} %copy-done.49, ...), custom_call_target="tpu_custom_call" | custom-call | flops 10000000 | bytes 10000000 | tf_op jit(solution)/shard_map/pallas_call | solution.py:584
  75.4 22.1 %all_to_all.19.refs_0_ = f32[32,104,128]{2,1,0:T(8,128)S(1)} all-to-all(f32[32,104,128]{2,1,0:T(8,128)S(1)} %get-tuple-element.88), channel_id=1, replica_groups=mesh['region'=4,'node'=32] {'node'}, dimensions={0} | all-to-all | bytes 3407872 | tf_op jit(solution)/shard_map/all_to_all | solution.py:790
  97.5 7.4 %collective-permute-start.64 = (f32[8,128]{1,0:T(8,128)S(1)}, f32[8,128]{1,0:T(8,128)S(1)}, u32[]{:S(2)}, u32[]{:S(2)}) collective-permute-start(f32[8,128]{1,0:T(8,128)S(1)} %slice_reduce_fusion), channel_id=1, source_target_pairs={{0,32},{32,0},{64,96},{96,64},{1,33},{33,1},{65,97},{97,65},{2,34}... | collective-permute-start | bytes 12296 | tf_op jit(solution)/shard_map/ppermute | solution.py:600
  104.9 0.8 collective-permute-done.64
  105.7 0.6 collective-permute-start.65
  107.5 1.3 %shard_map.115 = f32[3,32,4096]{2,1,0:T(8,128)} custom-call(f32[32,104,128]{2,1,0:T(8,128)S(1)} %all_to_all.19.refs_0_), custom_call_target="tpu_custom_call" | custom-call | flops 10000 | bytes 6000000 | tf_op jit(solution)/shard_map/pallas_call | solution.py:584
  108.8 0.9 collective-permute-done.65
  109.7 0.8 conditional.1
  109.7 0.8 copy.107
  (34 shorter events, 1.3 us)
Async XLA Ops:
  0.6 10.4 %copy-start.10 = (f32[9,3,3,32,128]{4,3,2,1,0:T(8,128)S(1)}, f32[9,3,3,32,128]{4,3,2,1,0:T(8,128)}, u32[]{:S(2)}) copy-start(f32[9,3,3,32,128]{4,3,2,1,0:T(8,128)} %param.12) | copy-start | bytes 3981316
  0.6 10.4 %copy-start.1 = (f32[3,32,32,128]{3,2,1,0:T(8,128)S(1)}, f32[3,32,32,128]{3,2,1,0:T(8,128)}, u32[]{:S(2)}) copy-start(f32[3,32,32,128]{3,2,1,0:T(8,128)} %v_ref.3) | copy-start | bytes 4718596
  3.0 12.2 %collective-permute-start.51 = (f32[464,128]{1,0:T(8,128)}, f32[464,128]{1,0:T(8,128)S(1)}, u32[]{:S(2)}, u32[]{:S(2)}) collective-permute-start(f32[464,128]{1,0:T(8,128)} %get-tuple-element.74), channel_id=1, source_target_pairs={{0,32},{32,64},{64,96},{1,33},{33,65},{65,97},{2,34},{34,66},{66,9... | collective-permute-start | bytes 712712 | tf_op jit(solution)/shard_map/ppermute | solution.py:621
  9.1 9.1 %collective-permute-start.52 = (f32[464,128]{1,0:T(8,128)}, f32[464,128]{1,0:T(8,128)S(1)}, u32[]{:S(2)}, u32[]{:S(2)}) collective-permute-start(f32[464,128]{1,0:T(8,128)} %get-tuple-element.75), channel_id=1, source_target_pairs={{32,0},{64,32},{96,64},{33,1},{65,33},{97,65},{34,2},{66,34},{98,6... | collective-permute-start | bytes 712712 | tf_op jit(solution)/shard_map/ppermute | solution.py:621
  11.0 0.8 copy-start
  19.6 10.0 %collective-permute-start.53 = (f32[232,128]{1,0:T(8,128)S(1)}, f32[232,128]{1,0:T(8,128)S(1)}, u32[]{:S(2)}, u32[]{:S(2)}) collective-permute-start(f32[232,128]{1,0:T(8,128)S(1)} %get-tuple-element.83), channel_id=1, source_target_pairs={{0,1},{1,2},{2,3},{3,4},{4,5},{5,6},{6,7},{7,8},{8,9},{9,10},{10,1... | collective-permute-start | bytes 356360 | tf_op jit(solution)/shard_map/ppermute | solution.py:621
  23.2 6.5 %collective-permute-start.54 = (f32[232,128]{1,0:T(8,128)S(1)}, f32[232,128]{1,0:T(8,128)S(1)}, u32[]{:S(2)}, u32[]{:S(2)}) collective-permute-start(f32[232,128]{1,0:T(8,128)S(1)} %get-tuple-element.84), channel_id=1, source_target_pairs={{1,0},{2,1},{3,2},{4,3},{5,4},{6,5},{7,6},{8,7},{9,8},{10,9},{11,1... | collective-permute-start | bytes 356360 | tf_op jit(solution)/shard_map/ppermute | solution.py:621
  24.5 5.2 %copy-start.11 = (f32[32,4096]{1,0:T(8,128)S(1)}, f32[32,4096]{1,0:T(8,128)}, u32[]{:S(2)}) copy-start(f32[32,4096]{1,0:T(8,128)} %mass_hbm.1) | copy-start | bytes 1572868
  29.7 39.5 %copy-start.49 = (s32[32,128]{1,0:T(8,128)S(1)}, s32[32,128]{1,0:T(8,128)}, u32[]{:S(2)}) copy-start(s32[32,128]{1,0:T(8,128)} %refs_2_.1) | copy-start | bytes 49156
  29.7 39.4 %copy-start.172 = (f32[64]{0:T(128)S(1)}, f32[64]{0:T(128)}, u32[]{:S(2)}) copy-start(f32[64]{0:T(128)} %refs_3_.1) | copy-start | bytes 772
  42.5 1.3 %collective-permute-start.55 = (f32[32,128]{1,0:T(8,128)S(1)}, f32[32,128]{1,0:T(8,128)S(1)}, u32[]{:S(2)}, u32[]{:S(2)}) collective-permute-start(f32[32,128]{1,0:T(8,128)S(1)} %get-tuple-element.85), channel_id=1, source_target_pairs={{0,32},{32,0},{64,96},{96,64},{1,33},{33,1},{65,97},{97,65},{2,34}... | collective-permute-start | bytes 49160 | tf_op jit(solution)/shard_map/ppermute | solution.py:600
  43.8 5.4 %collective-permute-start.56 = (f32[32,128]{1,0:T(8,128)S(1)}, f32[32,128]{1,0:T(8,128)S(1)}, u32[]{:S(2)}, u32[]{:S(2)}) collective-permute-start(f32[32,128]{1,0:T(8,128)S(1)} %add.1132), channel_id=1, source_target_pairs={{0,1},{1,0},{2,3},{3,2},{4,5},{5,4},{6,7},{7,6},{8,9},{9,8},{10,11... | collective-permute-start | bytes 49160 | tf_op jit(solution)/shard_map/ppermute | solution.py:600
  46.0 4.4 %collective-permute-start.57 = (f32[32,128]{1,0:T(8,128)S(1)}, f32[32,128]{1,0:T(8,128)S(1)}, u32[]{:S(2)}, u32[]{:S(2)}) collective-permute-start(f32[32,128]{1,0:T(8,128)S(1)} %add.1132), channel_id=1, source_target_pairs={{0,2},{1,3},{2,0},{3,1},{4,6},{5,7},{6,4},{7,5},{8,10},{9,11},{10,... | collective-permute-start | bytes 49160 | tf_op jit(solution)/shard_map/ppermute | solution.py:600
  49.1 3.8 %collective-permute-start.58 = (f32[32,128]{1,0:T(8,128)S(1)}, f32[32,128]{1,0:T(8,128)S(1)}, u32[]{:S(2)}, u32[]{:S(2)}) collective-permute-start(f32[32,128]{1,0:T(8,128)S(1)} %add.1132), channel_id=1, source_target_pairs={{0,3},{1,2},{2,1},{3,0},{4,7},{5,6},{6,5},{7,4},{8,11},{9,10},{10,... | collective-permute-start | bytes 49160 | tf_op jit(solution)/shard_map/ppermute | solution.py:600
  53.0 5.2 %collective-permute-start.59 = (f32[32,128]{1,0:T(8,128)S(1)}, f32[32,128]{1,0:T(8,128)S(1)}, u32[]{:S(2)}, u32[]{:S(2)}) collective-permute-start(f32[32,128]{1,0:T(8,128)S(1)} %add_add_fusion.9), channel_id=1, source_target_pairs={{0,4},{1,5},{2,6},{3,7},{4,0},{5,1},{6,2},{7,3},{8,12},{9,13},{10,... | collective-permute-start | bytes 49160 | tf_op jit(solution)/shard_map/ppermute | solution.py:600
  54.3 5.1 %collective-permute-start.60 = (f32[32,128]{1,0:T(8,128)S(1)}, f32[32,128]{1,0:T(8,128)S(1)}, u32[]{:S(2)}, u32[]{:S(2)}) collective-permute-start(f32[32,128]{1,0:T(8,128)S(1)} %add_add_fusion.9), channel_id=1, source_target_pairs={{0,8},{1,9},{2,10},{3,11},{4,12},{5,13},{6,14},{7,15},{8,0},{9,1},... | collective-permute-start | bytes 49160 | tf_op jit(solution)/shard_map/ppermute | solution.py:600
  58.1 3.9 %collective-permute-start.61 = (f32[32,128]{1,0:T(8,128)S(1)}, f32[32,128]{1,0:T(8,128)S(1)}, u32[]{:S(2)}, u32[]{:S(2)}) collective-permute-start(f32[32,128]{1,0:T(8,128)S(1)} %add_add_fusion.9), channel_id=1, source_target_pairs={{0,12},{1,13},{2,14},{3,15},{4,8},{5,9},{6,10},{7,11},{8,4},{9,5},... | collective-permute-start | bytes 49160 | tf_op jit(solution)/shard_map/ppermute | solution.py:600
  62.1 3.0 %collective-permute-start.62 = (f32[32,128]{1,0:T(8,128)S(1)}, f32[32,128]{1,0:T(8,128)S(1)}, u32[]{:S(2)}, u32[]{:S(2)}) collective-permute-start(f32[32,128]{1,0:T(8,128)S(1)} %add_add_fusion.8), channel_id=1, source_target_pairs={{0,16},{1,17},{2,18},{3,19},{4,20},{5,21},{6,22},{7,23},{8,24},{9,... | collective-permute-start | bytes 49160 | tf_op jit(solution)/shard_map/ppermute | solution.py:600
  65.0 4.1 %collective-permute-start.63 = (f32[32,128]{1,0:T(8,128)S(1)}, f32[32,128]{1,0:T(8,128)S(1)}, u32[]{:S(2)}, u32[]{:S(2)}) collective-permute-start(f32[32,128]{1,0:T(8,128)S(1)} %add.1139), channel_id=1, source_target_pairs={{0,64},{32,96},{64,0},{96,32},{1,65},{33,97},{65,1},{97,33},{2,66}... | collective-permute-start | bytes 49160 | tf_op jit(solution)/shard_map/ppermute | solution.py:600
  97.5 8.2 %collective-permute-start.64 = (f32[8,128]{1,0:T(8,128)S(1)}, f32[8,128]{1,0:T(8,128)S(1)}, u32[]{:S(2)}, u32[]{:S(2)}) collective-permute-start(f32[8,128]{1,0:T(8,128)S(1)} %slice_reduce_fusion), channel_id=1, source_target_pairs={{0,32},{32,0},{64,96},{96,64},{1,33},{33,1},{65,97},{97,65},{2,34}... | collective-permute-start | bytes 12296 | tf_op jit(solution)/shard_map/ppermute | solution.py:600
  105.7 4.0 %collective-permute-start.65 = (f32[8,128]{1,0:T(8,128)S(1)}, f32[8,128]{1,0:T(8,128)S(1)}, u32[]{:S(2)}, u32[]{:S(2)}) collective-permute-start(f32[8,128]{1,0:T(8,128)S(1)} %add.1141), channel_id=1, source_target_pairs={{0,64},{32,96},{64,0},{96,32},{1,65},{33,97},{65,1},{97,33},{2,66}... | collective-permute-start | bytes 12296 | tf_op jit(solution)/shard_map/ppermute | solution.py:600
  110.5 0.5 copy-start.173
  110.5 0.5 copy-start.174
